TPU v7x, 32 devices: a whole 2x2x4 slice. The times are simulated.
32 devices in a mesh: fibre: 4 (over z), blk: 8 (over y, x, core).
Axes of the slice: x: 2, y: 2, z: 4, core: 2. Of those that a mesh axis runs over, the one named last changes fastest.
Arguments:
- readings: bfloat16 [131072, 1024], P(('fibre', 'blk')), as said below
- values: bfloat16 [131072], P(('fibre', 'blk')), may hold values from -6 to 6
- counts: int32 [32], P(('fibre', 'blk')), may hold values from 1 to 4096, as said below
- prior_root: float32 [1024, 1024], P(('fibre', 'blk')), as said below
- prior_info: float32 [1024], P(('fibre', 'blk')), may hold values from -6 to 6
Outputs:
- post_root: float32 [1024, 1024], P('blk')
- post_info: float32 [1024], replicated
Inputs may be any that keep to these rules, and one draw needn't show every extreme that they name: `counts`: every owner has at least one live row, and in every draw some owner has all 4096 rows live. `prior_root`: upper triangular with a positive diagonal. `readings`: whitened measurement rows; nothing beyond the stated range is promised.
All inputs are finite; a program needn't handle non-finite values.
Results may differ from a plain program's by a relative error of at most 0.0003.
Values sent between devices are 32-bit elements; how exact they have to be, the bound alone decides.
No kernel may reach another device: no remote copies, remote signals or barrier semaphores. Data moves between devices by JAX's collectives and lax.ppermute only.
A program may use at most 128 MiB of HBM per device.

v0:
```python
import jax
import jax.numpy as jnp
from jax import lax
from jax.sharding import PartitionSpec as P


def accumulate(row_data, val_data, active, state_width):
    block_rows = min(512, row_data.shape[0])
    block_count = (active + block_rows - 1) // block_rows

    def add_block(turn_index, totals):
        row_piece = lax.dynamic_slice_in_dim(row_data, turn_index * block_rows, block_rows, 0)
        val_piece = lax.dynamic_slice_in_dim(val_data, turn_index * block_rows, block_rows, 0)
        gram_part = lax.dot_general(
            row_piece, row_piece, (((0,), (0,)), ((), ())), preferred_element_type=jnp.float32
        )
        info_part = jnp.dot(val_piece, row_piece, preferred_element_type=jnp.float32)
        return (totals[0] + gram_part, totals[1] + info_part)

    initial = (
        jnp.zeros((state_width, state_width), jnp.float32),
        jnp.zeros((state_width,), jnp.float32),
    )
    return lax.fori_loop(0, block_count, add_block, initial)


def local(readings, values, counts, prior_root, prior_info):
    capacity, state_width = readings.shape
    own_count = counts[0]
    live_mask = jnp.arange(capacity, dtype=jnp.int32) < own_count
    masked_rows = jnp.where(live_mask[:, None], readings, jnp.zeros((), readings.dtype))
    masked_vals = jnp.where(live_mask, values, jnp.zeros((), values.dtype))
    gram_local, info_local = accumulate(masked_rows, masked_vals, own_count, state_width)
    gram_local = gram_local + jnp.dot(prior_root.T, prior_root, precision=lax.Precision.HIGHEST)
    info_local = info_local + jnp.dot(prior_info, prior_root, precision=lax.Precision.HIGHEST)
    share_gram, share_info = (
        lax.psum_scatter(gram_local, "blk", scatter_dimension=0, tiled=True),
        lax.psum_scatter(info_local, "blk", scatter_dimension=0, tiled=True),
    )
    share_gram, share_info = lax.psum((share_gram, share_info), "fibre")
    total_gram, total_info = (
        lax.all_gather(share_gram, "blk", axis=0, tiled=True),
        lax.all_gather(share_info, "blk", axis=0, tiled=True),
    )
    factor = jnp.linalg.cholesky(total_gram)
    post_info = lax.linalg.triangular_solve(
        factor, total_info[:, None], left_side=True, lower=True
    )[:, 0]
    row_count = state_width // lax.axis_size("blk")
    post_root = lax.dynamic_slice_in_dim(factor.T, lax.axis_index("blk") * row_count, row_count, 0)
    return (post_root, post_info)


def solution(mesh):
    placed = (
        P(("fibre", "blk"), None),
        P(("fibre", "blk")),
        P(("fibre", "blk")),
        P(("fibre", "blk"), None),
        P(("fibre", "blk")),
    )
    return jax.shard_map(
        local, mesh=mesh, in_specs=placed, out_specs=(P("blk", None), P()), check_vma=False
    )
```

profile of v0, /device:TPU:0, one launch (start us, length us, event | category | flops | bytes accessed | tf_op | source)
XLA Modules:
  0.0 568.6 jit_solution(1290649281919089703)
XLA Ops:
  8.0 7.2 %broadcast_select_fusion = bf16[4096,1024]{1,0:T(8,128)(2,1)} fusion(bf16[4096,1024]{1,0:T(8,128)(2,1)} %param.7, pred[4096]{0:T(1024)(128)(4,1)S(1)} %iota_compare_fusion.3), kind=kLoop, calls=%fused_computation.8 | loop fusion | flops 4194304 | bytes 16781312 | tf_op jit(solution)/shard_map/jit(_where)/select_n | solution.py:31
  15.2 2.5 broadcast_in_dim.26
  17.7 30.7 %while.13 = (s32[]{:T(128)}, f32[1024,1024]{1,0:T(8,128)}, f32[1024]{0:T(1024)S(1)}, s32[]{:T(128)}, bf16[4096,1024]{1,0:T(8,128)(2,1)}, /*index=5*/bf16[4096]{0...) while((s32[]{:T(128)}, f32[1024,1024]{1,0:T(8,128)}, f32[1024]{0:T(1024)S(1)}, s32[]{:T(128)}, ...), condition=%wide.region_1.2_spmd, body=%wide.region_0.1_spmd.sunk | while | flops 1075840000 | bytes 10507423 | solution.py:24
  17.8 1.5 fusion.101
  19.3 6.1 %convolution_add_fusion.3 = f32[1024,1024]{1,0:T(8,128)} fusion(f32[1024,1024]{1,0:T(8,128)} %get-tuple-element.207, bf16[4096,1024]{1,0:T(8,128)(2,1)} %get-tuple-element.220, s32[]{:T(128)S(6)} %select_n.34), kind=kOutput, calls=%fused_computation.clone.1 | convolution fusion | flops 1074790400 | bytes 9437188 | tf_op jit(solution)/shard_map/while/body/dot_general | solution.py:14
  25.5 1.5 fusion.101
  26.9 6.1 %convolution_add_fusion.3 = f32[1024,1024]{1,0:T(8,128)} fusion(f32[1024,1024]{1,0:T(8,128)} %get-tuple-element.207, bf16[4096,1024]{1,0:T(8,128)(2,1)} %get-tuple-element.220, s32[]{:T(128)S(6)} %select_n.34), kind=kOutput, calls=%fused_computation.clone.1 | convolution fusion | flops 1074790400 | bytes 9437188 | tf_op jit(solution)/shard_map/while/body/dot_general | solution.py:14
  33.1 1.5 fusion.101
  34.6 6.1 %convolution_add_fusion.3 = f32[1024,1024]{1,0:T(8,128)} fusion(f32[1024,1024]{1,0:T(8,128)} %get-tuple-element.207, bf16[4096,1024]{1,0:T(8,128)(2,1)} %get-tuple-element.220, s32[]{:T(128)S(6)} %select_n.34), kind=kOutput, calls=%fused_computation.clone.1 | convolution fusion | flops 1074790400 | bytes 9437188 | tf_op jit(solution)/shard_map/while/body/dot_general | solution.py:14
  40.8 1.5 fusion.101
  42.3 6.2 %convolution_add_fusion.3 = f32[1024,1024]{1,0:T(8,128)} fusion(f32[1024,1024]{1,0:T(8,128)} %get-tuple-element.207, bf16[4096,1024]{1,0:T(8,128)(2,1)} %get-tuple-element.220, s32[]{:T(128)S(6)} %select_n.34), kind=kOutput, calls=%fused_computation.clone.1 | convolution fusion | flops 1074790400 | bytes 9437188 | tf_op jit(solution)/shard_map/while/body/dot_general | solution.py:14
  48.4 5.3 copy.11
  53.8 6.6 %convolution_add_fusion.1 = f32[1024,1024]{0,1:T(8,128)} fusion(f32[1024,1024]{0,1:T(8,128)} %copy.11, f32[32,1024]{1,0:T(8,128)S(1)} %copy-done), kind=kOutput, calls=%fused_computation.14 | convolution fusion | flops 403701760 | bytes 8519680 | tf_op jit(solution)/shard_map/dot_general | solution.py:34
  60.4 84.9 %reduce-scatter.2.cloned.1.call-done = f32[128,1024]{0,1:T(8,128)} async-done(((f32[1024,1024]{0,1:T(8,128)}), f32[128,1024]{0,1:T(8,128)}) %reduce-scatter.2.cloned.1.call-update) | async-done | bytes 524304 | tf_op jit(solution)/shard_map/reduce_scatter | solution.py:37
  145.4 40.7 %all-reduce.4.cloned.1.call-done = f32[128,1024]{0,1:T(8,128)} async-done(((f32[128,1024]{0,1:T(8,128)}), f32[128,1024]{0,1:T(8,128)}) %all-reduce.4.cloned.1.call-update) | async-done | bytes 524304 | tf_op jit(solution)/shard_map/psum | solution.py:40
  187.6 13.0 %all-reduce.1 = f32[1024]{0:T(1024)S(1)} all-reduce(f32[1024]{0:T(1024)S(1)} %add.114), channel_id=3, replica_groups=mesh['fibre'=4,'blk'=8] {'blk'}, use_global_device_ids=true, to_apply=%region_20.21.clone | all-reduce | flops 1024 | bytes 8192
  200.7 10.1 %psum.15 = f32[128]{0:T(128)S(1)} all-reduce(f32[128]{0:T(128)S(1)} %dynamic-slice.8), channel_id=1, replica_groups=mesh['fibre'=4,'blk'=8] {'fibre'}, use_global_device_ids=true, to_apply=%region_21.22 | all-reduce | flops 128 | bytes 1024 | tf_op jit(solution)/shard_map/psum | solution.py:40
  210.8 8.3 %all-gather = f32[8,1,128]{2,1,0:T(1,128)S(1)} all-gather(f32[1,1,128]{2,1,0:T(1,128)S(1)} %bitcast.245), channel_id=1, replica_groups=mesh['fibre'=4,'blk'=8] {'blk'}, dimensions={0}, use_global_device_ids=true | all-gather | bytes 4608 | tf_op jit(solution)/shard_map/all_gather | solution.py:43
  219.1 6.5 %all-gather.3.cloned.1.call-done = f32[1024,1024]{0,1:T(8,128)} async-done(((f32[128,1024]{0,1:T(8,128)}), f32[1024,1024]{0,1:T(8,128)}) %all-gather.3.cloned.1.call-update) | async-done | bytes 4194320 | tf_op jit(solution)/shard_map/all_gather | solution.py:42
  225.6 5.8 %copy.13 = f32[1024,1024]{1,0:T(8,128)} copy(f32[1024,1024]{0,1:T(8,128)} %all-gather.3.cloned.1.call-done) | data formatting | bytes 8388608 | tf_op jit(solution)/shard_map/all_gather | solution.py:42
  231.4 4.4 fusion.5
  235.9 1.9 copy-done.1
  237.8 11.7 %cholesky.222 = f32[128,128]{1,0:T(8,128)S(1)} custom-call(f32[128,128]{1,0:T(8,128)S(1)} %cholesky.577), custom_call_target="Cholesky" | custom-call | tf_op jit(solution)/shard_map/jit(cholesky)/cholesky | solution.py:45
  249.5 2.5 cholesky.254
  252.0 9.8 %custom-call.62 = f32[1,128,128]{1,2,0:T(8,128)S(1)} custom-call(f32[1,128,128]{2,1,0:T(8,128)S(1)} %get-tuple-element.95), custom_call_target="InvertDiagBlocksLowerTriangular" | custom-call | tf_op jit(solution)/shard_map/jit(cholesky)/cholesky | solution.py:45
  261.8 2.3 constant_dynamic-update-slice_fusion.32
  264.2 1.5 convolution_subtract_fusion
  265.8 11.9 %cholesky.243 = f32[128,128]{1,0:T(8,128)S(1)} custom-call(f32[128,128]{1,0:T(8,128)S(1)} %cholesky.581), custom_call_target="Cholesky" | custom-call | tf_op jit(solution)/shard_map/jit(cholesky)/cholesky | solution.py:45
  278.3 9.8 %custom-call.63 = f32[1,128,128]{1,2,0:T(8,128)S(1)} custom-call(f32[1,128,128]{2,1,0:T(8,128)S(1)} %get-tuple-element.92), custom_call_target="InvertDiagBlocksLowerTriangular" | custom-call | tf_op jit(solution)/shard_map/jit(cholesky)/cholesky | solution.py:45
  288.1 1.2 convolution_dynamic-update-slice_fusion
  289.3 2.1 convolution_subtract_fusion.1
  291.4 11.7 %cholesky.466 = f32[128,128]{1,0:T(8,128)S(1)} custom-call(f32[128,128]{1,0:T(8,128)S(1)} %cholesky.586), custom_call_target="Cholesky" | custom-call | tf_op jit(solution)/shard_map/jit(cholesky)/cholesky | solution.py:45
  304.4 9.8 %custom-call.64 = f32[1,128,128]{1,2,0:T(8,128)S(1)} custom-call(f32[1,128,128]{2,1,0:T(8,128)S(1)} %get-tuple-element.89), custom_call_target="InvertDiagBlocksLowerTriangular" | custom-call | tf_op jit(solution)/shard_map/jit(cholesky)/cholesky | solution.py:45
  314.3 1.2 convolution_dynamic-update-slice_fusion.1
  315.4 2.3 convolution_subtract_fusion.2
  317.8 11.9 %cholesky.485 = f32[128,128]{1,0:T(8,128)S(1)} custom-call(f32[128,128]{1,0:T(8,128)S(1)} %cholesky.591), custom_call_target="Cholesky" | custom-call | tf_op jit(solution)/shard_map/jit(cholesky)/cholesky | solution.py:45
  331.0 9.8 %custom-call.65 = f32[1,128,128]{1,2,0:T(8,128)S(1)} custom-call(f32[1,128,128]{2,1,0:T(8,128)S(1)} %get-tuple-element.86), custom_call_target="InvertDiagBlocksLowerTriangular" | custom-call | tf_op jit(solution)/shard_map/jit(cholesky)/cholesky | solution.py:45
  341.9 2.3 convolution_subtract_fusion.3
  344.3 11.7 %cholesky.504 = f32[128,128]{1,0:T(8,128)S(1)} custom-call(f32[128,128]{1,0:T(8,128)S(1)} %cholesky.596), custom_call_target="Cholesky" | custom-call | tf_op jit(solution)/shard_map/jit(cholesky)/cholesky | solution.py:45
  357.4 10.2 %custom-call.66 = f32[1,128,128]{1,2,0:T(8,128)S(1)} custom-call(f32[1,128,128]{2,1,0:T(8,128)S(1)} %get-tuple-element.83), custom_call_target="InvertDiagBlocksLowerTriangular" | custom-call | tf_op jit(solution)/shard_map/jit(cholesky)/cholesky | solution.py:45
  368.6 2.3 convolution_subtract_fusion.4
  370.9 11.7 %cholesky.524 = f32[128,128]{1,0:T(8,128)S(1)} custom-call(f32[128,128]{1,0:T(8,128)S(1)} %cholesky.601), custom_call_target="Cholesky" | custom-call | tf_op jit(solution)/shard_map/jit(cholesky)/cholesky | solution.py:45
  383.9 9.8 %custom-call.67 = f32[1,128,128]{1,2,0:T(8,128)S(1)} custom-call(f32[1,128,128]{2,1,0:T(8,128)S(1)} %get-tuple-element.80), custom_call_target="InvertDiagBlocksLowerTriangular" | custom-call | tf_op jit(solution)/shard_map/jit(cholesky)/cholesky | solution.py:45
  394.6 2.0 convolution_subtract_fusion.5
  396.7 11.9 %cholesky.544 = f32[128,128]{1,0:T(8,128)S(1)} custom-call(f32[128,128]{1,0:T(8,128)S(1)} %cholesky.606), custom_call_target="Cholesky" | custom-call | tf_op jit(solution)/shard_map/jit(cholesky)/cholesky | solution.py:45
  409.8 9.8 %custom-call.68 = f32[1,128,128]{1,2,0:T(8,128)S(1)} custom-call(f32[1,128,128]{2,1,0:T(8,128)S(1)} %get-tuple-element.77), custom_call_target="InvertDiagBlocksLowerTriangular" | custom-call | tf_op jit(solution)/shard_map/jit(cholesky)/cholesky | solution.py:45
  420.5 1.8 convolution_subtract_fusion.6
  422.3 11.7 %cholesky.562 = f32[128,128]{1,0:T(8,128)S(1)} custom-call(f32[128,128]{1,0:T(8,128)S(1)} %convolution_subtract_fusion.6), custom_call_target="Cholesky" | custom-call | tf_op jit(solution)/shard_map/jit(cholesky)/cholesky | solution.py:45
  441.0 6.6 %fusion.6 = (f32[1024,1024]{1,0:T(8,128)}, f32[1024,1024]{1,0:T(8,128)}) fusion(f32[1024,1024]{1,0:T(8,128)} %get-tuple-element.75, pred[]{:T(512)S(6)} %cholesky.576), kind=kLoop, calls=%fused_computation.13 | loop fusion | flops 4194304 | bytes 12582913 | tf_op jit(solution)/shard_map/triangular_solve | solution.py:46
  447.5 22.6 %while.14 = (s32[]{:T(128)}, f32[1024,1024]{1,0:T(8,128)}, s32[8,2]{0,1:T(2,128)S(1)}, f32[8,128,128]{2,1,0:T(8,128)S(1)}, s32[]{:T(128)}) while((s32[]{:T(128)}, f32[1024,1024]{1,0:T(8,128)}, s32[8,2]{0,1:T(2,128)S(1)}, f32[8,128,128]{2,1,0:T(8,128)S(1)}, s32[]{:T(128)}) %tuple.80), condition=%wide.while_cond, body=%wide.while_body.sunk | while | flops 2 | bytes 131181 | solution.py:46
  448.1 2.2 bitcast_dynamic-update-slice_fusion.2
  451.0 2.2 bitcast_dynamic-update-slice_fusion.2
  453.8 2.2 bitcast_dynamic-update-slice_fusion.2
  456.6 2.2 bitcast_dynamic-update-slice_fusion.2
  459.5 2.2 bitcast_dynamic-update-slice_fusion.2
  462.3 2.2 bitcast_dynamic-update-slice_fusion.2
  465.1 2.2 bitcast_dynamic-update-slice_fusion.2
  468.0 2.1 bitcast_dynamic-update-slice_fusion.2
  470.1 78.6 %custom-call.69 = f32[8,128,128]{1,2,0:T(8,128)S(1)} custom-call(f32[8,128,128]{2,1,0:T(8,128)S(1)} %get-tuple-element.45), custom_call_target="InvertDiagBlocksLowerTriangular" | custom-call | tf_op jit(solution)/shard_map/triangular_solve | solution.py:46
  551.4 1.2 fusion.21
  552.9 1.2 fusion.15
  554.3 1.4 fusion.19
  555.9 1.4 fusion.17
  557.5 1.5 fusion.13
  (93 shorter events, 25.7 us)
Async XLA Ops:
  7.2 46.6 %copy-start = (f32[32,1024]{1,0:T(8,128)S(1)}, f32[32,1024]{1,0:T(8,128)}, u32[]{:S(2)}) copy-start(f32[32,1024]{1,0:T(8,128)} %param.10) | copy-start | bytes 393220
  7.2 138.1 %reduce-scatter.2.cloned.1.call-start = ((), (), s32[]{:S(2)}) async-start(), calls=%async_computation.1 | async-start | bytes 4718592 | tf_op jit(solution)/shard_map/reduce_scatter | solution.py:37
  7.9 7.2 %copy-start.2 = (bf16[4096]{0:T(1024)(128)(2,1)S(1)}, bf16[4096]{0:T(1024)(128)(2,1)}, u32[]{:S(2)}) copy-start(bf16[4096]{0:T(1024)(128)(2,1)} %param.8) | copy-start | bytes 24580
  60.4 125.8 %copy-start.3 = (f32[32]{0:T(128)S(1)}, f32[32]{0:T(128)}, u32[]{:S(2)}) copy-start(f32[32]{0:T(128)} %param.11) | copy-start | bytes 388
  60.4 126.0 %copy-start.5 = (u32[32]{0:T(128)S(1)}, u32[32]{0:T(128)}, u32[]{:S(2)}) copy-start(u32[32]{0:T(128)} %constant.332) | copy-start | bytes 388
  60.4 125.7 %all-reduce.4.cloned.1.call-start = ((), (), s32[]{:S(2)}) async-start(), calls=%async_computation.2 | async-start | bytes 1048576 | tf_op jit(solution)/shard_map/psum | solution.py:40
  145.4 80.3 %all-gather.3.cloned.1.call-start = ((), (), s32[]{:S(2)}) async-start(), calls=%async_computation.3 | async-start | bytes 4718592 | tf_op jit(solution)/shard_map/all_gather | solution.py:42
  235.8 1.9 copy-start.1
  561.3 0.6 copy-start.4
Sparse Core Ops, SparseCore 0:
  60.5 84.7 reduce-scatter.1
  147.8 38.2 all-reduce.3
  188.1 37.4 all-gather.2
where the time goes:
time: 574 us; the launch traced here: 569 us
  other arithmetic  269 us (47%)
  waiting for transfers between devices  132 us (23%)
  matrix products  70.6 us (12%)
  local copies, waits for them, and re-layouts  44.3 us (8%)
  blocking collectives  31.4 us (5%)
  between operations  20.6 us (4%)
    another operation x30, other arithmetic, local(): factor = jnp.linalg.cholesky(total_gram)  172 us
    another operation x3, other arithmetic, local(): lax.linalg.triangular_solve(factor, total_info[:, None], left_side=True,...  85.2 us
    reduce_scatter x1, waiting for transfers between devices, local(): lax.psum_scatter(gram_local, 'blk', scatter_dimension=0, tiled=True)  84.9 us
    psum x1, waiting for transfers between devices, local(): share_gram, share_info = lax.psum((share_gram, share_info), 'fibre')  40.7 us
    dot_general x4, matrix products, add_block(): lax.dot_general(row_piece, row_piece, (((0,), (0,)), ((), ())), preferred...  24.5 us
    another operation x14, matrix products, local(): factor = jnp.linalg.cholesky(total_gram)  23.1 us
    another operation x24, local copies, waits for them, and re-layouts  22.4 us
    unnamed x1, blocking collectives  13 us
  transfers between devices with their start and end apart: 3, of which 3 were waited for; matrix products, arithmetic and copies ran while one was open for 0% of the time, Pallas kernels for 0%

commit v1 on v0

v1 whole, which is shorter than its diff:
```python
import functools

import jax
import jax.numpy as jnp
from jax import lax
from jax.experimental import pallas as pl
from jax.experimental.pallas import tpu as pltpu
from jax.sharding import PartitionSpec as P

F32 = jnp.float32
BF16 = jnp.bfloat16
NB = 128
VMEM = pltpu.CompilerParams(vmem_limit_bytes=56 * 2**20)


def split(x):
    hi = x.astype(BF16)
    return hi, (x - hi.astype(F32)).astype(BF16)


def block_at(width):
    nb = width // NB
    places, at = {}, 0
    for i in range(nb):
        for j in range(i, nb):
            places[i, j] = at
            at += 1
    return places


def dot_t(a, b):
    return lax.dot_general(a, b, (((0,), (0,)), ((), ())), preferred_element_type=F32)


def gram_kernel(step_rows, half, at_ref, rows_ref, vals_ref, prior_ref, pinfo_ref, keep_ref, send_ref, acc, info):
    t = pl.program_id(0)
    width = rows_ref.shape[1]
    tile = min(256, width)
    live = at_ref[0] - t * step_rows

    @pl.when(t == 0)
    def _():
        p = prior_ref[...]
        hi = p.astype(BF16)
        rest = p - hi.astype(F32)
        mid = rest.astype(BF16)
        lo = (rest - mid.astype(F32)).astype(BF16)
        left = jnp.concatenate([hi, hi, mid, mid, hi, lo], axis=0)
        right = jnp.concatenate([hi, mid, hi, mid, lo, hi], axis=0)
        for i in range(0, width, tile):
            acc[i : i + tile, i:] = dot_t(left[:, i : i + tile], right[:, i:])
        info[...] = jnp.broadcast_to(
            jnp.dot(pinfo_ref[...], p, precision=lax.Precision.HIGHEST, preferred_element_type=F32), info.shape
        )

    @pl.when(live > 0)
    def _():
        place = lax.broadcasted_iota(jnp.int32, (step_rows, 1), 0)
        x = jnp.where(place < live, rows_ref[...], jnp.zeros((), BF16))
        for i in range(0, width, tile):
            acc[i : i + tile, i:] += dot_t(x[:, i : i + tile], x[:, i:])
        v = jnp.broadcast_to(vals_ref[pl.ds(t, 1), :], (8, step_rows)).astype(BF16)
        info[...] += jnp.dot(v, x, preferred_element_type=F32)

    @pl.when(t == pl.num_programs(0) - 1)
    def _():
        nb = width // NB
        total = nb * (nb + 1) // 2 * NB

        def pack(halves):
            for (i, j), at in block_at(width).items():
                out, off = halves[at * NB // half], at * NB % half
                out[off : off + NB, :] = acc[i * NB : (i + 1) * NB, j * NB : (j + 1) * NB]
            out, off = halves[(total - NB) // half], (total - NB) % half + NB // 2
            hw = NB // 2
            for b in range(2 * nb):
                out[off + b : off + b + 1, 0:hw] = info[0:1, b * hw : (b + 1) * hw]
            for at in range(total, 2 * half, NB):
                halves[at // half][at % half : at % half + NB, :] = jnp.zeros((NB, NB), F32)

        @pl.when(at_ref[1] == 0)
        def _():
            pack((keep_ref, send_ref))

        @pl.when(at_ref[1] != 0)
        def _():
            pack((send_ref, keep_ref))


def gram(readings, values, counts, prior_root, prior_info, side, half):
    cap, width = readings.shape
    step_rows = min(512, cap)
    steps = cap // step_rows
    scalars = jnp.stack([counts[0], side]).astype(jnp.int32)
    whole = pl.BlockSpec(memory_space=pltpu.VMEM)
    return pl.pallas_call(
        functools.partial(gram_kernel, step_rows, half),
        grid=(steps,),
        in_specs=[
            pl.BlockSpec(memory_space=pltpu.SMEM),
            pl.BlockSpec((step_rows, width), lambda t: (t, 0)),
            whole,
            whole,
            whole,
        ],
        out_specs=[whole, whole],
        out_shape=[jax.ShapeDtypeStruct((half, NB), F32)] * 2,
        scratch_shapes=[pltpu.VMEM((width, width), F32), pltpu.VMEM((8, width), F32)],
        compiler_params=VMEM,
        name="gram",
    )(scalars, readings, values.astype(F32).reshape(steps, step_rows), prior_root, prior_info.reshape(1, -1))


def lane_of(v, at):
    return jnp.broadcast_to(v[:, at : at + 1], v.shape)


def row_of(v, at):
    return jnp.broadcast_to(v[at : at + 1, :], v.shape)


def factor_block(a):
    a = list(a)
    n = len(a)
    lane = lax.broadcasted_iota(jnp.int32, (8, NB), 1)
    sub = lax.broadcasted_iota(jnp.int32, (8, NB), 0)
    pivots = []
    for g in range(n):
        c0 = 8 * g
        col = {i: [lane_of(a[i], c0 + k) for k in range(8)] for i in range(g, n)}
        p = {(u, v): row_of(col[g][v], u) for u in range(8) for v in range(u, 8)}
        inv = [None] * 8
        for k in range(8):
            inv[k] = 1.0 / p[k, k]
            for u in range(k + 1, 8):
                f = p[k, u] * inv[k]
                for v in range(u, 8):
                    p[u, v] = p[u, v] - f * p[k, v]
        pivot = p[0, 0]
        for k in range(1, 8):
            pivot = jnp.where(sub == k, p[k, k], pivot)
        pivots.append(pivot)
        mult = {}
        for i in range(g, n):
            c = col[i]
            for k in range(8):
                m = c[k] * inv[k]
                if i == g:
                    m = jnp.where(sub > k, m, 0.0)
                mult[i, k] = m
                for v in range(k + 1, 8):
                    c[v] = c[v] - m * p[k, v]
        w = a[g]
        rows = []
        inside = (lane >= c0) & (lane < c0 + 8)
        for k in range(8):
            row = row_of(w, k)
            one = lane == c0 + k
            rows.append(jnp.where(inside & (lane > c0 + k), 0.0, jnp.where(one, 1.0, row)))
            if k < 7:
                w = jnp.where(one & (sub > k), 0.0, w) - mult[g, k] * jnp.where(one, 1.0, row)
        a[g] = w
        for i in range(g + 1, n):
            s = jnp.where(inside, 0.0, a[i])
            for k in range(8):
                s = s - mult[i, k] * rows[k]
            a[i] = s
    return a, pivots


def factor_kernel(pieces, at_ref, own_ref, far_ref, root_ref, info_ref, g, s, minv, r, uhi, ulo, y):
    nb = r.shape[0] // NB
    width = r.shape[1]
    place = block_at(width)
    side, quarter, layer = at_ref[0], at_ref[1], at_ref[2]
    n_quarter, n_layer, piece = pieces
    for ms in range(n_quarter):
        for mz in range(n_layer):
            for mc, ref in enumerate((own_ref, far_ref)):
                to = (((side ^ mc) * n_quarter + (quarter ^ ms)) * n_layer + (layer ^ mz)) * piece
                at = (ms * n_layer + mz) * piece
                g[pl.ds(pl.multiple_of(to, 8), piece), :] = ref[at : at + piece, :]

    last = place[nb - 1, nb - 1] * NB
    hw = NB // 2
    block = g[last : last + NB, :]
    mirror = block.T
    for b in range(nb):
        y[8 * b : 8 * b + 8, :] = jnp.broadcast_to(
            jnp.concatenate([block[hw + 2 * b : hw + 2 * b + 1, 0:hw], block[hw + 2 * b + 1 : hw + 2 * b + 2, 0:hw]], axis=1),
            (8, NB),
        )
    lane = lax.broadcasted_iota(jnp.int32, (hw, NB), 1)
    g[last + hw : last + NB, :] = jnp.where(lane < hw, mirror[hw:, :], block[hw:, :])

    s[:, 0:NB] = g[0:NB, :]
    lane = lax.broadcasted_iota(jnp.int32, (8, NB), 1)
    sub = lax.broadcasted_iota(jnp.int32, (8, NB), 0)

    def step(i, carry):
        a, pivots = factor_block([s[8 * u : 8 * u + 8, 0:NB] for u in range(NB // 8)])
        here = pl.multiple_of(i * NB, NB)
        for u in range(NB // 8):
            scale = lax.rsqrt(pivots[u])
            row = sub + 8 * u
            v = a[u] * scale
            s[8 * u : 8 * u + 8, 0:NB] = jnp.where(lane >= row, v, 0.0)
            minv[8 * u : 8 * u + 8, :] = jnp.where(lane < row, v, jnp.where(lane == row, scale, 0.0))
        for at in range(nb):
            @pl.when(i == at)
            def _():
                lo, hi = at * NB, at * NB + NB
                if at:
                    r[lo:hi, 0:lo] = jnp.zeros((NB, lo), F32)
                r[lo:hi, lo:hi] = s[:, 0:NB]
                m = minv[...]
                b = y[8 * at : 8 * at + 8, :]
                yi = lax.dot_general(
                    b, m, (((1,), (1,)), ((), ())), precision=lax.Precision.HIGHEST, preferred_element_type=F32
                )
                y[8 * at : 8 * at + 8, :] = yi
                if at + 1 < nb:
                    mh, ml = split(m)
                    rest = g_row(at, hi)
                    sh, sl = split(rest)
                    u = jnp.dot(
                        jnp.concatenate([mh, mh, ml], axis=1),
                        jnp.concatenate([sh, sl, sh], axis=0),
                        preferred_element_type=F32,
                    )
                    r[lo:hi, hi:] = u
                    uh, ul = split(u)
                    uhi[lo:hi, hi:] = uh
                    ulo[lo:hi, hi:] = ul
                    for b in range(at + 1, nb):
                        y[8 * b : 8 * b + 8, :] -= jnp.dot(
                            yi, u[:, b * NB - hi : b * NB - hi + NB],
                            precision=lax.Precision.HIGHEST, preferred_element_type=F32,
                        )
                    end = hi + NB
                    fh, fl = uhi[0:hi, hi:end], ulo[0:hi, hi:end]
                    for b in range(at + 1, nb):
                        c = slice(b * NB, b * NB + NB)
                        k = place[at + 1, b] * NB
                        t = g[k : k + NB, :] - (
                            dot_t(fh, uhi[0:hi, c]) + dot_t(fh, ulo[0:hi, c]) + dot_t(fl, uhi[0:hi, c])
                        )
                        if b == at + 1:
                            s[:, 0:NB] = t
                        else:
                            g[k : k + NB, :] = t
        return carry

    def g_row(i, start):
        return jnp.concatenate([g[place[i, j] * NB : place[i, j] * NB + NB, :] for j in range(start // NB, nb)], axis=1)

    lax.fori_loop(0, nb, step, 0)
    rows = root_ref.shape[0]
    root_ref[...] = r[pl.ds(pl.multiple_of(at_ref[3] * rows, 8), rows), :]
    for b in range(nb):
        info_ref[b : b + 1, :] = y[8 * b : 8 * b + 1, :]


def factor(own, far, scalars, pieces, width, rows):
    whole = pl.BlockSpec(memory_space=pltpu.VMEM)
    nb = width // NB
    return pl.pallas_call(
        functools.partial(factor_kernel, pieces),
        in_specs=[pl.BlockSpec(memory_space=pltpu.SMEM), whole, whole],
        out_specs=[whole, whole],
        out_shape=[jax.ShapeDtypeStruct((rows, width), F32), jax.ShapeDtypeStruct((nb, NB), F32)],
        scratch_shapes=[
            pltpu.VMEM((2 * own.shape[0], NB), F32),
            pltpu.VMEM((NB, NB), F32),
            pltpu.VMEM((NB, NB), F32),
            pltpu.VMEM((width, width), F32),
            pltpu.VMEM((width, width), BF16),
            pltpu.VMEM((width, width), BF16),
            pltpu.VMEM((8 * nb, NB), F32),
        ],
        compiler_params=VMEM,
        name="factor",
    )(scalars, own, far)


def swap(x, axis, mask):
    n = lax.axis_size(axis)
    return lax.ppermute(x, axis, [(d, d ^ mask) for d in range(n)])


def exchange_sum(parts, axis, masks, me):
    count = len(masks) + 1
    rows = parts[0].shape[0] // count

    def share(mask):
        terms = [lax.dynamic_slice_in_dim(x, (me ^ mask) * rows, rows, 0) for x in parts]
        return functools.reduce(lambda a, b: a + b, terms)

    out = [swap(share(m), axis, masks[m - 1]) for m in range(1, count)]
    return [share(0)] + out


def gather(x, axis, masks):
    return jnp.concatenate([x] + [swap(x, axis, m) for m in masks], axis=0)


def local(readings, values, counts, prior_root, prior_info):
    width = readings.shape[1]
    n_blk, n_fibre = lax.axis_size("blk"), lax.axis_size("fibre")
    blk, fibre = lax.axis_index("blk"), lax.axis_index("fibre")
    nb = width // NB
    unit = 8 * n_blk * n_fibre
    total = -(-(nb * (nb + 1) // 2 * NB) // unit) * unit
    half = total // 2
    side, quarter, layer = blk % 2, blk // 2, fibre
    quarters = [2 * m for m in range(1, n_blk // 2)]
    layers = list(range(1, n_fibre))

    keep, send = gram(readings, values, counts, prior_root, prior_info, side, half)
    parts = [keep, swap(send, "blk", 1)]
    parts = exchange_sum(parts, "blk", quarters, quarter)
    parts = exchange_sum(parts, "fibre", layers, layer)
    piece = functools.reduce(lambda a, b: a + b, parts)
    own = gather(gather(piece, "fibre", layers), "blk", quarters)
    far = swap(own, "blk", 1)
    scalars = jnp.stack([side, quarter, layer, blk]).astype(jnp.int32)
    rows = width // n_blk
    root, info = factor(own, far, scalars, (n_blk // 2, n_fibre, piece.shape[0]), width, rows)
    return root, info.reshape(width)


def solution(mesh):
    placed = (
        P(("fibre", "blk"), None),
        P(("fibre", "blk")),
        P(("fibre", "blk")),
        P(("fibre", "blk"), None),
        P(("fibre", "blk")),
    )
    return jax.shard_map(
        local, mesh=mesh, in_specs=placed, out_specs=(P("blk", None), P()), check_vma=False
    )
```

time: 574 us -> 123 us (0.21)
  other arithmetic: 269 us -> 2.9 us
  waiting for transfers between devices: 132 us -> 38.9 us
  matrix products: 70.6 us -> 0 us
  Pallas kernels: 0 us -> 60.6 us
  local copies, waits for them, and re-layouts: 44.3 us -> 2.4 us
  blocking collectives: 31.4 us -> 0 us
  between operations: 20.6 us -> 1.36 us
  starting transfers between devices: 0.12 us -> 16.7 us
    another operation x33 -> x2, other arithmetic: 258 us -> 1.44 us  [the longest x1 0.79 us: local(): scalars = jnp.stack([side, quarter, layer, blk]).astype(jnp.int32)]
    reduce_scatter x1 -> x0, waiting for transfers between devices: 84.9 us -> none  [local(): lax.psum_scatter(gram_local, 'blk', scatter_dimension=0, tiled=True)]
    pallas_call x0 -> x2, Pallas kernels: none -> 60.6 us  [the longest x1 48.3 us: factor(): pl.pallas_call(functools.partial(factor_kernel, pieces), in_specs=[pl.Blo...]
    psum x1 -> x0, waiting for transfers between devices: 40.7 us -> none  [local(): share_gram, share_info = lax.psum((share_gram, share_info), 'fibre')]
    ppermute x0 -> x14, waiting for transfers between devices: none -> 38.9 us  [swap(): return lax.ppermute(x, axis, [(d, d ^ mask) for d in range(n)])]
    dot_general x10 -> x0, matrix products: 37.1 us -> none  [the longest x4 24.5 us: add_block(): lax.dot_general(row_piece, row_piece, (((0,), (0,)), ((), ())), preferred...]
    another operation x29 -> x0, matrix products: 33.5 us -> none  [the longest x14 23.1 us: local(): factor = jnp.linalg.cholesky(total_gram)]
    another operation x33 -> x0, local copies, waits for them, and re-layouts: 25 us -> none
  transfers between devices with their start and end apart: 3 -> 14, of which waited for: 3 -> 11; matrix products, arithmetic and copies ran while one was open for 0% -> 1% of each run, Pallas kernels for 0% -> 0%
where the time goes in v1:
time: 123 us
  Pallas kernels  60.6 us (49%)
  waiting for transfers between devices  38.9 us (32%)
  starting transfers between devices  16.7 us (14%)
  other arithmetic  2.9 us (2%)
  local copies, waits for them, and re-layouts  2.4 us (2%)
  between operations  1.36 us (1%)
    pallas_call x1, Pallas kernels, factor(): pl.pallas_call(functools.partial(factor_kernel, pieces), in_specs=[pl.Blo...  48.3 us
    ppermute x14, waiting for transfers between devices, swap(): return lax.ppermute(x, axis, [(d, d ^ mask) for d in range(n)])  38.9 us
    ppermute x14, starting transfers between devices, swap(): return lax.ppermute(x, axis, [(d, d ^ mask) for d in range(n)])  16.7 us
    pallas_call x1, Pallas kernels, gram(): pl.pallas_call(functools.partial(gram_kernel, step_rows, half), grid=(ste...  12.3 us
  transfers between devices with their start and end apart: 14, of which 11 were waited for; matrix products, arithmetic and copies ran while one was open for 1% of the time, Pallas kernels for 0%

profile of v1, /device:TPU:0, one launch (start us, length us, event | category | flops | bytes accessed | tf_op | source)
XLA Modules:
  0.0 122.9 jit_solution(3021555252741507944)
XLA Ops:
  1.3 1.3 %reshape.20.vals_ref = f32[8,512]{1,0:T(8,128)} reshape(bf16[4096]{0:T(1024)(128)(2,1)} %param.6) | data formatting | bytes 24576 | tf_op jit(solution)/shard_map/reshape | solution.py:111
  2.6 0.6 pad_add_fusion.1.at_ref
  3.3 12.3 %gram.1 = (f32[2304,128]{1,0:T(8,128)}, f32[2304,128]{1,0:T(8,128)}) custom-call(s32[2]{0:T(128)} %pad_add_fusion.1.at_ref, bf16[4096,1024]{1,0:T(8,128)(2,1)} %rows_ref.1, f32[8,512]{1,0:T(8,128)} %reshape.20.vals_ref, f32[32,1024]{1,0:T(8,128)} %prior_ref.1, f32[1,32]{1,0:T(1,128)} %bitcast.6), custom_call_target="tpu_custom_call" | custom-call | tf_op jit(solution)/shard_map/gram/pallas_call | solution.py:96
  15.6 0.0 collective-permute-start
  15.6 3.1 %collective-permute-done = f32[2304,128]{1,0:T(8,128)S(1)} collective-permute-done((f32[2304,128]{1,0:T(8,128)}, f32[2304,128]{1,0:T(8,128)S(1)}, u32[]{:S(2)}, u32[]{:S(2)}) %collective-permute-start) | collective-permute-done | bytes 1179680 | tf_op jit(solution)/shard_map/ppermute | solution.py:288
  18.7 1.3 %dynamic-slice_add_fusion.3 = (f32[576,128]{1,0:T(8,128)S(1)}, f32[576,128]{1,0:T(8,128)S(1)}, f32[576,128]{1,0:T(8,128)S(1)}, f32[576,128]{1,0:T(8,128)S(1)}) fusion(f32[2304,128]{1,0:T(8,128)S(1)} %collective-permute-done, s32[]{:T(128)S(6)} %select_n.53, f32[2304,128]{1,0:T(8,128)} %get-tuple-element.6, s32[]{:T(128)S(6)} %select_n.57, s32[]{:T(128)S(6)} %select_n.56, ...), kind=kLoop, calls=%fused_computation.4 | loop fusion | flops 294912 | bytes 3538960 | tf_op jit(solution)/shard_map/add | solution.py:297
  20.0 3.0 %collective-permute-start.3 = (f32[576,128]{1,0:T(8,128)S(1)}, f32[576,128]{1,0:T(8,128)S(1)}, u32[]{:S(2)}, u32[]{:S(2)}) collective-permute-start(f32[576,128]{1,0:T(8,128)S(1)} %get-tuple-element.13), channel_id=1, source_target_pairs={{0,6},{1,7},{2,4},{3,5},{4,2},{5,3},{6,0},{7,1},{8,14},{9,15},{10,... | collective-permute-start | bytes 884744 | tf_op jit(solution)/shard_map/ppermute | solution.py:288
  23.0 0.0 collective-permute-start.2
  23.0 0.6 collective-permute-start.1
  23.6 7.2 %collective-permute-done.3 = f32[576,128]{1,0:T(8,128)S(1)} collective-permute-done((f32[576,128]{1,0:T(8,128)S(1)}, f32[576,128]{1,0:T(8,128)S(1)}, u32[]{:S(2)}, u32[]{:S(2)}) %collective-permute-start.3) | collective-permute-done | bytes 294944 | tf_op jit(solution)/shard_map/ppermute | solution.py:288
  30.8 5.8 %collective-permute-done.2 = f32[576,128]{1,0:T(8,128)S(1)} collective-permute-done((f32[576,128]{1,0:T(8,128)S(1)}, f32[576,128]{1,0:T(8,128)S(1)}, u32[]{:S(2)}, u32[]{:S(2)}) %collective-permute-start.2) | collective-permute-done | bytes 294944 | tf_op jit(solution)/shard_map/ppermute | solution.py:288
  36.6 0.0 collective-permute-done.1
  36.6 0.1 dynamic-slice_add_fusion.6
  36.7 4.4 %collective-permute-start.6 = (f32[144,128]{1,0:T(8,128)S(1)}, f32[144,128]{1,0:T(8,128)S(1)}, u32[]{:S(2)}, u32[]{:S(2)}) collective-permute-start(f32[144,128]{1,0:T(8,128)S(1)} %get-tuple-element.17), channel_id=1, source_target_pairs={{0,24},{8,16},{16,8},{24,0},{1,25},{9,17},{17,9},{25,1},{2,26},{10... | collective-permute-start | bytes 221192 | tf_op jit(solution)/shard_map/ppermute | solution.py:288
  41.0 0.0 collective-permute-start.5
  41.0 0.6 collective-permute-start.4
  41.7 2.4 %collective-permute-done.6 = f32[144,128]{1,0:T(8,128)S(1)} collective-permute-done((f32[144,128]{1,0:T(8,128)S(1)}, f32[144,128]{1,0:T(8,128)S(1)}, u32[]{:S(2)}, u32[]{:S(2)}) %collective-permute-start.6) | collective-permute-done | bytes 73760 | tf_op jit(solution)/shard_map/ppermute | solution.py:288
  44.1 3.6 %collective-permute-done.5 = f32[144,128]{1,0:T(8,128)S(1)} collective-permute-done((f32[144,128]{1,0:T(8,128)S(1)}, f32[144,128]{1,0:T(8,128)S(1)}, u32[]{:S(2)}, u32[]{:S(2)}) %collective-permute-start.5) | collective-permute-done | bytes 73760 | tf_op jit(solution)/shard_map/ppermute | solution.py:288
  47.7 0.0 collective-permute-done.4
  47.7 0.8 collective-permute-start.7
  48.5 2.3 %collective-permute-start.8 = (f32[144,128]{1,0:T(8,128)S(1)}, f32[144,128]{1,0:T(8,128)S(1)}, u32[]{:S(2)}, u32[]{:S(2)}) collective-permute-start(f32[144,128]{1,0:T(8,128)S(1)} %get-tuple-element.11), channel_id=1, source_target_pairs={{0,16},{8,24},{16,0},{24,8},{1,17},{9,25},{17,1},{25,9},{2,18},{10... | collective-permute-start | bytes 221192 | tf_op jit(solution)/shard_map/ppermute | solution.py:288
  50.8 1.3 %collective-permute-start.9 = (f32[144,128]{1,0:T(8,128)S(1)}, f32[144,128]{1,0:T(8,128)S(1)}, u32[]{:S(2)}, u32[]{:S(2)}) collective-permute-start(f32[144,128]{1,0:T(8,128)S(1)} %get-tuple-element.11), channel_id=1, source_target_pairs={{0,24},{8,16},{16,8},{24,0},{1,25},{9,17},{17,9},{25,1},{2,26},{10... | collective-permute-start | bytes 221192 | tf_op jit(solution)/shard_map/ppermute | solution.py:288
  52.2 0.2 collective-permute-done.7
  52.4 3.2 %collective-permute-done.8 = f32[144,128]{1,0:T(8,128)S(1)} collective-permute-done((f32[144,128]{1,0:T(8,128)S(1)}, f32[144,128]{1,0:T(8,128)S(1)}, u32[]{:S(2)}, u32[]{:S(2)}) %collective-permute-start.8) | collective-permute-done | bytes 73760 | tf_op jit(solution)/shard_map/ppermute | solution.py:288
  55.6 1.5 %collective-permute-done.9 = f32[144,128]{1,0:T(8,128)S(1)} collective-permute-done((f32[144,128]{1,0:T(8,128)S(1)}, f32[144,128]{1,0:T(8,128)S(1)}, u32[]{:S(2)}, u32[]{:S(2)}) %collective-permute-start.9) | collective-permute-done | bytes 73760 | tf_op jit(solution)/shard_map/ppermute | solution.py:288
  57.1 0.6 collective-permute-start.10
  57.7 0.8 collective-permute-start.11
  58.6 2.1 %collective-permute-start.12 = (f32[576,128]{1,0:T(8,128)S(1)}, f32[576,128]{1,0:T(8,128)S(1)}, u32[]{:S(2)}, u32[]{:S(2)}) collective-permute-start(f32[576,128]{1,0:T(8,128)S(1)} %pad_maximum_fusion), channel_id=1, source_target_pairs={{0,6},{1,7},{2,4},{3,5},{4,2},{5,3},{6,0},{7,1},{8,14},{9,15},{10,... | collective-permute-start | bytes 884744 | tf_op jit(solution)/shard_map/ppermute | solution.py:288
  60.7 6.0 %collective-permute-done.10 = f32[576,128]{1,0:T(8,128)S(1)} collective-permute-done((f32[576,128]{1,0:T(8,128)S(1)}, f32[576,128]{1,0:T(8,128)S(1)}, u32[]{:S(2)}, u32[]{:S(2)}) %collective-permute-start.10) | collective-permute-done | bytes 294944 | tf_op jit(solution)/shard_map/ppermute | solution.py:288
  66.7 4.0 %collective-permute-done.11 = f32[576,128]{1,0:T(8,128)S(1)} collective-permute-done((f32[576,128]{1,0:T(8,128)S(1)}, f32[576,128]{1,0:T(8,128)S(1)}, u32[]{:S(2)}, u32[]{:S(2)}) %collective-permute-start.11) | collective-permute-done | bytes 294944 | tf_op jit(solution)/shard_map/ppermute | solution.py:288
  70.7 0.0 collective-permute-done.12
  70.7 0.0 copy-start
  70.7 0.1 collective-permute-start.13
  70.8 0.8 pad_add_fusion.at_ref
  71.6 2.0 %collective-permute-done.13.far_ref = f32[2304,128]{1,0:T(8,128)S(1)} collective-permute-done((f32[2304,128]{1,0:T(8,128)S(1)}, f32[2304,128]{1,0:T(8,128)S(1)}, u32[]{:S(2)}, u32[]{:S(2)}) %collective-permute-start.13) | collective-permute-done | bytes 1179680 | tf_op jit(solution)/shard_map/ppermute | solution.py:288
  73.7 0.0 copy-done
  73.7 0.0 copy-start.1
  73.7 1.0 copy-done.1
  74.7 48.3 %factor.1 = (f32[128,1024]{1,0:T(8,128)}, f32[8,128]{1,0:T(8,128)}) custom-call(s32[4]{0:T(128)} %pad_add_fusion.at_ref, f32[2304,128]{1,0:T(8,128)} %copy-done, f32[2304,128]{1,0:T(8,128)} %copy-done.1), custom_call_target="tpu_custom_call" | custom-call | tf_op jit(solution)/shard_map/factor/pallas_call | solution.py:267
  (8 shorter events, 0.1 us)
Async XLA Ops:
  15.6 3.1 %collective-permute-start = (f32[2304,128]{1,0:T(8,128)}, f32[2304,128]{1,0:T(8,128)S(1)}, u32[]{:S(2)}, u32[]{:S(2)}) collective-permute-start(f32[2304,128]{1,0:T(8,128)} %get-tuple-element.7), channel_id=1, source_target_pairs={{0,1},{1,0},{2,3},{3,2},{4,5},{5,4},{6,7},{7,6},{8,9},{9,8},{10,11... | collective-permute-start | bytes 3538952 | tf_op jit(solution)/shard_map/ppermute | solution.py:288
  20.0 10.8 %collective-permute-start.3 = (f32[576,128]{1,0:T(8,128)S(1)}, f32[576,128]{1,0:T(8,128)S(1)}, u32[]{:S(2)}, u32[]{:S(2)}) collective-permute-start(f32[576,128]{1,0:T(8,128)S(1)} %get-tuple-element.13), channel_id=1, source_target_pairs={{0,6},{1,7},{2,4},{3,5},{4,2},{5,3},{6,0},{7,1},{8,14},{9,15},{10,... | collective-permute-start | bytes 884744 | tf_op jit(solution)/shard_map/ppermute | solution.py:288
  23.0 13.6 %collective-permute-start.2 = (f32[576,128]{1,0:T(8,128)S(1)}, f32[576,128]{1,0:T(8,128)S(1)}, u32[]{:S(2)}, u32[]{:S(2)}) collective-permute-start(f32[576,128]{1,0:T(8,128)S(1)} %get-tuple-element.14), channel_id=1, source_target_pairs={{0,4},{1,5},{2,6},{3,7},{4,0},{5,1},{6,2},{7,3},{8,12},{9,13},{10,... | collective-permute-start | bytes 884744 | tf_op jit(solution)/shard_map/ppermute | solution.py:288
  23.0 13.6 %collective-permute-start.1 = (f32[576,128]{1,0:T(8,128)S(1)}, f32[576,128]{1,0:T(8,128)S(1)}, u32[]{:S(2)}, u32[]{:S(2)}) collective-permute-start(f32[576,128]{1,0:T(8,128)S(1)} %get-tuple-element.15), channel_id=1, source_target_pairs={{0,2},{1,3},{2,0},{3,1},{4,6},{5,7},{6,4},{7,5},{8,10},{9,11},{10,... | collective-permute-start | bytes 884744 | tf_op jit(solution)/shard_map/ppermute | solution.py:288
  36.7 7.4 %collective-permute-start.6 = (f32[144,128]{1,0:T(8,128)S(1)}, f32[144,128]{1,0:T(8,128)S(1)}, u32[]{:S(2)}, u32[]{:S(2)}) collective-permute-start(f32[144,128]{1,0:T(8,128)S(1)} %get-tuple-element.17), channel_id=1, source_target_pairs={{0,24},{8,16},{16,8},{24,0},{1,25},{9,17},{17,9},{25,1},{2,26},{10... | collective-permute-start | bytes 221192 | tf_op jit(solution)/shard_map/ppermute | solution.py:288
  41.0 6.6 %collective-permute-start.5 = (f32[144,128]{1,0:T(8,128)S(1)}, f32[144,128]{1,0:T(8,128)S(1)}, u32[]{:S(2)}, u32[]{:S(2)}) collective-permute-start(f32[144,128]{1,0:T(8,128)S(1)} %get-tuple-element.18), channel_id=1, source_target_pairs={{0,16},{8,24},{16,0},{24,8},{1,17},{9,25},{17,1},{25,9},{2,18},{10... | collective-permute-start | bytes 221192 | tf_op jit(solution)/shard_map/ppermute | solution.py:288
  41.0 6.6 %collective-permute-start.4 = (f32[144,128]{1,0:T(8,128)S(1)}, f32[144,128]{1,0:T(8,128)S(1)}, u32[]{:S(2)}, u32[]{:S(2)}) collective-permute-start(f32[144,128]{1,0:T(8,128)S(1)} %get-tuple-element.16), channel_id=1, source_target_pairs={{0,8},{8,0},{16,24},{24,16},{1,9},{9,1},{17,25},{25,17},{2,10},{10... | collective-permute-start | bytes 221192 | tf_op jit(solution)/shard_map/ppermute | solution.py:288
  47.7 4.7 %collective-permute-start.7 = (f32[144,128]{1,0:T(8,128)S(1)}, f32[144,128]{1,0:T(8,128)S(1)}, u32[]{:S(2)}, u32[]{:S(2)}) collective-permute-start(f32[144,128]{1,0:T(8,128)S(1)} %get-tuple-element.11), channel_id=1, source_target_pairs={{0,8},{8,0},{16,24},{24,16},{1,9},{9,1},{17,25},{25,17},{2,10},{10... | collective-permute-start | bytes 221192 | tf_op jit(solution)/shard_map/ppermute | solution.py:288
  48.5 7.1 %collective-permute-start.8 = (f32[144,128]{1,0:T(8,128)S(1)}, f32[144,128]{1,0:T(8,128)S(1)}, u32[]{:S(2)}, u32[]{:S(2)}) collective-permute-start(f32[144,128]{1,0:T(8,128)S(1)} %get-tuple-element.11), channel_id=1, source_target_pairs={{0,16},{8,24},{16,0},{24,8},{1,17},{9,25},{17,1},{25,9},{2,18},{10... | collective-permute-start | bytes 221192 | tf_op jit(solution)/shard_map/ppermute | solution.py:288
  50.8 6.3 %collective-permute-start.9 = (f32[144,128]{1,0:T(8,128)S(1)}, f32[144,128]{1,0:T(8,128)S(1)}, u32[]{:S(2)}, u32[]{:S(2)}) collective-permute-start(f32[144,128]{1,0:T(8,128)S(1)} %get-tuple-element.11), channel_id=1, source_target_pairs={{0,24},{8,16},{16,8},{24,0},{1,25},{9,17},{17,9},{25,1},{2,26},{10... | collective-permute-start | bytes 221192 | tf_op jit(solution)/shard_map/ppermute | solution.py:288
  57.1 9.6 %collective-permute-start.10 = (f32[576,128]{1,0:T(8,128)S(1)}, f32[576,128]{1,0:T(8,128)S(1)}, u32[]{:S(2)}, u32[]{:S(2)}) collective-permute-start(f32[576,128]{1,0:T(8,128)S(1)} %pad_maximum_fusion), channel_id=1, source_target_pairs={{0,2},{1,3},{2,0},{3,1},{4,6},{5,7},{6,4},{7,5},{8,10},{9,11},{10,... | collective-permute-start | bytes 884744 | tf_op jit(solution)/shard_map/ppermute | solution.py:288
  57.7 12.9 %collective-permute-start.11 = (f32[576,128]{1,0:T(8,128)S(1)}, f32[576,128]{1,0:T(8,128)S(1)}, u32[]{:S(2)}, u32[]{:S(2)}) collective-permute-start(f32[576,128]{1,0:T(8,128)S(1)} %pad_maximum_fusion), channel_id=1, source_target_pairs={{0,4},{1,5},{2,6},{3,7},{4,0},{5,1},{6,2},{7,3},{8,12},{9,13},{10,... | collective-permute-start | bytes 884744 | tf_op jit(solution)/shard_map/ppermute | solution.py:288
  58.6 12.1 %collective-permute-start.12 = (f32[576,128]{1,0:T(8,128)S(1)}, f32[576,128]{1,0:T(8,128)S(1)}, u32[]{:S(2)}, u32[]{:S(2)}) collective-permute-start(f32[576,128]{1,0:T(8,128)S(1)} %pad_maximum_fusion), channel_id=1, source_target_pairs={{0,6},{1,7},{2,4},{3,5},{4,2},{5,3},{6,0},{7,1},{8,14},{9,15},{10,... | collective-permute-start | bytes 884744 | tf_op jit(solution)/shard_map/ppermute | solution.py:288
  70.7 2.9 %copy-start = (f32[2304,128]{1,0:T(8,128)}, f32[2304,128]{1,0:T(8,128)S(1)}, u32[]{:S(2)}) copy-start(f32[2304,128]{1,0:T(8,128)S(1)} %constant_dynamic-update-slice_fusion.own_ref) | copy-start | bytes 3538948
  70.7 2.9 %collective-permute-start.13 = (f32[2304,128]{1,0:T(8,128)S(1)}, f32[2304,128]{1,0:T(8,128)S(1)}, u32[]{:S(2)}, u32[]{:S(2)}) collective-permute-start(f32[2304,128]{1,0:T(8,128)S(1)} %constant_dynamic-update-slice_fusion.own_ref), channel_id=1, source_target_pairs={{0,1},{1,0},{2,3},{3,2},{4,5},{5,4},{6,7},{7,6},{8,9},{9,8},{10,11... | collective-permute-start | bytes 3538952 | tf_op jit(solution)/shard_map/ppermute | solution.py:288
  73.7 1.0 copy-start.1

commit v2 on v1

--- a/solution.py
+++ b/solution.py
@@ -119,53 +119,63 @@
     return jnp.broadcast_to(v[at : at + 1, :], v.shape)
 
 
-def factor_block(a):
-    a = list(a)
-    n = len(a)
+PANEL, STRIP = 16, 32
+
+
+def factor_block(read, write):
     lane = lax.broadcasted_iota(jnp.int32, (8, NB), 1)
     sub = lax.broadcasted_iota(jnp.int32, (8, NB), 0)
-    pivots = []
-    for g in range(n):
-        c0 = 8 * g
-        col = {i: [lane_of(a[i], c0 + k) for k in range(8)] for i in range(g, n)}
-        p = {(u, v): row_of(col[g][v], u) for u in range(8) for v in range(u, 8)}
-        inv = [None] * 8
-        for k in range(8):
-            inv[k] = 1.0 / p[k, k]
-            for u in range(k + 1, 8):
-                f = p[k, u] * inv[k]
-                for v in range(u, 8):
-                    p[u, v] = p[u, v] - f * p[k, v]
-        pivot = p[0, 0]
-        for k in range(1, 8):
-            pivot = jnp.where(sub == k, p[k, k], pivot)
-        pivots.append(pivot)
-        mult = {}
-        for i in range(g, n):
-            c = col[i]
-            for k in range(8):
-                m = c[k] * inv[k]
-                if i == g:
-                    m = jnp.where(sub > k, m, 0.0)
-                mult[i, k] = m
-                for v in range(k + 1, 8):
-                    c[v] = c[v] - m * p[k, v]
-        w = a[g]
-        rows = []
-        inside = (lane >= c0) & (lane < c0 + 8)
-        for k in range(8):
-            row = row_of(w, k)
-            one = lane == c0 + k
-            rows.append(jnp.where(inside & (lane > c0 + k), 0.0, jnp.where(one, 1.0, row)))
-            if k < 7:
-                w = jnp.where(one & (sub > k), 0.0, w) - mult[g, k] * jnp.where(one, 1.0, row)
-        a[g] = w
-        for i in range(g + 1, n):
-            s = jnp.where(inside, 0.0, a[i])
-            for k in range(8):
-                s = s - mult[i, k] * rows[k]
-            a[i] = s
-    return a, pivots
+    groups = NB // 8
+    per = STRIP // 8
+    a = [read(u) for u in range(groups)]
+    for t in range(NB // STRIP):
+        s0 = STRIP * t
+        w = a[per * t : per * t + per]
+        pivot = [None] * per
+        for panel in range(STRIP // PANEL):
+            g0 = panel * (PANEL // 8)
+            c0 = s0 + PANEL * panel
+            col = {}
+            for k in range(PANEL):
+                for i in range(g0 + k // 8, per):
+                    col[i, k] = lane_of(w[i], c0 + k)
+            d = row_of(col[g0, 0], 0)
+            inv = 1.0 / d
+            for k in range(PANEL):
+                gk, ks = g0 + k // 8, k % 8
+                pivot[gk] = d if ks == 0 else jnp.where(sub == ks, d, pivot[gk])
+                below = {v: row_of(col[g0 + v // 8, k], v % 8) for v in range(k + 1, PANEL)}
+                if k + 1 < PANEL:
+                    ahead = row_of(col[g0 + (k + 1) // 8, k + 1], (k + 1) % 8)
+                    d_next = ahead - (below[k + 1] * below[k + 1]) * inv
+                    inv_next = 1.0 / d_next
+                one = lane == c0 + k
+                row = jnp.where(one, 1.0, row_of(w[gk], ks))
+                for i in range(gk, per):
+                    m = col[i, k] * inv
+                    if i == gk:
+                        m = jnp.where(sub > ks, m, 0.0)
+                    for v in range(k + 1, PANEL):
+                        if i >= g0 + v // 8:
+                            col[i, v] = col[i, v] - m * below[v]
+                    gone = one & (sub > ks) if i == gk else one
+                    w[i] = jnp.where(gone, 0.0, w[i]) - m * row
+                if k + 1 < PANEL:
+                    d, inv = d_next, inv_next
+        inside = (lane >= s0) & (lane < s0 + STRIP)
+        scaled = []
+        for i in range(per):
+            scale = lax.rsqrt(pivot[i])
+            v = w[i] * scale
+            row = sub + (s0 + 8 * i)
+            lower = jnp.where(lane < row, v, jnp.where(lane == row, scale, 0.0))
+            write(per * t + i, jnp.where(lane >= row, v, 0.0), lower)
+            scaled.append(jnp.where(inside, lower, v))
+        if s0 + STRIP < NB:
+            hi, lo = split(jnp.concatenate(scaled, axis=0))
+            off = dot_t(jnp.concatenate([hi, hi, lo], axis=0), jnp.concatenate([hi, lo, hi], axis=0))
+            for i in range(per * (t + 1), groups):
+                a[i] = jnp.where(inside, 0.0, a[i]) - off[8 * i : 8 * i + 8, :]
 
 
 def factor_kernel(pieces, at_ref, own_ref, far_ref, root_ref, info_ref, g, s, minv, r, uhi, ulo, y):
@@ -194,18 +204,16 @@
     g[last + hw : last + NB, :] = jnp.where(lane < hw, mirror[hw:, :], block[hw:, :])
 
     s[:, 0:NB] = g[0:NB, :]
-    lane = lax.broadcasted_iota(jnp.int32, (8, NB), 1)
-    sub = lax.broadcasted_iota(jnp.int32, (8, NB), 0)
 
     def step(i, carry):
-        a, pivots = factor_block([s[8 * u : 8 * u + 8, 0:NB] for u in range(NB // 8)])
-        here = pl.multiple_of(i * NB, NB)
-        for u in range(NB // 8):
-            scale = lax.rsqrt(pivots[u])
-            row = sub + 8 * u
-            v = a[u] * scale
-            s[8 * u : 8 * u + 8, 0:NB] = jnp.where(lane >= row, v, 0.0)
-            minv[8 * u : 8 * u + 8, :] = jnp.where(lane < row, v, jnp.where(lane == row, scale, 0.0))
+        def read(u):
+            return s[8 * u : 8 * u + 8, 0:NB]
+
+        def write(u, upper, lower):
+            s[8 * u : 8 * u + 8, 0:NB] = upper
+            minv[8 * u : 8 * u + 8, :] = lower
+
+        factor_block(read, write)
         for at in range(nb):
             @pl.when(i == at)
             def _():

time: 123 us -> 107 us (0.87)
  Pallas kernels: 60.6 us -> 42.5 us
  starting transfers between devices: 16.7 us -> 18.9 us
    pallas_call x1, Pallas kernels: 48.3 us -> 32.1 us  [factor(): pl.pallas_call(functools.partial(factor_kernel, pieces), in_specs=[pl.Blo...]
    ppermute x14, starting transfers between devices: 16.7 us -> 18.9 us  [swap(): return lax.ppermute(x, axis, [(d, d ^ mask) for d in range(n)])]
    pallas_call x1, Pallas kernels: 12.3 us -> 10.4 us  [gram(): pl.pallas_call(functools.partial(gram_kernel, step_rows, half), grid=(ste...]
  transfers between devices with their start and end apart: 14 -> 14, of which waited for: 11 -> 13; matrix products, arithmetic and copies ran while one was open for 1% -> 1% of each run, Pallas kernels for 0% -> 0%
where the time goes in v2:
time: 107 us
  Pallas kernels  42.5 us (40%)
  waiting for transfers between devices  39.2 us (37%)
  starting transfers between devices  18.9 us (18%)
  other arithmetic  2.9 us (3%)
  local copies, waits for them, and re-layouts  2.4 us (2%)
  between operations  1.35 us (1%)
    ppermute x14, waiting for transfers between devices, swap(): return lax.ppermute(x, axis, [(d, d ^ mask) for d in range(n)])  39.2 us
    pallas_call x1, Pallas kernels, factor(): pl.pallas_call(functools.partial(factor_kernel, pieces), in_specs=[pl.Blo...  32.1 us
    ppermute x14, starting transfers between devices, swap(): return lax.ppermute(x, axis, [(d, d ^ mask) for d in range(n)])  18.9 us
    pallas_call x1, Pallas kernels, gram(): pl.pallas_call(functools.partial(gram_kernel, step_rows, half), grid=(ste...  10.4 us
  transfers between devices with their start and end apart: 14, of which 13 were waited for; matrix products, arithmetic and copies ran while one was open for 1% of the time, Pallas kernels for 0%

profile of v2, /device:TPU:0, one launch (start us, length us, event | category | flops | bytes accessed | tf_op | source)
XLA Modules:
  0.0 107.2 jit_solution(4951980667014789690)
XLA Ops:
  1.3 1.3 %reshape.20.vals_ref = f32[8,512]{1,0:T(8,128)} reshape(bf16[4096]{0:T(1024)(128)(2,1)} %param.6) | data formatting | bytes 24576 | tf_op jit(solution)/shard_map/reshape | solution.py:111
  2.6 0.6 pad_add_fusion.1.at_ref
  3.3 10.4 %gram.1 = (f32[2304,128]{1,0:T(8,128)}, f32[2304,128]{1,0:T(8,128)}) custom-call(s32[2]{0:T(128)} %pad_add_fusion.1.at_ref, bf16[4096,1024]{1,0:T(8,128)(2,1)} %rows_ref.1, f32[8,512]{1,0:T(8,128)} %reshape.20.vals_ref, f32[32,1024]{1,0:T(8,128)} %prior_ref.1, f32[1,32]{1,0:T(1,128)} %bitcast.6), custom_call_target="tpu_custom_call" | custom-call | tf_op jit(solution)/shard_map/gram/pallas_call | solution.py:96
  13.7 0.4 collective-permute-start
  14.1 2.7 %collective-permute-done = f32[2304,128]{1,0:T(8,128)S(1)} collective-permute-done((f32[2304,128]{1,0:T(8,128)}, f32[2304,128]{1,0:T(8,128)S(1)}, u32[]{:S(2)}, u32[]{:S(2)}) %collective-permute-start) | collective-permute-done | bytes 1179680 | tf_op jit(solution)/shard_map/ppermute | solution.py:296
  16.8 1.3 %dynamic-slice_add_fusion.3 = (f32[576,128]{1,0:T(8,128)S(1)}, f32[576,128]{1,0:T(8,128)S(1)}, f32[576,128]{1,0:T(8,128)S(1)}, f32[576,128]{1,0:T(8,128)S(1)}) fusion(f32[2304,128]{1,0:T(8,128)S(1)} %collective-permute-done, s32[]{:T(128)S(6)} %select_n.53, f32[2304,128]{1,0:T(8,128)} %get-tuple-element.6, s32[]{:T(128)S(6)} %select_n.57, s32[]{:T(128)S(6)} %select_n.56, ...), kind=kLoop, calls=%fused_computation.4 | loop fusion | flops 294912 | bytes 3538960 | tf_op jit(solution)/shard_map/add | solution.py:305
  18.1 3.9 %collective-permute-start.3 = (f32[576,128]{1,0:T(8,128)S(1)}, f32[576,128]{1,0:T(8,128)S(1)}, u32[]{:S(2)}, u32[]{:S(2)}) collective-permute-start(f32[576,128]{1,0:T(8,128)S(1)} %get-tuple-element.13), channel_id=1, source_target_pairs={{0,6},{1,7},{2,4},{3,5},{4,2},{5,3},{6,0},{7,1},{8,14},{9,15},{10,... | collective-permute-start | bytes 884744 | tf_op jit(solution)/shard_map/ppermute | solution.py:296
  22.0 0.7 collective-permute-start.2
  22.7 0.0 collective-permute-start.1
  22.7 7.1 %collective-permute-done.3 = f32[576,128]{1,0:T(8,128)S(1)} collective-permute-done((f32[576,128]{1,0:T(8,128)S(1)}, f32[576,128]{1,0:T(8,128)S(1)}, u32[]{:S(2)}, u32[]{:S(2)}) %collective-permute-start.3) | collective-permute-done | bytes 294944 | tf_op jit(solution)/shard_map/ppermute | solution.py:296
  29.8 5.8 %collective-permute-done.2 = f32[576,128]{1,0:T(8,128)S(1)} collective-permute-done((f32[576,128]{1,0:T(8,128)S(1)}, f32[576,128]{1,0:T(8,128)S(1)}, u32[]{:S(2)}, u32[]{:S(2)}) %collective-permute-start.2) | collective-permute-done | bytes 294944 | tf_op jit(solution)/shard_map/ppermute | solution.py:296
  35.6 0.4 collective-permute-done.1
  36.1 0.1 dynamic-slice_add_fusion.6
  36.2 5.2 %collective-permute-start.6 = (f32[144,128]{1,0:T(8,128)S(1)}, f32[144,128]{1,0:T(8,128)S(1)}, u32[]{:S(2)}, u32[]{:S(2)}) collective-permute-start(f32[144,128]{1,0:T(8,128)S(1)} %get-tuple-element.17), channel_id=1, source_target_pairs={{0,24},{8,16},{16,8},{24,0},{1,25},{9,17},{17,9},{25,1},{2,26},{10... | collective-permute-start | bytes 221192 | tf_op jit(solution)/shard_map/ppermute | solution.py:296
  41.3 0.0 collective-permute-start.5
  41.3 0.6 collective-permute-start.4
  42.0 2.5 %collective-permute-done.6 = f32[144,128]{1,0:T(8,128)S(1)} collective-permute-done((f32[144,128]{1,0:T(8,128)S(1)}, f32[144,128]{1,0:T(8,128)S(1)}, u32[]{:S(2)}, u32[]{:S(2)}) %collective-permute-start.6) | collective-permute-done | bytes 73760 | tf_op jit(solution)/shard_map/ppermute | solution.py:296
  44.5 2.9 %collective-permute-done.5 = f32[144,128]{1,0:T(8,128)S(1)} collective-permute-done((f32[144,128]{1,0:T(8,128)S(1)}, f32[144,128]{1,0:T(8,128)S(1)}, u32[]{:S(2)}, u32[]{:S(2)}) %collective-permute-start.5) | collective-permute-done | bytes 73760 | tf_op jit(solution)/shard_map/ppermute | solution.py:296
  47.3 0.0 collective-permute-done.4
  47.4 1.0 collective-permute-start.7
  48.4 1.8 %collective-permute-start.8 = (f32[144,128]{1,0:T(8,128)S(1)}, f32[144,128]{1,0:T(8,128)S(1)}, u32[]{:S(2)}, u32[]{:S(2)}) collective-permute-start(f32[144,128]{1,0:T(8,128)S(1)} %get-tuple-element.11), channel_id=1, source_target_pairs={{0,16},{8,24},{16,0},{24,8},{1,17},{9,25},{17,1},{25,9},{2,18},{10... | collective-permute-start | bytes 221192 | tf_op jit(solution)/shard_map/ppermute | solution.py:296
  50.2 1.7 %collective-permute-start.9 = (f32[144,128]{1,0:T(8,128)S(1)}, f32[144,128]{1,0:T(8,128)S(1)}, u32[]{:S(2)}, u32[]{:S(2)}) collective-permute-start(f32[144,128]{1,0:T(8,128)S(1)} %get-tuple-element.11), channel_id=1, source_target_pairs={{0,24},{8,16},{16,8},{24,0},{1,25},{9,17},{17,9},{25,1},{2,26},{10... | collective-permute-start | bytes 221192 | tf_op jit(solution)/shard_map/ppermute | solution.py:296
  51.8 0.3 collective-permute-done.7
  52.1 3.2 %collective-permute-done.8 = f32[144,128]{1,0:T(8,128)S(1)} collective-permute-done((f32[144,128]{1,0:T(8,128)S(1)}, f32[144,128]{1,0:T(8,128)S(1)}, u32[]{:S(2)}, u32[]{:S(2)}) %collective-permute-start.8) | collective-permute-done | bytes 73760 | tf_op jit(solution)/shard_map/ppermute | solution.py:296
  55.3 1.1 %collective-permute-done.9 = f32[144,128]{1,0:T(8,128)S(1)} collective-permute-done((f32[144,128]{1,0:T(8,128)S(1)}, f32[144,128]{1,0:T(8,128)S(1)}, u32[]{:S(2)}, u32[]{:S(2)}) %collective-permute-start.9) | collective-permute-done | bytes 73760 | tf_op jit(solution)/shard_map/ppermute | solution.py:296
  56.4 1.6 %collective-permute-start.10 = (f32[576,128]{1,0:T(8,128)S(1)}, f32[576,128]{1,0:T(8,128)S(1)}, u32[]{:S(2)}, u32[]{:S(2)}) collective-permute-start(f32[576,128]{1,0:T(8,128)S(1)} %pad_maximum_fusion), channel_id=1, source_target_pairs={{0,2},{1,3},{2,0},{3,1},{4,6},{5,7},{6,4},{7,5},{8,10},{9,11},{10,... | collective-permute-start | bytes 884744 | tf_op jit(solution)/shard_map/ppermute | solution.py:296
  58.1 0.5 collective-permute-start.11
  58.6 1.4 %collective-permute-start.12 = (f32[576,128]{1,0:T(8,128)S(1)}, f32[576,128]{1,0:T(8,128)S(1)}, u32[]{:S(2)}, u32[]{:S(2)}) collective-permute-start(f32[576,128]{1,0:T(8,128)S(1)} %pad_maximum_fusion), channel_id=1, source_target_pairs={{0,6},{1,7},{2,4},{3,5},{4,2},{5,3},{6,0},{7,1},{8,14},{9,15},{10,... | collective-permute-start | bytes 884744 | tf_op jit(solution)/shard_map/ppermute | solution.py:296
  60.0 6.4 %collective-permute-done.10 = f32[576,128]{1,0:T(8,128)S(1)} collective-permute-done((f32[576,128]{1,0:T(8,128)S(1)}, f32[576,128]{1,0:T(8,128)S(1)}, u32[]{:S(2)}, u32[]{:S(2)}) %collective-permute-start.10) | collective-permute-done | bytes 294944 | tf_op jit(solution)/shard_map/ppermute | solution.py:296
  66.5 2.9 %collective-permute-done.11 = f32[576,128]{1,0:T(8,128)S(1)} collective-permute-done((f32[576,128]{1,0:T(8,128)S(1)}, f32[576,128]{1,0:T(8,128)S(1)}, u32[]{:S(2)}, u32[]{:S(2)}) %collective-permute-start.11) | collective-permute-done | bytes 294944 | tf_op jit(solution)/shard_map/ppermute | solution.py:296
  69.4 1.8 %collective-permute-done.12 = f32[576,128]{1,0:T(8,128)S(1)} collective-permute-done((f32[576,128]{1,0:T(8,128)S(1)}, f32[576,128]{1,0:T(8,128)S(1)}, u32[]{:S(2)}, u32[]{:S(2)}) %collective-permute-start.12) | collective-permute-done | bytes 294944 | tf_op jit(solution)/shard_map/ppermute | solution.py:296
  71.2 0.0 copy-start
  71.2 0.1 collective-permute-start.13
  71.3 0.8 pad_add_fusion.at_ref
  72.1 2.0 %collective-permute-done.13.far_ref = f32[2304,128]{1,0:T(8,128)S(1)} collective-permute-done((f32[2304,128]{1,0:T(8,128)S(1)}, f32[2304,128]{1,0:T(8,128)S(1)}, u32[]{:S(2)}, u32[]{:S(2)}) %collective-permute-start.13) | collective-permute-done | bytes 1179680 | tf_op jit(solution)/shard_map/ppermute | solution.py:296
  74.1 0.0 copy-done
  74.1 0.0 copy-start.1
  74.1 1.0 copy-done.1
  75.1 32.1 %factor.1 = (f32[128,1024]{1,0:T(8,128)}, f32[8,128]{1,0:T(8,128)}) custom-call(s32[4]{0:T(128)} %pad_add_fusion.at_ref, f32[2304,128]{1,0:T(8,128)} %copy-done, f32[2304,128]{1,0:T(8,128)} %copy-done.1), custom_call_target="tpu_custom_call" | custom-call | tf_op jit(solution)/shard_map/factor/pallas_call | solution.py:275
  (8 shorter events, 0.1 us)
Async XLA Ops:
  13.7 3.1 %collective-permute-start = (f32[2304,128]{1,0:T(8,128)}, f32[2304,128]{1,0:T(8,128)S(1)}, u32[]{:S(2)}, u32[]{:S(2)}) collective-permute-start(f32[2304,128]{1,0:T(8,128)} %get-tuple-element.7), channel_id=1, source_target_pairs={{0,1},{1,0},{2,3},{3,2},{4,5},{5,4},{6,7},{7,6},{8,9},{9,8},{10,11... | collective-permute-start | bytes 3538952 | tf_op jit(solution)/shard_map/ppermute | solution.py:296
  18.1 11.7 %collective-permute-start.3 = (f32[576,128]{1,0:T(8,128)S(1)}, f32[576,128]{1,0:T(8,128)S(1)}, u32[]{:S(2)}, u32[]{:S(2)}) collective-permute-start(f32[576,128]{1,0:T(8,128)S(1)} %get-tuple-element.13), channel_id=1, source_target_pairs={{0,6},{1,7},{2,4},{3,5},{4,2},{5,3},{6,0},{7,1},{8,14},{9,15},{10,... | collective-permute-start | bytes 884744 | tf_op jit(solution)/shard_map/ppermute | solution.py:296
  22.0 13.6 %collective-permute-start.2 = (f32[576,128]{1,0:T(8,128)S(1)}, f32[576,128]{1,0:T(8,128)S(1)}, u32[]{:S(2)}, u32[]{:S(2)}) collective-permute-start(f32[576,128]{1,0:T(8,128)S(1)} %get-tuple-element.14), channel_id=1, source_target_pairs={{0,4},{1,5},{2,6},{3,7},{4,0},{5,1},{6,2},{7,3},{8,12},{9,13},{10,... | collective-permute-start | bytes 884744 | tf_op jit(solution)/shard_map/ppermute | solution.py:296
  22.7 13.4 %collective-permute-start.1 = (f32[576,128]{1,0:T(8,128)S(1)}, f32[576,128]{1,0:T(8,128)S(1)}, u32[]{:S(2)}, u32[]{:S(2)}) collective-permute-start(f32[576,128]{1,0:T(8,128)S(1)} %get-tuple-element.15), channel_id=1, source_target_pairs={{0,2},{1,3},{2,0},{3,1},{4,6},{5,7},{6,4},{7,5},{8,10},{9,11},{10,... | collective-permute-start | bytes 884744 | tf_op jit(solution)/shard_map/ppermute | solution.py:296
  36.2 8.3 %collective-permute-start.6 = (f32[144,128]{1,0:T(8,128)S(1)}, f32[144,128]{1,0:T(8,128)S(1)}, u32[]{:S(2)}, u32[]{:S(2)}) collective-permute-start(f32[144,128]{1,0:T(8,128)S(1)} %get-tuple-element.17), channel_id=1, source_target_pairs={{0,24},{8,16},{16,8},{24,0},{1,25},{9,17},{17,9},{25,1},{2,26},{10... | collective-permute-start | bytes 221192 | tf_op jit(solution)/shard_map/ppermute | solution.py:296
  41.3 6.0 %collective-permute-start.5 = (f32[144,128]{1,0:T(8,128)S(1)}, f32[144,128]{1,0:T(8,128)S(1)}, u32[]{:S(2)}, u32[]{:S(2)}) collective-permute-start(f32[144,128]{1,0:T(8,128)S(1)} %get-tuple-element.18), channel_id=1, source_target_pairs={{0,16},{8,24},{16,0},{24,8},{1,17},{9,25},{17,1},{25,9},{2,18},{10... | collective-permute-start | bytes 221192 | tf_op jit(solution)/shard_map/ppermute | solution.py:296
  41.3 6.0 %collective-permute-start.4 = (f32[144,128]{1,0:T(8,128)S(1)}, f32[144,128]{1,0:T(8,128)S(1)}, u32[]{:S(2)}, u32[]{:S(2)}) collective-permute-start(f32[144,128]{1,0:T(8,128)S(1)} %get-tuple-element.16), channel_id=1, source_target_pairs={{0,8},{8,0},{16,24},{24,16},{1,9},{9,1},{17,25},{25,17},{2,10},{10... | collective-permute-start | bytes 221192 | tf_op jit(solution)/shard_map/ppermute | solution.py:296
  47.4 4.7 %collective-permute-start.7 = (f32[144,128]{1,0:T(8,128)S(1)}, f32[144,128]{1,0:T(8,128)S(1)}, u32[]{:S(2)}, u32[]{:S(2)}) collective-permute-start(f32[144,128]{1,0:T(8,128)S(1)} %get-tuple-element.11), channel_id=1, source_target_pairs={{0,8},{8,0},{16,24},{24,16},{1,9},{9,1},{17,25},{25,17},{2,10},{10... | collective-permute-start | bytes 221192 | tf_op jit(solution)/shard_map/ppermute | solution.py:296
  48.4 7.0 %collective-permute-start.8 = (f32[144,128]{1,0:T(8,128)S(1)}, f32[144,128]{1,0:T(8,128)S(1)}, u32[]{:S(2)}, u32[]{:S(2)}) collective-permute-start(f32[144,128]{1,0:T(8,128)S(1)} %get-tuple-element.11), channel_id=1, source_target_pairs={{0,16},{8,24},{16,0},{24,8},{1,17},{9,25},{17,1},{25,9},{2,18},{10... | collective-permute-start | bytes 221192 | tf_op jit(solution)/shard_map/ppermute | solution.py:296
  50.2 6.3 %collective-permute-start.9 = (f32[144,128]{1,0:T(8,128)S(1)}, f32[144,128]{1,0:T(8,128)S(1)}, u32[]{:S(2)}, u32[]{:S(2)}) collective-permute-start(f32[144,128]{1,0:T(8,128)S(1)} %get-tuple-element.11), channel_id=1, source_target_pairs={{0,24},{8,16},{16,8},{24,0},{1,25},{9,17},{17,9},{25,1},{2,26},{10... | collective-permute-start | bytes 221192 | tf_op jit(solution)/shard_map/ppermute | solution.py:296
  56.4 10.0 %collective-permute-start.10 = (f32[576,128]{1,0:T(8,128)S(1)}, f32[576,128]{1,0:T(8,128)S(1)}, u32[]{:S(2)}, u32[]{:S(2)}) collective-permute-start(f32[576,128]{1,0:T(8,128)S(1)} %pad_maximum_fusion), channel_id=1, source_target_pairs={{0,2},{1,3},{2,0},{3,1},{4,6},{5,7},{6,4},{7,5},{8,10},{9,11},{10,... | collective-permute-start | bytes 884744 | tf_op jit(solution)/shard_map/ppermute | solution.py:296
  58.1 11.3 %collective-permute-start.11 = (f32[576,128]{1,0:T(8,128)S(1)}, f32[576,128]{1,0:T(8,128)S(1)}, u32[]{:S(2)}, u32[]{:S(2)}) collective-permute-start(f32[576,128]{1,0:T(8,128)S(1)} %pad_maximum_fusion), channel_id=1, source_target_pairs={{0,4},{1,5},{2,6},{3,7},{4,0},{5,1},{6,2},{7,3},{8,12},{9,13},{10,... | collective-permute-start | bytes 884744 | tf_op jit(solution)/shard_map/ppermute | solution.py:296
  58.6 12.6 %collective-permute-start.12 = (f32[576,128]{1,0:T(8,128)S(1)}, f32[576,128]{1,0:T(8,128)S(1)}, u32[]{:S(2)}, u32[]{:S(2)}) collective-permute-start(f32[576,128]{1,0:T(8,128)S(1)} %pad_maximum_fusion), channel_id=1, source_target_pairs={{0,6},{1,7},{2,4},{3,5},{4,2},{5,3},{6,0},{7,1},{8,14},{9,15},{10,... | collective-permute-start | bytes 884744 | tf_op jit(solution)/shard_map/ppermute | solution.py:296
  71.2 2.9 %copy-start = (f32[2304,128]{1,0:T(8,128)}, f32[2304,128]{1,0:T(8,128)S(1)}, u32[]{:S(2)}) copy-start(f32[2304,128]{1,0:T(8,128)S(1)} %constant_dynamic-update-slice_fusion.own_ref) | copy-start | bytes 3538948
  71.2 2.9 %collective-permute-start.13 = (f32[2304,128]{1,0:T(8,128)S(1)}, f32[2304,128]{1,0:T(8,128)S(1)}, u32[]{:S(2)}, u32[]{:S(2)}) collective-permute-start(f32[2304,128]{1,0:T(8,128)S(1)} %constant_dynamic-update-slice_fusion.own_ref), channel_id=1, source_target_pairs={{0,1},{1,0},{2,3},{3,2},{4,5},{5,4},{6,7},{7,6},{8,9},{9,8},{10,11... | collective-permute-start | bytes 3538952 | tf_op jit(solution)/shard_map/ppermute | solution.py:296
  74.1 1.0 copy-start.1

commit v3 on v2

--- a/solution.py
+++ b/solution.py
@@ -32,11 +32,22 @@
     return lax.dot_general(a, b, (((0,), (0,)), ((), ())), preferred_element_type=F32)
 
 
-def gram_kernel(step_rows, half, at_ref, rows_ref, vals_ref, prior_ref, pinfo_ref, keep_ref, send_ref, acc, info):
+def chunks_of(width, devices):
+    nb = width // NB
+    unit = 8 * devices
+    first = max(1, nb // 4)
+    end = block_at(width)[first, first] if first < nb else nb * (nb + 1) // 2
+    end += end % 2 if first < nb else 0
+    cuts = [(0, end, 0, first), (end, nb * (nb + 1) // 2, first, nb)] if first < nb else [(0, end, 0, nb)]
+    return [(lo, hi, i, j, -(-(hi - lo) * NB // unit) * unit) for lo, hi, i, j in cuts]
+
+
+def gram_kernel(step_rows, chunks, count_ref, rows_ref, vals_ref, prior_ref, pinfo_ref, *refs):
+    outs, (acc, info) = refs[:-2], refs[-2:]
     t = pl.program_id(0)
     width = rows_ref.shape[1]
     tile = min(256, width)
-    live = at_ref[0] - t * step_rows
+    live = count_ref[0] - t * step_rows
 
     @pl.when(t == 0)
     def _():
@@ -65,36 +76,40 @@
     @pl.when(t == pl.num_programs(0) - 1)
     def _():
         nb = width // NB
-        total = nb * (nb + 1) // 2 * NB
-
-        def pack(halves):
-            for (i, j), at in block_at(width).items():
-                out, off = halves[at * NB // half], at * NB % half
-                out[off : off + NB, :] = acc[i * NB : (i + 1) * NB, j * NB : (j + 1) * NB]
-            out, off = halves[(total - NB) // half], (total - NB) % half + NB // 2
+        side = lax.axis_index("blk") % 2
+
+        def pack(side):
+            for c, (b0, b1, _, _, rows) in enumerate(chunks):
+                half = rows // 2
+                pair = (outs[2 * c + side], outs[2 * c + 1 - side])
+                for (i, j), at in block_at(width).items():
+                    if b0 <= at < b1:
+                        out, off = pair[(at - b0) * NB // half], (at - b0) * NB % half
+                        out[off : off + NB, :] = acc[i * NB : (i + 1) * NB, j * NB : (j + 1) * NB]
+                for row in range((b1 - b0) * NB, rows, NB):
+                    pair[row // half][row % half : row % half + NB, :] = jnp.zeros((NB, NB), F32)
             hw = NB // 2
+            out = outs[side]
             for b in range(2 * nb):
-                out[off + b : off + b + 1, 0:hw] = info[0:1, b * hw : (b + 1) * hw]
-            for at in range(total, 2 * half, NB):
-                halves[at // half][at % half : at % half + NB, :] = jnp.zeros((NB, NB), F32)
-
-        @pl.when(at_ref[1] == 0)
+                out[hw + b : hw + b + 1, 0:hw] = info[0:1, b * hw : (b + 1) * hw]
+
+        @pl.when(side == 0)
         def _():
-            pack((keep_ref, send_ref))
-
-        @pl.when(at_ref[1] != 0)
+            pack(0)
+
+        @pl.when(side != 0)
         def _():
-            pack((send_ref, keep_ref))
-
-
-def gram(readings, values, counts, prior_root, prior_info, side, half):
+            pack(1)
+
+
+def gram(readings, values, counts, prior_root, prior_info, chunks):
     cap, width = readings.shape
     step_rows = min(512, cap)
     steps = cap // step_rows
-    scalars = jnp.stack([counts[0], side]).astype(jnp.int32)
     whole = pl.BlockSpec(memory_space=pltpu.VMEM)
+    shapes = [jax.ShapeDtypeStruct((c[4] // 2, NB), F32) for c in chunks for _ in range(2)]
     return pl.pallas_call(
-        functools.partial(gram_kernel, step_rows, half),
+        functools.partial(gram_kernel, step_rows, chunks),
         grid=(steps,),
         in_specs=[
             pl.BlockSpec(memory_space=pltpu.SMEM),
@@ -103,12 +118,12 @@
             whole,
             whole,
         ],
-        out_specs=[whole, whole],
-        out_shape=[jax.ShapeDtypeStruct((half, NB), F32)] * 2,
+        out_specs=[whole] * len(shapes),
+        out_shape=shapes,
         scratch_shapes=[pltpu.VMEM((width, width), F32), pltpu.VMEM((8, width), F32)],
         compiler_params=VMEM,
         name="gram",
-    )(scalars, readings, values.astype(F32).reshape(steps, step_rows), prior_root, prior_info.reshape(1, -1))
+    )(counts, readings, values.astype(F32).reshape(steps, step_rows), prior_root, prior_info.reshape(1, -1))
 
 
 def lane_of(v, at):
@@ -178,12 +193,20 @@
                 a[i] = jnp.where(inside, 0.0, a[i]) - off[8 * i : 8 * i + 8, :]
 
 
-def factor_kernel(pieces, at_ref, own_ref, far_ref, root_ref, info_ref, g, s, minv, r, uhi, ulo, y):
-    nb = r.shape[0] // NB
-    width = r.shape[1]
+def factor_kernel(chunk, n_quarter, n_layer, width, *refs):
+    b0, b1, first, last, sent = chunk
+    nb = width // NB
     place = block_at(width)
-    side, quarter, layer = at_ref[0], at_ref[1], at_ref[2]
-    n_quarter, n_layer, piece = pieces
+    own_ref, far_ref, refs = refs[0], refs[1], refs[2:]
+    if first:
+        (hi_in, lo_in, y_in, block_in, root_in), refs = refs[:5], refs[5:]
+    root_ref, y_ref, refs = refs[0], refs[1], refs[2:]
+    if last < nb:
+        (hi_out, lo_out, block_out), refs = refs[:3], refs[3:]
+    g, s, minv, r, uhi, ulo, y = refs
+    blk, layer = lax.axis_index("blk"), lax.axis_index("fibre")
+    side, quarter = blk % 2, blk // 2
+    piece = sent // (2 * n_quarter * n_layer)
     for ms in range(n_quarter):
         for mz in range(n_layer):
             for mc, ref in enumerate((own_ref, far_ref)):
@@ -191,52 +214,70 @@
                 at = (ms * n_layer + mz) * piece
                 g[pl.ds(pl.multiple_of(to, 8), piece), :] = ref[at : at + piece, :]
 
-    last = place[nb - 1, nb - 1] * NB
-    hw = NB // 2
-    block = g[last : last + NB, :]
-    mirror = block.T
-    for b in range(nb):
-        y[8 * b : 8 * b + 8, :] = jnp.broadcast_to(
-            jnp.concatenate([block[hw + 2 * b : hw + 2 * b + 1, 0:hw], block[hw + 2 * b + 1 : hw + 2 * b + 2, 0:hw]], axis=1),
-            (8, NB),
-        )
-    lane = lax.broadcasted_iota(jnp.int32, (hw, NB), 1)
-    g[last + hw : last + NB, :] = jnp.where(lane < hw, mirror[hw:, :], block[hw:, :])
-
-    s[:, 0:NB] = g[0:NB, :]
+    def block(i, j):
+        k = (place[i, j] - b0) * NB
+        return g[k : k + NB, :] if k >= 0 else block_in[...]
+
+    if first == 0:
+        hw = NB // 2
+        corner = g[0:NB, :]
+        mirror = corner.T
+        for b in range(nb):
+            y[8 * b : 8 * b + 8, :] = jnp.broadcast_to(
+                jnp.concatenate([corner[hw + 2 * b + e : hw + 2 * b + e + 1, 0:hw] for e in range(2)], axis=1), (8, NB)
+            )
+        lane = lax.broadcasted_iota(jnp.int32, (hw, NB), 1)
+        g[hw:NB, :] = jnp.where(lane < hw, mirror[hw:, :], corner[hw:, :])
+    else:
+        y[...] = y_in[...]
+        uhi[0 : first * NB, :] = hi_in[...]
+        ulo[0 : first * NB, :] = lo_in[...]
+
+    def next_row(at):
+        lo, hi = at * NB, at * NB + NB
+        if at:
+            fh, fl = uhi[0:lo, lo:hi], ulo[0:lo, lo:hi]
+        for b in range(at, nb):
+            t = block(at, b)
+            if at:
+                c = slice(b * NB, b * NB + NB)
+                t = t - (dot_t(fh, uhi[0:lo, c]) + dot_t(fh, ulo[0:lo, c]) + dot_t(fl, uhi[0:lo, c]))
+            s[:, (b - at) * NB : (b - at) * NB + NB] = t
+
+    next_row(first)
+
+    def read(u):
+        return s[8 * u : 8 * u + 8, 0:NB]
+
+    def write(u, upper, lower):
+        s[8 * u : 8 * u + 8, 0:NB] = upper
+        minv[8 * u : 8 * u + 8, :] = lower
 
     def step(i, carry):
-        def read(u):
-            return s[8 * u : 8 * u + 8, 0:NB]
-
-        def write(u, upper, lower):
-            s[8 * u : 8 * u + 8, 0:NB] = upper
-            minv[8 * u : 8 * u + 8, :] = lower
-
         factor_block(read, write)
-        for at in range(nb):
+        for at in range(first, last):
             @pl.when(i == at)
             def _():
                 lo, hi = at * NB, at * NB + NB
+                here = slice(lo - first * NB, hi - first * NB)
                 if at:
-                    r[lo:hi, 0:lo] = jnp.zeros((NB, lo), F32)
-                r[lo:hi, lo:hi] = s[:, 0:NB]
+                    r[here, 0:lo] = jnp.zeros((NB, lo), F32)
+                r[here, lo:hi] = s[:, 0:NB]
                 m = minv[...]
-                b = y[8 * at : 8 * at + 8, :]
                 yi = lax.dot_general(
-                    b, m, (((1,), (1,)), ((), ())), precision=lax.Precision.HIGHEST, preferred_element_type=F32
+                    y[8 * at : 8 * at + 8, :], m, (((1,), (1,)), ((), ())),
+                    precision=lax.Precision.HIGHEST, preferred_element_type=F32,
                 )
                 y[8 * at : 8 * at + 8, :] = yi
                 if at + 1 < nb:
                     mh, ml = split(m)
-                    rest = g_row(at, hi)
-                    sh, sl = split(rest)
+                    sh, sl = split(s[:, NB : (nb - at) * NB])
                     u = jnp.dot(
                         jnp.concatenate([mh, mh, ml], axis=1),
                         jnp.concatenate([sh, sl, sh], axis=0),
                         preferred_element_type=F32,
                     )
-                    r[lo:hi, hi:] = u
+                    r[here, hi:] = u
                     uh, ul = split(u)
                     uhi[lo:hi, hi:] = uh
                     ulo[lo:hi, hi:] = ul
@@ -245,50 +286,66 @@
                             yi, u[:, b * NB - hi : b * NB - hi + NB],
                             precision=lax.Precision.HIGHEST, preferred_element_type=F32,
                         )
-                    end = hi + NB
-                    fh, fl = uhi[0:hi, hi:end], ulo[0:hi, hi:end]
-                    for b in range(at + 1, nb):
-                        c = slice(b * NB, b * NB + NB)
-                        k = place[at + 1, b] * NB
-                        t = g[k : k + NB, :] - (
-                            dot_t(fh, uhi[0:hi, c]) + dot_t(fh, ulo[0:hi, c]) + dot_t(fl, uhi[0:hi, c])
-                        )
-                        if b == at + 1:
-                            s[:, 0:NB] = t
-                        else:
-                            g[k : k + NB, :] = t
+                    if at + 1 < last:
+                        next_row(at + 1)
         return carry
 
-    def g_row(i, start):
-        return jnp.concatenate([g[place[i, j] * NB : place[i, j] * NB + NB, :] for j in range(start // NB, nb)], axis=1)
-
-    lax.fori_loop(0, nb, step, 0)
+    lax.fori_loop(first, last, step, 0)
     rows = root_ref.shape[0]
-    root_ref[...] = r[pl.ds(pl.multiple_of(at_ref[3] * rows, 8), rows), :]
-    for b in range(nb):
-        info_ref[b : b + 1, :] = y[8 * b : 8 * b + 1, :]
-
-
-def factor(own, far, scalars, pieces, width, rows):
+    start = blk * rows - first * NB
+    if first:
+        root_ref[...] = root_in[...]
+
+    @pl.when((start >= 0) & (start < (last - first) * NB))
+    def _():
+        root_ref[...] = r[pl.ds(pl.multiple_of(start, 8), rows), :]
+
+    if last < nb:
+        y_ref[...] = y[...]
+        hi_out[...] = uhi[first * NB : last * NB, :]
+        lo_out[...] = ulo[first * NB : last * NB, :]
+        block_out[...] = g[(place[last, last] - b0) * NB : (place[last, last] - b0 + 1) * NB, :] if b1 > place[last, last] else jnp.zeros((NB, NB), F32)
+    else:
+        for b in range(nb):
+            y_ref[b : b + 1, :] = y[8 * b : 8 * b + 1, :]
+
+
+def factor(own, far, state, chunk, n_quarter, n_layer, width, rows):
     whole = pl.BlockSpec(memory_space=pltpu.VMEM)
     nb = width // NB
+    b0, b1, first, last, sent = chunk
+    shapes = [jax.ShapeDtypeStruct((rows, width), F32)]
+    if last < nb:
+        shapes += [
+            jax.ShapeDtypeStruct((8 * nb, NB), F32),
+            jax.ShapeDtypeStruct((last * NB, width), BF16),
+            jax.ShapeDtypeStruct((last * NB, width), BF16),
+            jax.ShapeDtypeStruct((NB, NB), F32),
+        ]
+    else:
+        shapes += [jax.ShapeDtypeStruct((nb, NB), F32)]
+    args = [own, far]
+    if first:
+        root, y, hi, lo, block = state
+        args += [hi, lo, y, block, root]
     return pl.pallas_call(
-        functools.partial(factor_kernel, pieces),
-        in_specs=[pl.BlockSpec(memory_space=pltpu.SMEM), whole, whole],
-        out_specs=[whole, whole],
-        out_shape=[jax.ShapeDtypeStruct((rows, width), F32), jax.ShapeDtypeStruct((nb, NB), F32)],
+        functools.partial(factor_kernel, chunk, n_quarter, n_layer, width),
+        in_specs=[whole] * len(args),
+        out_specs=[whole] * len(shapes),
+        out_shape=shapes,
         scratch_shapes=[
-            pltpu.VMEM((2 * own.shape[0], NB), F32),
+            pltpu.VMEM((sent, NB), F32),
+            pltpu.VMEM((NB, width), F32),
             pltpu.VMEM((NB, NB), F32),
-            pltpu.VMEM((NB, NB), F32),
-            pltpu.VMEM((width, width), F32),
+            pltpu.VMEM(((last - first) * NB, width), F32),
             pltpu.VMEM((width, width), BF16),
             pltpu.VMEM((width, width), BF16),
             pltpu.VMEM((8 * nb, NB), F32),
         ],
         compiler_params=VMEM,
-        name="factor",
-    )(scalars, own, far)
+        cost_estimate=pl.CostEstimate(flops=(last - first) * 4_000_000_000, bytes_accessed=4 * sent * NB, transcendentals=0),
+        name="factor_rows_%d" % first,
+    )(*args)
 
 
 def swap(x, axis, mask):
@@ -316,25 +373,23 @@
     width = readings.shape[1]
     n_blk, n_fibre = lax.axis_size("blk"), lax.axis_size("fibre")
     blk, fibre = lax.axis_index("blk"), lax.axis_index("fibre")
-    nb = width // NB
-    unit = 8 * n_blk * n_fibre
-    total = -(-(nb * (nb + 1) // 2 * NB) // unit) * unit
-    half = total // 2
-    side, quarter, layer = blk % 2, blk // 2, fibre
+    quarter, layer = blk // 2, fibre
     quarters = [2 * m for m in range(1, n_blk // 2)]
     layers = list(range(1, n_fibre))
-
-    keep, send = gram(readings, values, counts, prior_root, prior_info, side, half)
-    parts = [keep, swap(send, "blk", 1)]
-    parts = exchange_sum(parts, "blk", quarters, quarter)
-    parts = exchange_sum(parts, "fibre", layers, layer)
-    piece = functools.reduce(lambda a, b: a + b, parts)
-    own = gather(gather(piece, "fibre", layers), "blk", quarters)
-    far = swap(own, "blk", 1)
-    scalars = jnp.stack([side, quarter, layer, blk]).astype(jnp.int32)
-    rows = width // n_blk
-    root, info = factor(own, far, scalars, (n_blk // 2, n_fibre, piece.shape[0]), width, rows)
-    return root, info.reshape(width)
+    chunks = chunks_of(width, n_blk * n_fibre)
+
+    terms = gram(readings, values, counts, prior_root, prior_info, chunks)
+    state = None
+    for c, chunk in enumerate(chunks):
+        keep, send = terms[2 * c : 2 * c + 2]
+        parts = [keep, swap(send, "blk", 1)]
+        parts = exchange_sum(parts, "blk", quarters, quarter)
+        parts = exchange_sum(parts, "fibre", layers, layer)
+        piece = functools.reduce(lambda a, b: a + b, parts)
+        own = gather(gather(piece, "fibre", layers), "blk", quarters)
+        far = swap(own, "blk", 1)
+        state = factor(own, far, state, chunk, n_blk // 2, n_fibre, width, width // n_blk)
+    return state[0], state[1].reshape(width)
 
 
 def solution(mesh):

time: 107 us -> 115 us (1.075)
  starting transfers between devices: 18.9 us -> 35.9 us
  waiting for transfers between devices: 39.2 us -> 27.2 us
  Pallas kernels: 42.5 us -> 44.3 us
    ppermute x14 -> x28, starting transfers between devices: 18.9 us -> 35.9 us  [swap(): return lax.ppermute(x, axis, [(d, d ^ mask) for d in range(n)])]
    ppermute x14 -> x28, waiting for transfers between devices: 39.2 us -> 27.2 us  [swap(): return lax.ppermute(x, axis, [(d, d ^ mask) for d in range(n)])]
    pallas_call x2 -> x3, Pallas kernels: 42.5 us -> 44.3 us  [the longest x2 35 us: factor(): pl.pallas_call(functools.partial(factor_kernel, chunk, n_quarter, n_layer...]
    another operation x2 -> x0, other arithmetic: 1.44 us -> none  [the longest x1 0.79 us: local(): scalars = jnp.stack([side, quarter, layer, blk]).astype(jnp.int32)]
    add x2 -> x4, other arithmetic: 1.41 us -> 2.43 us  [share(): return functools.reduce(lambda a, b: a + b, terms)]
  transfers between devices with their start and end apart: 14 -> 28, of which waited for: 13 -> 15; matrix products, arithmetic and copies ran while one was open for 1% -> 2% of each run, Pallas kernels for 0% -> 9%
where the time goes in v3:
time: 115 us
  Pallas kernels  44.3 us (39%)
  starting transfers between devices  35.9 us (31%)
  waiting for transfers between devices  27.2 us (24%)
  local copies, waits for them, and re-layouts  3.2 us (3%)
  other arithmetic  2.49 us (2%)
  between operations  1.46 us (1%)
    ppermute x28, starting transfers between devices, swap(): return lax.ppermute(x, axis, [(d, d ^ mask) for d in range(n)])  35.9 us
    pallas_call x2, Pallas kernels, factor(): pl.pallas_call(functools.partial(factor_kernel, chunk, n_quarter, n_layer...  35 us
    ppermute x28, waiting for transfers between devices, swap(): return lax.ppermute(x, axis, [(d, d ^ mask) for d in range(n)])  27.2 us
    pallas_call x1, Pallas kernels, gram(): pl.pallas_call(functools.partial(gram_kernel, step_rows, chunks), grid=(s...  9.32 us
    add x4, other arithmetic, share(): return functools.reduce(lambda a, b: a + b, terms)  2.43 us
  transfers between devices with their start and end apart: 28, of which 15 were waited for; matrix products, arithmetic and copies ran while one was open for 2% of the time, Pallas kernels for 9%

profile of v3, /device:TPU:0, one launch (start us, length us, event | category | flops | bytes accessed | tf_op | source)
XLA Modules:
  0.0 114.5 jit_solution(9137332634286409634)
XLA Ops:
  1.3 1.3 %reshape.20.vals_ref = f32[8,512]{1,0:T(8,128)} reshape(bf16[4096]{0:T(1024)(128)(2,1)} %param.6) | data formatting | bytes 24576 | tf_op jit(solution)/shard_map/reshape | solution.py:126
  2.6 9.3 %gram.1 = (f32[1024,128]{1,0:T(8,128)}, f32[1024,128]{1,0:T(8,128)}, f32[1280,128]{1,0:T(8,128)}, f32[1280,128]{1,0:T(8,128)}) custom-call(s32[1]{0:T(128)S(6)} %copy.19.count_ref, bf16[4096,1024]{1,0:T(8,128)(2,1)} %rows_ref.1, f32[8,512]{1,0:T(8,128)} %reshape.20.vals_ref, f32[32,1024]{1,0:T(8,128)} %prior_ref.1, f32[1,32]{1,0:T(1,128)} %bitcast.2), custom_call_target="tpu_custom_call" | custom-call | tf_op jit(solution)/shard_map/gram/pallas_call | solution.py:111
  11.9 1.4 %collective-permute-start.14 = (f32[1024,128]{1,0:T(8,128)}, f32[1024,128]{1,0:T(8,128)S(1)}, u32[]{:S(2)}, u32[]{:S(2)}) collective-permute-start(f32[1024,128]{1,0:T(8,128)} %get-tuple-element.16), channel_id=1, source_target_pairs={{0,1},{1,0},{2,3},{3,2},{4,5},{5,4},{6,7},{7,6},{8,9},{9,8},{10,11... | collective-permute-start | bytes 1572872 | tf_op jit(solution)/shard_map/ppermute | solution.py:353
  13.3 0.0 collective-permute-start
  13.3 1.7 %collective-permute-done.14 = f32[1024,128]{1,0:T(8,128)S(1)} collective-permute-done((f32[1024,128]{1,0:T(8,128)}, f32[1024,128]{1,0:T(8,128)S(1)}, u32[]{:S(2)}, u32[]{:S(2)}) %collective-permute-start.14) | collective-permute-done | bytes 524320 | tf_op jit(solution)/shard_map/ppermute | solution.py:353
  15.1 1.1 %dynamic-slice_add_fusion.7 = (f32[256,128]{1,0:T(8,128)S(1)}, f32[256,128]{1,0:T(8,128)S(1)}, f32[256,128]{1,0:T(8,128)S(1)}, f32[256,128]{1,0:T(8,128)S(1)}) fusion(f32[1024,128]{1,0:T(8,128)S(1)} %collective-permute-done.14, s32[]{:T(128)S(6)} %select_n.46, f32[1024,128]{1,0:T(8,128)} %get-tuple-element.15, s32[]{:T(128)S(6)} %select_n.98, ...), kind=kLoop, calls=%fused_computation.9 | loop fusion | flops 131072 | bytes 1572880 | tf_op jit(solution)/shard_map/add | solution.py:362
  16.2 4.8 %collective-permute-start.17 = (f32[256,128]{1,0:T(8,128)S(1)}, f32[256,128]{1,0:T(8,128)S(1)}, u32[]{:S(2)}, u32[]{:S(2)}) collective-permute-start(f32[256,128]{1,0:T(8,128)S(1)} %get-tuple-element.33), channel_id=1, source_target_pairs={{0,6},{1,7},{2,4},{3,5},{4,2},{5,3},{6,0},{7,1},{8,14},{9,15},{10,... | collective-permute-start | bytes 393224 | tf_op jit(solution)/shard_map/ppermute | solution.py:353
  21.1 0.0 collective-permute-start.16
  21.1 0.6 collective-permute-start.15
  21.7 3.3 %collective-permute-done.17 = f32[256,128]{1,0:T(8,128)S(1)} collective-permute-done((f32[256,128]{1,0:T(8,128)S(1)}, f32[256,128]{1,0:T(8,128)S(1)}, u32[]{:S(2)}, u32[]{:S(2)}) %collective-permute-start.17) | collective-permute-done | bytes 131104 | tf_op jit(solution)/shard_map/ppermute | solution.py:353
  25.0 2.7 %collective-permute-done.16 = f32[256,128]{1,0:T(8,128)S(1)} collective-permute-done((f32[256,128]{1,0:T(8,128)S(1)}, f32[256,128]{1,0:T(8,128)S(1)}, u32[]{:S(2)}, u32[]{:S(2)}) %collective-permute-start.16) | collective-permute-done | bytes 131104 | tf_op jit(solution)/shard_map/ppermute | solution.py:353
  27.7 0.3 collective-permute-done.15
  28.0 3.7 %collective-permute-start.20 = (f32[64,128]{1,0:T(8,128)S(1)}, f32[64,128]{1,0:T(8,128)S(1)}, u32[]{:S(2)}, u32[]{:S(2)}) collective-permute-start(f32[64,128]{1,0:T(8,128)S(1)} %get-tuple-element.40), channel_id=1, source_target_pairs={{0,24},{8,16},{16,8},{24,0},{1,25},{9,17},{17,9},{25,1},{2,26},{10... | collective-permute-start | bytes 98312 | tf_op jit(solution)/shard_map/ppermute | solution.py:353
  31.8 0.4 collective-permute-start.19
  32.1 0.3 collective-permute-start.18
  32.5 1.3 %collective-permute-done.20 = f32[64,128]{1,0:T(8,128)S(1)} collective-permute-done((f32[64,128]{1,0:T(8,128)S(1)}, f32[64,128]{1,0:T(8,128)S(1)}, u32[]{:S(2)}, u32[]{:S(2)}) %collective-permute-start.20) | collective-permute-done | bytes 32800 | tf_op jit(solution)/shard_map/ppermute | solution.py:353
  33.8 2.8 %collective-permute-done.19 = f32[64,128]{1,0:T(8,128)S(1)} collective-permute-done((f32[64,128]{1,0:T(8,128)S(1)}, f32[64,128]{1,0:T(8,128)S(1)}, u32[]{:S(2)}, u32[]{:S(2)}) %collective-permute-start.19) | collective-permute-done | bytes 32800 | tf_op jit(solution)/shard_map/ppermute | solution.py:353
  36.6 0.0 collective-permute-done.18
  36.6 0.2 collective-permute-start.21
  36.8 1.9 %collective-permute-start.22 = (f32[64,128]{1,0:T(8,128)S(1)}, f32[64,128]{1,0:T(8,128)S(1)}, u32[]{:S(2)}, u32[]{:S(2)}) collective-permute-start(f32[64,128]{1,0:T(8,128)S(1)} %get-tuple-element.25), channel_id=1, source_target_pairs={{0,16},{8,24},{16,0},{24,8},{1,17},{9,25},{17,1},{25,9},{2,18},{10... | collective-permute-start | bytes 98312 | tf_op jit(solution)/shard_map/ppermute | solution.py:353
  38.8 2.3 %collective-permute-start.23 = (f32[64,128]{1,0:T(8,128)S(1)}, f32[64,128]{1,0:T(8,128)S(1)}, u32[]{:S(2)}, u32[]{:S(2)}) collective-permute-start(f32[64,128]{1,0:T(8,128)S(1)} %get-tuple-element.25), channel_id=1, source_target_pairs={{0,24},{8,16},{16,8},{24,0},{1,25},{9,17},{17,9},{25,1},{2,26},{10... | collective-permute-start | bytes 98312 | tf_op jit(solution)/shard_map/ppermute | solution.py:353
  41.1 0.0 collective-permute-done
  41.1 1.2 %dynamic-slice_add_fusion.3 = (f32[320,128]{1,0:T(8,128)S(1)}, f32[320,128]{1,0:T(8,128)S(1)}, f32[320,128]{1,0:T(8,128)S(1)}, f32[320,128]{1,0:T(8,128)S(1)}) fusion(f32[1280,128]{1,0:T(8,128)S(1)} %collective-permute-done, s32[]{:T(128)S(6)} %select_n.38, f32[1280,128]{1,0:T(8,128)} %get-tuple-element.13, s32[]{:T(128)S(6)} %select_n.42, s32[]{:T(128)S(6)} %select_n.41, ...), kind=kLoop, calls=%fused_computation.4 | loop fusion | flops 163840 | bytes 1966096 | tf_op jit(solution)/shard_map/add | solution.py:362
  42.3 1.7 %collective-permute-start.3 = (f32[320,128]{1,0:T(8,128)S(1)}, f32[320,128]{1,0:T(8,128)S(1)}, u32[]{:S(2)}, u32[]{:S(2)}) collective-permute-start(f32[320,128]{1,0:T(8,128)S(1)} %get-tuple-element.29), channel_id=1, source_target_pairs={{0,6},{1,7},{2,4},{3,5},{4,2},{5,3},{6,0},{7,1},{8,14},{9,15},{10,... | collective-permute-start | bytes 491528 | tf_op jit(solution)/shard_map/ppermute | solution.py:353
  44.0 1.3 %collective-permute-start.2 = (f32[320,128]{1,0:T(8,128)S(1)}, f32[320,128]{1,0:T(8,128)S(1)}, u32[]{:S(2)}, u32[]{:S(2)}) collective-permute-start(f32[320,128]{1,0:T(8,128)S(1)} %get-tuple-element.30), channel_id=1, source_target_pairs={{0,4},{1,5},{2,6},{3,7},{4,0},{5,1},{6,2},{7,3},{8,12},{9,13},{10,... | collective-permute-start | bytes 491528 | tf_op jit(solution)/shard_map/ppermute | solution.py:353
  45.3 0.0 collective-permute-done.21
  45.3 0.6 collective-permute-start.1
  45.8 0.0 collective-permute-done.22
  45.8 0.0 collective-permute-done.23
  45.9 1.5 %collective-permute-start.24 = (f32[256,128]{1,0:T(8,128)S(1)}, f32[256,128]{1,0:T(8,128)S(1)}, u32[]{:S(2)}, u32[]{:S(2)}) collective-permute-start(f32[256,128]{1,0:T(8,128)S(1)} %pad_maximum_fusion.1), channel_id=1, source_target_pairs={{0,2},{1,3},{2,0},{3,1},{4,6},{5,7},{6,4},{7,5},{8,10},{9,11},{10,... | collective-permute-start | bytes 393224 | tf_op jit(solution)/shard_map/ppermute | solution.py:353
  47.4 0.7 collective-permute-start.25
  48.2 2.3 %collective-permute-done.3 = f32[320,128]{1,0:T(8,128)S(1)} collective-permute-done((f32[320,128]{1,0:T(8,128)S(1)}, f32[320,128]{1,0:T(8,128)S(1)}, u32[]{:S(2)}, u32[]{:S(2)}) %collective-permute-start.3) | collective-permute-done | bytes 163872 | tf_op jit(solution)/shard_map/ppermute | solution.py:353
  50.5 1.6 %collective-permute-start.26 = (f32[256,128]{1,0:T(8,128)S(1)}, f32[256,128]{1,0:T(8,128)S(1)}, u32[]{:S(2)}, u32[]{:S(2)}) collective-permute-start(f32[256,128]{1,0:T(8,128)S(1)} %pad_maximum_fusion.1), channel_id=1, source_target_pairs={{0,6},{1,7},{2,4},{3,5},{4,2},{5,3},{6,0},{7,1},{8,14},{9,15},{10,... | collective-permute-start | bytes 393224 | tf_op jit(solution)/shard_map/ppermute | solution.py:353
  52.1 0.9 collective-permute-done.2
  53.1 0.0 collective-permute-done.1
  53.1 2.0 %collective-permute-start.6 = (f32[80,128]{1,0:T(8,128)S(1)}, f32[80,128]{1,0:T(8,128)S(1)}, u32[]{:S(2)}, u32[]{:S(2)}) collective-permute-start(f32[80,128]{1,0:T(8,128)S(1)} %get-tuple-element.37), channel_id=1, source_target_pairs={{0,24},{8,16},{16,8},{24,0},{1,25},{9,17},{17,9},{25,1},{2,26},{10... | collective-permute-start | bytes 122888 | tf_op jit(solution)/shard_map/ppermute | solution.py:353
  55.1 0.0 collective-permute-start.5
  55.1 0.0 collective-permute-done.24
  55.1 2.5 %collective-permute-start.4 = (f32[80,128]{1,0:T(8,128)S(1)}, f32[80,128]{1,0:T(8,128)S(1)}, u32[]{:S(2)}, u32[]{:S(2)}) collective-permute-start(f32[80,128]{1,0:T(8,128)S(1)} %get-tuple-element.36), channel_id=1, source_target_pairs={{0,8},{8,0},{16,24},{24,16},{1,9},{9,1},{17,25},{25,17},{2,10},{10... | collective-permute-start | bytes 122888 | tf_op jit(solution)/shard_map/ppermute | solution.py:353
  57.6 0.0 collective-permute-done.25
  57.6 1.5 %collective-permute-done.6 = f32[80,128]{1,0:T(8,128)S(1)} collective-permute-done((f32[80,128]{1,0:T(8,128)S(1)}, f32[80,128]{1,0:T(8,128)S(1)}, u32[]{:S(2)}, u32[]{:S(2)}) %collective-permute-start.6) | collective-permute-done | bytes 40992 | tf_op jit(solution)/shard_map/ppermute | solution.py:353
  59.1 1.3 %collective-permute-done.5 = f32[80,128]{1,0:T(8,128)S(1)} collective-permute-done((f32[80,128]{1,0:T(8,128)S(1)}, f32[80,128]{1,0:T(8,128)S(1)}, u32[]{:S(2)}, u32[]{:S(2)}) %collective-permute-start.5) | collective-permute-done | bytes 40992 | tf_op jit(solution)/shard_map/ppermute | solution.py:353
  60.4 0.0 collective-permute-done.4
  60.5 1.2 %collective-permute-start.7 = (f32[80,128]{1,0:T(8,128)S(1)}, f32[80,128]{1,0:T(8,128)S(1)}, u32[]{:S(2)}, u32[]{:S(2)}) collective-permute-start(f32[80,128]{1,0:T(8,128)S(1)} %get-tuple-element.27), channel_id=1, source_target_pairs={{0,8},{8,0},{16,24},{24,16},{1,9},{9,1},{17,25},{25,17},{2,10},{10... | collective-permute-start | bytes 122888 | tf_op jit(solution)/shard_map/ppermute | solution.py:353
  61.7 1.5 %collective-permute-start.8 = (f32[80,128]{1,0:T(8,128)S(1)}, f32[80,128]{1,0:T(8,128)S(1)}, u32[]{:S(2)}, u32[]{:S(2)}) collective-permute-start(f32[80,128]{1,0:T(8,128)S(1)} %get-tuple-element.27), channel_id=1, source_target_pairs={{0,16},{8,24},{16,0},{24,8},{1,17},{9,25},{17,1},{25,9},{2,18},{10... | collective-permute-start | bytes 122888 | tf_op jit(solution)/shard_map/ppermute | solution.py:353
  63.1 1.8 %collective-permute-start.9 = (f32[80,128]{1,0:T(8,128)S(1)}, f32[80,128]{1,0:T(8,128)S(1)}, u32[]{:S(2)}, u32[]{:S(2)}) collective-permute-start(f32[80,128]{1,0:T(8,128)S(1)} %get-tuple-element.27), channel_id=1, source_target_pairs={{0,24},{8,16},{16,8},{24,0},{1,25},{9,17},{17,9},{25,1},{2,26},{10... | collective-permute-start | bytes 122888 | tf_op jit(solution)/shard_map/ppermute | solution.py:353
  64.9 0.0 collective-permute-done.26
  64.9 0.0 copy-start.1
  64.9 0.1 collective-permute-start.27
  65.0 2.0 %collective-permute-done.8 = f32[80,128]{1,0:T(8,128)S(1)} collective-permute-done((f32[80,128]{1,0:T(8,128)S(1)}, f32[80,128]{1,0:T(8,128)S(1)}, u32[]{:S(2)}, u32[]{:S(2)}) %collective-permute-start.8) | collective-permute-done | bytes 40992 | tf_op jit(solution)/shard_map/ppermute | solution.py:353
  67.0 1.9 %collective-permute-done.9 = f32[80,128]{1,0:T(8,128)S(1)} collective-permute-done((f32[80,128]{1,0:T(8,128)S(1)}, f32[80,128]{1,0:T(8,128)S(1)}, u32[]{:S(2)}, u32[]{:S(2)}) %collective-permute-start.9) | collective-permute-done | bytes 40992 | tf_op jit(solution)/shard_map/ppermute | solution.py:353
  69.0 1.6 %collective-permute-start.10 = (f32[320,128]{1,0:T(8,128)S(1)}, f32[320,128]{1,0:T(8,128)S(1)}, u32[]{:S(2)}, u32[]{:S(2)}) collective-permute-start(f32[320,128]{1,0:T(8,128)S(1)} %pad_maximum_fusion), channel_id=1, source_target_pairs={{0,2},{1,3},{2,0},{3,1},{4,6},{5,7},{6,4},{7,5},{8,10},{9,11},{10,... | collective-permute-start | bytes 491528 | tf_op jit(solution)/shard_map/ppermute | solution.py:353
  70.5 0.9 collective-permute-start.11
  71.4 1.1 collective-permute-start.12
  72.5 1.8 %collective-permute-done.10 = f32[320,128]{1,0:T(8,128)S(1)} collective-permute-done((f32[320,128]{1,0:T(8,128)S(1)}, f32[320,128]{1,0:T(8,128)S(1)}, u32[]{:S(2)}, u32[]{:S(2)}) %collective-permute-start.10) | collective-permute-done | bytes 163872 | tf_op jit(solution)/shard_map/ppermute | solution.py:353
  74.4 1.5 %collective-permute-done.11 = f32[320,128]{1,0:T(8,128)S(1)} collective-permute-done((f32[320,128]{1,0:T(8,128)S(1)}, f32[320,128]{1,0:T(8,128)S(1)}, u32[]{:S(2)}, u32[]{:S(2)}) %collective-permute-start.11) | collective-permute-done | bytes 163872 | tf_op jit(solution)/shard_map/ppermute | solution.py:353
  75.9 1.8 %collective-permute-done.12 = f32[320,128]{1,0:T(8,128)S(1)} collective-permute-done((f32[320,128]{1,0:T(8,128)S(1)}, f32[320,128]{1,0:T(8,128)S(1)}, u32[]{:S(2)}, u32[]{:S(2)}) %collective-permute-start.12) | collective-permute-done | bytes 163872 | tf_op jit(solution)/shard_map/ppermute | solution.py:353
  77.7 0.1 collective-permute-start.13
  77.7 0.0 collective-permute-done.27.refs_1_
  77.8 0.9 copy-done.3
  78.7 10.0 %factor_rows_0.1 = (f32[128,1024]{1,0:T(8,128)}, f32[64,128]{1,0:T(8,128)}, bf16[256,1024]{1,0:T(8,128)(2,1)}, bf16[256,1024]{1,0:T(8,128)(2,1)}, f32[128,128]{1,0:T(8,128)}) custom-call(f32[1024,128]{1,0:T(8,128)} %copy-done.1, f32[1024,128]{1,0:T(8,128)} %copy-done.3), custom_call_target="tpu_custom_call" | custom-call | flops 8000000000 | bytes 1048576 | tf_op jit(solution)/shard_map/factor_rows_0/pallas_call | solution.py:331
  88.7 0.0 collective-permute-done.13.refs_1_
  88.7 0.9 copy-done.2
  89.6 24.9 %factor_rows_2.1 = (f32[128,1024]{1,0:T(8,128)}, f32[8,128]{1,0:T(8,128)}) custom-call(f32[1280,128]{1,0:T(8,128)} %copy-done, f32[1280,128]{1,0:T(8,128)} %copy-done.2, bf16[256,1024]{1,0:T(8,128)(2,1)} %get-tuple-element.17.refs_2_, bf16[256,1024]{1,0:T(8,128)(2,1)} %get-tuple-element.18.refs_3_, f32[64,128]{1,0:T(8,128)} %get-tuple-element.19.refs_4_, ...), custom_call_target="tpu_custom_call" | custom-call | flops 24000000000 | bytes 1310720 | tf_op jit(solution)/shard_map/factor_rows_2/pallas_call | solution.py:331
  (24 shorter events, 0.2 us)
Async XLA Ops:
  11.9 3.2 %collective-permute-start.14 = (f32[1024,128]{1,0:T(8,128)}, f32[1024,128]{1,0:T(8,128)S(1)}, u32[]{:S(2)}, u32[]{:S(2)}) collective-permute-start(f32[1024,128]{1,0:T(8,128)} %get-tuple-element.16), channel_id=1, source_target_pairs={{0,1},{1,0},{2,3},{3,2},{4,5},{5,4},{6,7},{7,6},{8,9},{9,8},{10,11... | collective-permute-start | bytes 1572872 | tf_op jit(solution)/shard_map/ppermute | solution.py:353
  13.3 27.7 %collective-permute-start = (f32[1280,128]{1,0:T(8,128)}, f32[1280,128]{1,0:T(8,128)S(1)}, u32[]{:S(2)}, u32[]{:S(2)}) collective-permute-start(f32[1280,128]{1,0:T(8,128)} %get-tuple-element.14), channel_id=1, source_target_pairs={{0,1},{1,0},{2,3},{3,2},{4,5},{5,4},{6,7},{7,6},{8,9},{9,8},{10,11... | collective-permute-start | bytes 1966088 | tf_op jit(solution)/shard_map/ppermute | solution.py:353
  16.2 8.7 %collective-permute-start.17 = (f32[256,128]{1,0:T(8,128)S(1)}, f32[256,128]{1,0:T(8,128)S(1)}, u32[]{:S(2)}, u32[]{:S(2)}) collective-permute-start(f32[256,128]{1,0:T(8,128)S(1)} %get-tuple-element.33), channel_id=1, source_target_pairs={{0,6},{1,7},{2,4},{3,5},{4,2},{5,3},{6,0},{7,1},{8,14},{9,15},{10,... | collective-permute-start | bytes 393224 | tf_op jit(solution)/shard_map/ppermute | solution.py:353
  21.1 6.6 %collective-permute-start.16 = (f32[256,128]{1,0:T(8,128)S(1)}, f32[256,128]{1,0:T(8,128)S(1)}, u32[]{:S(2)}, u32[]{:S(2)}) collective-permute-start(f32[256,128]{1,0:T(8,128)S(1)} %get-tuple-element.34), channel_id=1, source_target_pairs={{0,4},{1,5},{2,6},{3,7},{4,0},{5,1},{6,2},{7,3},{8,12},{9,13},{10,... | collective-permute-start | bytes 393224 | tf_op jit(solution)/shard_map/ppermute | solution.py:353
  21.1 6.9 %collective-permute-start.15 = (f32[256,128]{1,0:T(8,128)S(1)}, f32[256,128]{1,0:T(8,128)S(1)}, u32[]{:S(2)}, u32[]{:S(2)}) collective-permute-start(f32[256,128]{1,0:T(8,128)S(1)} %get-tuple-element.35), channel_id=1, source_target_pairs={{0,2},{1,3},{2,0},{3,1},{4,6},{5,7},{6,4},{7,5},{8,10},{9,11},{10,... | collective-permute-start | bytes 393224 | tf_op jit(solution)/shard_map/ppermute | solution.py:353
  28.0 5.8 %collective-permute-start.20 = (f32[64,128]{1,0:T(8,128)S(1)}, f32[64,128]{1,0:T(8,128)S(1)}, u32[]{:S(2)}, u32[]{:S(2)}) collective-permute-start(f32[64,128]{1,0:T(8,128)S(1)} %get-tuple-element.40), channel_id=1, source_target_pairs={{0,24},{8,16},{16,8},{24,0},{1,25},{9,17},{17,9},{25,1},{2,26},{10... | collective-permute-start | bytes 98312 | tf_op jit(solution)/shard_map/ppermute | solution.py:353
  31.8 4.8 %collective-permute-start.19 = (f32[64,128]{1,0:T(8,128)S(1)}, f32[64,128]{1,0:T(8,128)S(1)}, u32[]{:S(2)}, u32[]{:S(2)}) collective-permute-start(f32[64,128]{1,0:T(8,128)S(1)} %get-tuple-element.41), channel_id=1, source_target_pairs={{0,16},{8,24},{16,0},{24,8},{1,17},{9,25},{17,1},{25,9},{2,18},{10... | collective-permute-start | bytes 98312 | tf_op jit(solution)/shard_map/ppermute | solution.py:353
  32.1 4.5 %collective-permute-start.18 = (f32[64,128]{1,0:T(8,128)S(1)}, f32[64,128]{1,0:T(8,128)S(1)}, u32[]{:S(2)}, u32[]{:S(2)}) collective-permute-start(f32[64,128]{1,0:T(8,128)S(1)} %get-tuple-element.39), channel_id=1, source_target_pairs={{0,8},{8,0},{16,24},{24,16},{1,9},{9,1},{17,25},{25,17},{2,10},{10... | collective-permute-start | bytes 98312 | tf_op jit(solution)/shard_map/ppermute | solution.py:353
  36.6 8.7 %collective-permute-start.21 = (f32[64,128]{1,0:T(8,128)S(1)}, f32[64,128]{1,0:T(8,128)S(1)}, u32[]{:S(2)}, u32[]{:S(2)}) collective-permute-start(f32[64,128]{1,0:T(8,128)S(1)} %get-tuple-element.25), channel_id=1, source_target_pairs={{0,8},{8,0},{16,24},{24,16},{1,9},{9,1},{17,25},{25,17},{2,10},{10... | collective-permute-start | bytes 98312 | tf_op jit(solution)/shard_map/ppermute | solution.py:353
  36.8 9.0 %collective-permute-start.22 = (f32[64,128]{1,0:T(8,128)S(1)}, f32[64,128]{1,0:T(8,128)S(1)}, u32[]{:S(2)}, u32[]{:S(2)}) collective-permute-start(f32[64,128]{1,0:T(8,128)S(1)} %get-tuple-element.25), channel_id=1, source_target_pairs={{0,16},{8,24},{16,0},{24,8},{1,17},{9,25},{17,1},{25,9},{2,18},{10... | collective-permute-start | bytes 98312 | tf_op jit(solution)/shard_map/ppermute | solution.py:353
  38.8 7.1 %collective-permute-start.23 = (f32[64,128]{1,0:T(8,128)S(1)}, f32[64,128]{1,0:T(8,128)S(1)}, u32[]{:S(2)}, u32[]{:S(2)}) collective-permute-start(f32[64,128]{1,0:T(8,128)S(1)} %get-tuple-element.25), channel_id=1, source_target_pairs={{0,24},{8,16},{16,8},{24,0},{1,25},{9,17},{17,9},{25,1},{2,26},{10... | collective-permute-start | bytes 98312 | tf_op jit(solution)/shard_map/ppermute | solution.py:353
  42.3 8.2 %collective-permute-start.3 = (f32[320,128]{1,0:T(8,128)S(1)}, f32[320,128]{1,0:T(8,128)S(1)}, u32[]{:S(2)}, u32[]{:S(2)}) collective-permute-start(f32[320,128]{1,0:T(8,128)S(1)} %get-tuple-element.29), channel_id=1, source_target_pairs={{0,6},{1,7},{2,4},{3,5},{4,2},{5,3},{6,0},{7,1},{8,14},{9,15},{10,... | collective-permute-start | bytes 491528 | tf_op jit(solution)/shard_map/ppermute | solution.py:353
  44.0 9.1 %collective-permute-start.2 = (f32[320,128]{1,0:T(8,128)S(1)}, f32[320,128]{1,0:T(8,128)S(1)}, u32[]{:S(2)}, u32[]{:S(2)}) collective-permute-start(f32[320,128]{1,0:T(8,128)S(1)} %get-tuple-element.30), channel_id=1, source_target_pairs={{0,4},{1,5},{2,6},{3,7},{4,0},{5,1},{6,2},{7,3},{8,12},{9,13},{10,... | collective-permute-start | bytes 491528 | tf_op jit(solution)/shard_map/ppermute | solution.py:353
  45.3 7.8 %collective-permute-start.1 = (f32[320,128]{1,0:T(8,128)S(1)}, f32[320,128]{1,0:T(8,128)S(1)}, u32[]{:S(2)}, u32[]{:S(2)}) collective-permute-start(f32[320,128]{1,0:T(8,128)S(1)} %get-tuple-element.31), channel_id=1, source_target_pairs={{0,2},{1,3},{2,0},{3,1},{4,6},{5,7},{6,4},{7,5},{8,10},{9,11},{10,... | collective-permute-start | bytes 491528 | tf_op jit(solution)/shard_map/ppermute | solution.py:353
  45.9 9.2 %collective-permute-start.24 = (f32[256,128]{1,0:T(8,128)S(1)}, f32[256,128]{1,0:T(8,128)S(1)}, u32[]{:S(2)}, u32[]{:S(2)}) collective-permute-start(f32[256,128]{1,0:T(8,128)S(1)} %pad_maximum_fusion.1), channel_id=1, source_target_pairs={{0,2},{1,3},{2,0},{3,1},{4,6},{5,7},{6,4},{7,5},{8,10},{9,11},{10,... | collective-permute-start | bytes 393224 | tf_op jit(solution)/shard_map/ppermute | solution.py:353
  47.4 10.2 %collective-permute-start.25 = (f32[256,128]{1,0:T(8,128)S(1)}, f32[256,128]{1,0:T(8,128)S(1)}, u32[]{:S(2)}, u32[]{:S(2)}) collective-permute-start(f32[256,128]{1,0:T(8,128)S(1)} %pad_maximum_fusion.1), channel_id=1, source_target_pairs={{0,4},{1,5},{2,6},{3,7},{4,0},{5,1},{6,2},{7,3},{8,12},{9,13},{10,... | collective-permute-start | bytes 393224 | tf_op jit(solution)/shard_map/ppermute | solution.py:353
  50.5 14.4 %collective-permute-start.26 = (f32[256,128]{1,0:T(8,128)S(1)}, f32[256,128]{1,0:T(8,128)S(1)}, u32[]{:S(2)}, u32[]{:S(2)}) collective-permute-start(f32[256,128]{1,0:T(8,128)S(1)} %pad_maximum_fusion.1), channel_id=1, source_target_pairs={{0,6},{1,7},{2,4},{3,5},{4,2},{5,3},{6,0},{7,1},{8,14},{9,15},{10,... | collective-permute-start | bytes 393224 | tf_op jit(solution)/shard_map/ppermute | solution.py:353
  53.1 6.0 %collective-permute-start.6 = (f32[80,128]{1,0:T(8,128)S(1)}, f32[80,128]{1,0:T(8,128)S(1)}, u32[]{:S(2)}, u32[]{:S(2)}) collective-permute-start(f32[80,128]{1,0:T(8,128)S(1)} %get-tuple-element.37), channel_id=1, source_target_pairs={{0,24},{8,16},{16,8},{24,0},{1,25},{9,17},{17,9},{25,1},{2,26},{10... | collective-permute-start | bytes 122888 | tf_op jit(solution)/shard_map/ppermute | solution.py:353
  55.1 5.3 %collective-permute-start.5 = (f32[80,128]{1,0:T(8,128)S(1)}, f32[80,128]{1,0:T(8,128)S(1)}, u32[]{:S(2)}, u32[]{:S(2)}) collective-permute-start(f32[80,128]{1,0:T(8,128)S(1)} %get-tuple-element.38), channel_id=1, source_target_pairs={{0,16},{8,24},{16,0},{24,8},{1,17},{9,25},{17,1},{25,9},{2,18},{10... | collective-permute-start | bytes 122888 | tf_op jit(solution)/shard_map/ppermute | solution.py:353
  55.1 5.3 %collective-permute-start.4 = (f32[80,128]{1,0:T(8,128)S(1)}, f32[80,128]{1,0:T(8,128)S(1)}, u32[]{:S(2)}, u32[]{:S(2)}) collective-permute-start(f32[80,128]{1,0:T(8,128)S(1)} %get-tuple-element.36), channel_id=1, source_target_pairs={{0,8},{8,0},{16,24},{24,16},{1,9},{9,1},{17,25},{25,17},{2,10},{10... | collective-permute-start | bytes 122888 | tf_op jit(solution)/shard_map/ppermute | solution.py:353
  60.5 4.6 %collective-permute-start.7 = (f32[80,128]{1,0:T(8,128)S(1)}, f32[80,128]{1,0:T(8,128)S(1)}, u32[]{:S(2)}, u32[]{:S(2)}) collective-permute-start(f32[80,128]{1,0:T(8,128)S(1)} %get-tuple-element.27), channel_id=1, source_target_pairs={{0,8},{8,0},{16,24},{24,16},{1,9},{9,1},{17,25},{25,17},{2,10},{10... | collective-permute-start | bytes 122888 | tf_op jit(solution)/shard_map/ppermute | solution.py:353
  61.7 5.3 %collective-permute-start.8 = (f32[80,128]{1,0:T(8,128)S(1)}, f32[80,128]{1,0:T(8,128)S(1)}, u32[]{:S(2)}, u32[]{:S(2)}) collective-permute-start(f32[80,128]{1,0:T(8,128)S(1)} %get-tuple-element.27), channel_id=1, source_target_pairs={{0,16},{8,24},{16,0},{24,8},{1,17},{9,25},{17,1},{25,9},{2,18},{10... | collective-permute-start | bytes 122888 | tf_op jit(solution)/shard_map/ppermute | solution.py:353
  63.1 5.8 %collective-permute-start.9 = (f32[80,128]{1,0:T(8,128)S(1)}, f32[80,128]{1,0:T(8,128)S(1)}, u32[]{:S(2)}, u32[]{:S(2)}) collective-permute-start(f32[80,128]{1,0:T(8,128)S(1)} %get-tuple-element.27), channel_id=1, source_target_pairs={{0,24},{8,16},{16,8},{24,0},{1,25},{9,17},{17,9},{25,1},{2,26},{10... | collective-permute-start | bytes 122888 | tf_op jit(solution)/shard_map/ppermute | solution.py:353
  64.9 12.8 %copy-start.1 = (f32[1024,128]{1,0:T(8,128)}, f32[1024,128]{1,0:T(8,128)S(1)}, u32[]{:S(2)}) copy-start(f32[1024,128]{1,0:T(8,128)S(1)} %constant_dynamic-update-slice_fusion.7.refs_0_) | copy-start | bytes 1572868
  64.9 12.8 %collective-permute-start.27 = (f32[1024,128]{1,0:T(8,128)S(1)}, f32[1024,128]{1,0:T(8,128)S(1)}, u32[]{:S(2)}, u32[]{:S(2)}) collective-permute-start(f32[1024,128]{1,0:T(8,128)S(1)} %constant_dynamic-update-slice_fusion.7.refs_0_), channel_id=1, source_target_pairs={{0,1},{1,0},{2,3},{3,2},{4,5},{5,4},{6,7},{7,6},{8,9},{9,8},{10,11... | collective-permute-start | bytes 1572872 | tf_op jit(solution)/shard_map/ppermute | solution.py:353
  69.0 5.4 %collective-permute-start.10 = (f32[320,128]{1,0:T(8,128)S(1)}, f32[320,128]{1,0:T(8,128)S(1)}, u32[]{:S(2)}, u32[]{:S(2)}) collective-permute-start(f32[320,128]{1,0:T(8,128)S(1)} %pad_maximum_fusion), channel_id=1, source_target_pairs={{0,2},{1,3},{2,0},{3,1},{4,6},{5,7},{6,4},{7,5},{8,10},{9,11},{10,... | collective-permute-start | bytes 491528 | tf_op jit(solution)/shard_map/ppermute | solution.py:353
  70.5 5.3 %collective-permute-start.11 = (f32[320,128]{1,0:T(8,128)S(1)}, f32[320,128]{1,0:T(8,128)S(1)}, u32[]{:S(2)}, u32[]{:S(2)}) collective-permute-start(f32[320,128]{1,0:T(8,128)S(1)} %pad_maximum_fusion), channel_id=1, source_target_pairs={{0,4},{1,5},{2,6},{3,7},{4,0},{5,1},{6,2},{7,3},{8,12},{9,13},{10,... | collective-permute-start | bytes 491528 | tf_op jit(solution)/shard_map/ppermute | solution.py:353
  71.4 6.2 %collective-permute-start.12 = (f32[320,128]{1,0:T(8,128)S(1)}, f32[320,128]{1,0:T(8,128)S(1)}, u32[]{:S(2)}, u32[]{:S(2)}) collective-permute-start(f32[320,128]{1,0:T(8,128)S(1)} %pad_maximum_fusion), channel_id=1, source_target_pairs={{0,6},{1,7},{2,4},{3,5},{4,2},{5,3},{6,0},{7,1},{8,14},{9,15},{10,... | collective-permute-start | bytes 491528 | tf_op jit(solution)/shard_map/ppermute | solution.py:353
  77.7 11.1 %copy-start = (f32[1280,128]{1,0:T(8,128)}, f32[1280,128]{1,0:T(8,128)S(1)}, u32[]{:S(2)}) copy-start(f32[1280,128]{1,0:T(8,128)S(1)} %constant_dynamic-update-slice_fusion.refs_0_) | copy-start | bytes 1966084
  77.7 11.1 %collective-permute-start.13 = (f32[1280,128]{1,0:T(8,128)S(1)}, f32[1280,128]{1,0:T(8,128)S(1)}, u32[]{:S(2)}, u32[]{:S(2)}) collective-permute-start(f32[1280,128]{1,0:T(8,128)S(1)} %constant_dynamic-update-slice_fusion.refs_0_), channel_id=1, source_target_pairs={{0,1},{1,0},{2,3},{3,2},{4,5},{5,4},{6,7},{7,6},{8,9},{9,8},{10,11... | collective-permute-start | bytes 1966088 | tf_op jit(solution)/shard_map/ppermute | solution.py:353
  77.8 0.9 copy-start.3
  88.7 0.9 copy-start.2

commit v4 on v2

v4 whole, which is shorter than its diff:
```python
import functools

import jax
import jax.numpy as jnp
from jax import lax
from jax.experimental import pallas as pl
from jax.experimental.pallas import tpu as pltpu
from jax.sharding import PartitionSpec as P

F32 = jnp.float32
BF16 = jnp.bfloat16
NB = 128
VMEM = pltpu.CompilerParams(vmem_limit_bytes=56 * 2**20)


def split(x):
    hi = x.astype(BF16)
    return hi, (x - hi.astype(F32)).astype(BF16)


def block_at(width):
    nb = width // NB
    places, at = {}, 0
    for i in range(nb):
        for j in range(i, nb):
            places[i, j] = at
            at += 1
    return places


def dot_t(a, b):
    return lax.dot_general(a, b, (((0,), (0,)), ((), ())), preferred_element_type=F32)


def gram_kernel(step_rows, sent, count_ref, rows_ref, vals_ref, prior_ref, pinfo_ref, keep_ref, send_ref, acc, info):
    t = pl.program_id(0)
    width = rows_ref.shape[1]
    nb = width // NB
    live = count_ref[0] - t * step_rows
    tile = min(2 * NB, width)
    tiles = [(i, i + tile, i, width) for i in range(0, width, tile)]

    @pl.when(t == 0)
    def _():
        p = prior_ref[...]
        hi = p.astype(BF16)
        rest = p - hi.astype(F32)
        mid = rest.astype(BF16)
        lo = (rest - mid.astype(F32)).astype(BF16)
        left = jnp.concatenate([hi, hi, mid, mid, hi, lo], axis=0)
        right = jnp.concatenate([hi, mid, hi, mid, lo, hi], axis=0)
        for i0, i1, j0, j1 in tiles:
            acc[i0:i1, j0:j1] = dot_t(left[:, i0:i1], right[:, j0:j1])
        info[...] = jnp.broadcast_to(
            jnp.dot(pinfo_ref[...], p, precision=lax.Precision.HIGHEST, preferred_element_type=F32), info.shape
        )

    @pl.when(live > 0)
    def _():
        place = lax.broadcasted_iota(jnp.int32, (step_rows, 1), 0)
        x = jnp.where(place < live, rows_ref[...], jnp.zeros((), BF16))
        for i0, i1, j0, j1 in tiles:
            acc[i0:i1, j0:j1] += dot_t(x[:, i0:i1], x[:, j0:j1])
        v = vals_ref[pl.ds(pl.multiple_of(t * step_rows, step_rows), step_rows)].astype(F32).reshape(1, step_rows)
        v = jnp.broadcast_to(v, (8, step_rows)).astype(BF16)
        info[...] += jnp.dot(v, x, preferred_element_type=F32)

    @pl.when(t == pl.num_programs(0) - 1)
    def _():
        half = sent // 2
        side = lax.axis_index("blk") % 2

        def pack(pair):
            for (i, j), n in block_at(width).items():
                out, off = pair[n * NB // half], n * NB % half
                out[off : off + NB, :] = acc[i * NB : (i + 1) * NB, j * NB : (j + 1) * NB]
            for row in range(nb * (nb + 1) // 2 * NB, sent, NB):
                pair[row // half][row % half : row % half + NB, :] = jnp.zeros((NB, NB), F32)
            hw = NB // 2
            for b in range(2 * nb):
                pair[0][hw + b : hw + b + 1, 0:hw] = info[0:1, b * hw : (b + 1) * hw]

        @pl.when(side == 0)
        def _():
            pack((keep_ref, send_ref))

        @pl.when(side != 0)
        def _():
            pack((send_ref, keep_ref))


def gram(readings, values, counts, prior_root, prior_info, sent):
    cap, width = readings.shape
    step_rows = min(1024, cap)
    whole = pl.BlockSpec(memory_space=pltpu.VMEM)
    return pl.pallas_call(
        functools.partial(gram_kernel, step_rows, sent),
        grid=(cap // step_rows,),
        in_specs=[
            pl.BlockSpec(memory_space=pltpu.SMEM),
            pl.BlockSpec((step_rows, width), lambda t: (t, 0)),
            whole,
            whole,
            whole,
        ],
        out_specs=[whole] * 2,
        out_shape=[jax.ShapeDtypeStruct((sent // 2, NB), F32)] * 2,
        scratch_shapes=[pltpu.VMEM((width, width), F32), pltpu.VMEM((8, width), F32)],
        compiler_params=VMEM,
        cost_estimate=pl.CostEstimate(flops=2 * cap * width * width, bytes_accessed=2 * cap * width, transcendentals=0),
        name="gram",
    )(counts, readings, values, prior_root, prior_info.reshape(1, -1))


def lane_of(v, at):
    return jnp.broadcast_to(v[:, at : at + 1], v.shape)


def row_of(v, at):
    return jnp.broadcast_to(v[at : at + 1, :], v.shape)


PANEL, STRIP = 16, 32


def factor_block(read, write, other_work):
    lane = lax.broadcasted_iota(jnp.int32, (8, NB), 1)
    sub = lax.broadcasted_iota(jnp.int32, (8, NB), 0)
    groups = NB // 8
    per = STRIP // 8
    a = [read(u) for u in range(groups)]
    for t in range(NB // STRIP):
        s0 = STRIP * t
        w = a[per * t : per * t + per]
        pivot = [None] * per
        for panel in range(STRIP // PANEL):
            g0 = panel * (PANEL // 8)
            c0 = s0 + PANEL * panel
            col = {}
            for k in range(PANEL):
                for i in range(g0 + k // 8, per):
                    col[i, k] = lane_of(w[i], c0 + k)
            next(other_work, None)
            d = row_of(col[g0, 0], 0)
            inv = 1.0 / d
            for k in range(PANEL):
                gk, ks = g0 + k // 8, k % 8
                pivot[gk] = d if ks == 0 else jnp.where(sub == ks, d, pivot[gk])
                below = {v: row_of(col[g0 + v // 8, k], v % 8) for v in range(k + 1, PANEL)}
                if k + 1 < PANEL:
                    ahead = row_of(col[g0 + (k + 1) // 8, k + 1], (k + 1) % 8)
                    d_next = ahead - (below[k + 1] * below[k + 1]) * inv
                    inv_next = 1.0 / d_next
                one = lane == c0 + k
                row = jnp.where(one, 1.0, row_of(w[gk], ks))
                for i in range(gk, per):
                    m = col[i, k] * inv
                    if i == gk:
                        m = jnp.where(sub > ks, m, 0.0)
                    for v in range(k + 1, PANEL):
                        if i >= g0 + v // 8:
                            col[i, v] = col[i, v] - m * below[v]
                    gone = one & (sub > ks) if i == gk else one
                    w[i] = jnp.where(gone, 0.0, w[i]) - m * row
                if k + 1 < PANEL:
                    d, inv = d_next, inv_next
        inside = (lane >= s0) & (lane < s0 + STRIP)
        scaled = []
        for i in range(per):
            scale = lax.rsqrt(pivot[i])
            v = w[i] * scale
            row = sub + (s0 + 8 * i)
            lower = jnp.where(lane < row, v, jnp.where(lane == row, scale, 0.0))
            write(per * t + i, jnp.where(lane >= row, v, 0.0), lower)
            scaled.append(jnp.where(inside, lower, v))
        if s0 + STRIP < NB:
            hi, lo = split(jnp.concatenate(scaled, axis=0))
            off = dot_t(jnp.concatenate([hi, hi, lo], axis=0), jnp.concatenate([hi, lo, hi], axis=0))
            for i in range(per * (t + 1), groups):
                a[i] = jnp.where(inside, 0.0, a[i]) - off[8 * i : 8 * i + 8, :]


def three(hi, lo, axis):
    return jnp.concatenate([hi, hi, lo], axis=axis)


def three_other(hi, lo, axis):
    return jnp.concatenate([hi, lo, hi], axis=axis)


def factor_kernel(n_quarter, n_layer, own_ref, far_ref, root_ref, info_ref, g, s, minv, r, uhi, ulo, thi, tlo, y):
    width = r.shape[1]
    nb = width // NB
    place = block_at(width)
    blk, layer = lax.axis_index("blk"), lax.axis_index("fibre")
    side, quarter = blk % 2, blk // 2
    piece = own_ref.shape[0] // (n_quarter * n_layer)
    for ms in range(n_quarter):
        for mz in range(n_layer):
            for mc, ref in enumerate((own_ref, far_ref)):
                to = (((side ^ mc) * n_quarter + (quarter ^ ms)) * n_layer + (layer ^ mz)) * piece
                at = (ms * n_layer + mz) * piece
                g[pl.ds(pl.multiple_of(to, 8), piece), :] = ref[at : at + piece, :]

    def block(i, j):
        return g[place[i, j] * NB : place[i, j] * NB + NB, :]

    def span(i):
        return slice(i * NB, i * NB + NB)

    hw = NB // 2
    corner = g[0:NB, :]
    mirror = corner.T
    for b in range(2 * nb):
        y[:, b * hw : (b + 1) * hw] = jnp.broadcast_to(corner[hw + b : hw + b + 1, 0:hw], (8, hw))
    lane = lax.broadcasted_iota(jnp.int32, (hw, NB), 1)
    s[0:hw, 0:NB] = corner[0:hw, :]
    s[hw:NB, 0:NB] = jnp.where(lane < hw, mirror[hw:, :], corner[hw:, :])
    for b in range(1, nb):
        s[0:NB, span(b)] = block(0, b)

    def inverse(i):
        return split(minv[span(i), :])

    def solve(i, c):
        mh, ml = inverse(i)
        sh, sl = split(s[span(i), c])
        u = jnp.dot(three(mh, ml, 1), three_other(sh, sl, 0), preferred_element_type=F32)
        r[span(i), c] = u
        uh, ul = split(u)
        uhi[span(i), c] = uh
        ulo[span(i), c] = ul
        for b in range(c.start // NB, c.stop // NB):
            t = u[:, b * NB - c.start : b * NB - c.start + NB].T
            th, tl = split(t)
            thi[span(b), span(i)] = th
            tlo[span(b), span(i)] = tl

    def reduce(i, c):
        up = slice(0, i * NB)
        off = jnp.dot(
            three(thi[span(i), up], tlo[span(i), up], 1),
            three_other(uhi[up, c], ulo[up, c], 0),
            preferred_element_type=F32,
        )
        for b in range(c.start // NB, c.stop // NB):
            s[span(i), span(b)] = block(i, b) - off[:, b * NB - c.start : b * NB - c.start + NB]

    def rest_of(i):
        cuts = [slice(c, min(c + 2 * NB, width)) for c in range((i + 2) * NB, width, 2 * NB)]
        for c in cuts:
            solve(i, c)
            yield
        for c in cuts:
            reduce(i + 1, c)
            yield
        mh, ml = inverse(i)
        bh, bl = split(y[:, span(i)])
        yi = lax.dot_general(
            three(bh, bl, 1), three_other(mh, ml, 1), (((1,), (1,)), ((), ())), preferred_element_type=F32
        )
        y[:, span(i)] = yi
        yield
        if i + 1 < nb:
            c = slice((i + 1) * NB, width)
            yh, yl = split(yi)
            y[:, c] -= jnp.dot(
                three(yh, yl, 1), three_other(uhi[span(i), c], ulo[span(i), c], 0), preferred_element_type=F32
            )
            yield
        if i:
            r[span(i), 0 : i * NB] = jnp.zeros((NB, i * NB), F32)
            yield

    other_work = iter(())
    for i in range(nb):

        def read(u):
            return s[i * NB + 8 * u : i * NB + 8 * u + 8, span(i)]

        def write(u, upper, lower):
            at = slice(i * NB + 8 * u, i * NB + 8 * u + 8)
            r[at, span(i)] = upper
            minv[at, :] = lower

        factor_block(read, write, other_work)
        for _ in other_work:
            pass
        if i + 1 < nb:
            solve(i, span(i + 1))
            reduce(i + 1, span(i + 1))
        other_work = rest_of(i)
    for _ in other_work:
        pass
    rows = root_ref.shape[0]
    root_ref[...] = r[pl.ds(pl.multiple_of(blk * rows, 8), rows), :]
    for b in range(nb):
        info_ref[b : b + 1, :] = y[0:1, span(b)]


def factor(own, far, n_quarter, n_layer, width, rows):
    whole = pl.BlockSpec(memory_space=pltpu.VMEM)
    nb = width // NB
    return pl.pallas_call(
        functools.partial(factor_kernel, n_quarter, n_layer),
        in_specs=[whole] * 2,
        out_specs=[whole] * 2,
        out_shape=[jax.ShapeDtypeStruct((rows, width), F32), jax.ShapeDtypeStruct((nb, NB), F32)],
        scratch_shapes=[
            pltpu.VMEM((2 * own.shape[0], NB), F32),
            pltpu.VMEM((width, width), F32),
            pltpu.VMEM((width, NB), F32),
            pltpu.VMEM((width, width), F32),
        ]
        + [pltpu.VMEM((width, width), BF16)] * 4
        + [pltpu.VMEM((8, width), F32)],
        compiler_params=VMEM,
        name="factor",
    )(own, far)


def swap(x, axis, mask):
    n = lax.axis_size(axis)
    return lax.ppermute(x, axis, [(d, d ^ mask) for d in range(n)])


def shares(parts, count, me):
    rows = parts[0].shape[0] // count
    return [
        functools.reduce(lambda a, b: a + b, [lax.dynamic_slice_in_dim(x, (me ^ m) * rows, rows, 0) for x in parts])
        for m in range(count)
    ]


def trade(mine, axis, masks):
    return [mine[0]] + [swap(x, axis, m) for x, m in zip(mine[1:], masks)]


def gather(x, axis, masks):
    return jnp.concatenate([x] + [swap(x, axis, m) for m in masks], axis=0)


def local(readings, values, counts, prior_root, prior_info):
    width = readings.shape[1]
    n_blk, n_fibre = lax.axis_size("blk"), lax.axis_size("fibre")
    blk, fibre = lax.axis_index("blk"), lax.axis_index("fibre")
    n_quarter = n_blk // 2
    quarters = [2 * m for m in range(1, n_quarter)]
    layers = list(range(1, n_fibre))
    unit = 8 * n_blk * n_fibre
    nb = width // NB
    sent = -(-(nb * (nb + 1) // 2 * NB) // unit) * unit

    keep, send = gram(readings, values, counts, prior_root, prior_info, sent)
    parts = [keep, swap(send, "blk", 1)]
    parts = trade(shares(parts, n_quarter, blk // 2), "blk", quarters)
    parts = trade(shares(parts, n_fibre, fibre), "fibre", layers)
    own = functools.reduce(lambda x, y: x + y, parts)
    own = gather(gather(own, "fibre", layers), "blk", quarters)
    far = swap(own, "blk", 1)
    root, info = factor(own, far, n_quarter, n_fibre, width, width // n_blk)
    return root, info.reshape(width)


def solution(mesh):
    placed = (
        P(("fibre", "blk"), None),
        P(("fibre", "blk")),
        P(("fibre", "blk")),
        P(("fibre", "blk"), None),
        P(("fibre", "blk")),
    )
    return jax.shard_map(
        local, mesh=mesh, in_specs=placed, out_specs=(P("blk", None), P()), check_vma=False
    )
```

time: 107 us -> 99.6 us (0.931)
  Pallas kernels: 42.5 us -> 35.7 us
  starting transfers between devices: 18.9 us -> 21.3 us
  other arithmetic: 2.9 us -> 1.47 us
  local copies, waits for them, and re-layouts: 2.4 us -> 1.08 us
  waiting for transfers between devices: 39.2 us -> 38.1 us
    pallas_call x2, Pallas kernels: 42.5 us -> 35.7 us  [the longest x1 27.9 us: factor(): pl.pallas_call(functools.partial(factor_kernel, n_quarter, n_layer), in_s...]
    ppermute x14, starting transfers between devices: 18.9 us -> 21.3 us  [swap(): return lax.ppermute(x, axis, [(d, d ^ mask) for d in range(n)])]
    another operation x2 -> x0, other arithmetic: 1.44 us -> none  [the longest x1 0.79 us: local(): scalars = jnp.stack([side, quarter, layer, blk]).astype(jnp.int32)]
    reshape x1 -> x0, local copies, waits for them, and re-layouts: 1.32 us -> none  [gram(): values.astype(F32).reshape(steps, step_rows)]
    ppermute x14, waiting for transfers between devices: 39.2 us -> 38.1 us  [swap(): return lax.ppermute(x, axis, [(d, d ^ mask) for d in range(n)])]
  transfers between devices with their start and end apart: 14 -> 14, of which waited for: 13 -> 13; matrix products, arithmetic and copies ran while one was open for 1% -> 0% of each run, Pallas kernels for 0% -> 0%
where the time goes in v4:
time: 99.6 us; the launch traced here: 99.1 us
  waiting for transfers between devices  38.1 us (38%)
  Pallas kernels  35.7 us (36%)
  starting transfers between devices  21.3 us (21%)
  other arithmetic  1.47 us (1%)
  between operations  1.35 us (1%)
  local copies, waits for them, and re-layouts  1.08 us (1%)
    ppermute x14, waiting for transfers between devices, swap(): return lax.ppermute(x, axis, [(d, d ^ mask) for d in range(n)])  38.1 us
    pallas_call x1, Pallas kernels, factor(): pl.pallas_call(functools.partial(factor_kernel, n_quarter, n_layer), in_s...  27.9 us
    ppermute x14, starting transfers between devices, swap(): return lax.ppermute(x, axis, [(d, d ^ mask) for d in range(n)])  21.3 us
    pallas_call x1, Pallas kernels, gram(): pl.pallas_call(functools.partial(gram_kernel, step_rows, sent), grid=(cap...  7.86 us
  transfers between devices with their start and end apart: 14, of which 13 were waited for; matrix products, arithmetic and copies ran while one was open for 0% of the time, Pallas kernels for 0%

profile of v4, /device:TPU:0, one launch (start us, length us, event | category | flops | bytes accessed | tf_op | source)
XLA Modules:
  0.0 99.1 jit_solution(8281280296934891558)
XLA Ops:
  1.3 7.9 %gram.1 = (f32[2304,128]{1,0:T(8,128)}, f32[2304,128]{1,0:T(8,128)}) custom-call(s32[1]{0:T(128)S(6)} %copy.13.count_ref, bf16[4096,1024]{1,0:T(8,128)(2,1)} %rows_ref.1, bf16[4096]{0:T(1024)(128)(2,1)} %vals_ref.1, f32[32,1024]{1,0:T(8,128)} %prior_ref.1, f32[1,32]{1,0:T(1,128)} %bitcast.3), custom_call_target="tpu_custom_call" | custom-call | flops 8589934592 | bytes 8388608 | tf_op jit(solution)/shard_map/gram/pallas_call | solution.py:96
  9.1 1.6 %collective-permute-start = (f32[2304,128]{1,0:T(8,128)}, f32[2304,128]{1,0:T(8,128)S(1)}, u32[]{:S(2)}, u32[]{:S(2)}) collective-permute-start(f32[2304,128]{1,0:T(8,128)} %get-tuple-element.7), channel_id=1, source_target_pairs={{0,1},{1,0},{2,3},{3,2},{4,5},{5,4},{6,7},{7,6},{8,9},{9,8},{10,11... | collective-permute-start | bytes 3538952 | tf_op jit(solution)/shard_map/ppermute | solution.py:324
  10.8 2.7 %collective-permute-done = f32[2304,128]{1,0:T(8,128)S(1)} collective-permute-done((f32[2304,128]{1,0:T(8,128)}, f32[2304,128]{1,0:T(8,128)S(1)}, u32[]{:S(2)}, u32[]{:S(2)}) %collective-permute-start) | collective-permute-done | bytes 1179680 | tf_op jit(solution)/shard_map/ppermute | solution.py:324
  13.5 1.3 %dynamic-slice_add_fusion.3 = (f32[576,128]{1,0:T(8,128)S(1)}, f32[576,128]{1,0:T(8,128)S(1)}, f32[576,128]{1,0:T(8,128)S(1)}, f32[576,128]{1,0:T(8,128)S(1)}) fusion(f32[2304,128]{1,0:T(8,128)S(1)} %collective-permute-done, s32[]{:T(128)S(6)} %select_n.22, f32[2304,128]{1,0:T(8,128)} %get-tuple-element.6, s32[]{:T(128)S(6)} %select_n.50, s32[]{:T(128)S(6)} %select_n.25, ...), kind=kLoop, calls=%fused_computation.4 | loop fusion | flops 294912 | bytes 3538960 | tf_op jit(solution)/shard_map/add | solution.py:330
  14.8 3.9 %collective-permute-start.3 = (f32[576,128]{1,0:T(8,128)S(1)}, f32[576,128]{1,0:T(8,128)S(1)}, u32[]{:S(2)}, u32[]{:S(2)}) collective-permute-start(f32[576,128]{1,0:T(8,128)S(1)} %get-tuple-element.13), channel_id=1, source_target_pairs={{0,6},{1,7},{2,4},{3,5},{4,2},{5,3},{6,0},{7,1},{8,14},{9,15},{10,... | collective-permute-start | bytes 884744 | tf_op jit(solution)/shard_map/ppermute | solution.py:324
  18.7 2.6 %collective-permute-start.2 = (f32[576,128]{1,0:T(8,128)S(1)}, f32[576,128]{1,0:T(8,128)S(1)}, u32[]{:S(2)}, u32[]{:S(2)}) collective-permute-start(f32[576,128]{1,0:T(8,128)S(1)} %get-tuple-element.14), channel_id=1, source_target_pairs={{0,4},{1,5},{2,6},{3,7},{4,0},{5,1},{6,2},{7,3},{8,12},{9,13},{10,... | collective-permute-start | bytes 884744 | tf_op jit(solution)/shard_map/ppermute | solution.py:324
  21.3 0.0 collective-permute-start.1
  21.3 5.3 %collective-permute-done.3 = f32[576,128]{1,0:T(8,128)S(1)} collective-permute-done((f32[576,128]{1,0:T(8,128)S(1)}, f32[576,128]{1,0:T(8,128)S(1)}, u32[]{:S(2)}, u32[]{:S(2)}) %collective-permute-start.3) | collective-permute-done | bytes 294944 | tf_op jit(solution)/shard_map/ppermute | solution.py:324
  26.5 5.9 %collective-permute-done.2 = f32[576,128]{1,0:T(8,128)S(1)} collective-permute-done((f32[576,128]{1,0:T(8,128)S(1)}, f32[576,128]{1,0:T(8,128)S(1)}, u32[]{:S(2)}, u32[]{:S(2)}) %collective-permute-start.2) | collective-permute-done | bytes 294944 | tf_op jit(solution)/shard_map/ppermute | solution.py:324
  32.4 1.1 %collective-permute-done.1 = f32[576,128]{1,0:T(8,128)S(1)} collective-permute-done((f32[576,128]{1,0:T(8,128)S(1)}, f32[576,128]{1,0:T(8,128)S(1)}, u32[]{:S(2)}, u32[]{:S(2)}) %collective-permute-start.1) | collective-permute-done | bytes 294944 | tf_op jit(solution)/shard_map/ppermute | solution.py:324
  33.5 0.1 dynamic-slice_add_fusion.6
  33.5 4.5 %collective-permute-start.6 = (f32[144,128]{1,0:T(8,128)S(1)}, f32[144,128]{1,0:T(8,128)S(1)}, u32[]{:S(2)}, u32[]{:S(2)}) collective-permute-start(f32[144,128]{1,0:T(8,128)S(1)} %get-tuple-element.17), channel_id=1, source_target_pairs={{0,24},{8,16},{16,8},{24,0},{1,25},{9,17},{17,9},{25,1},{2,26},{10... | collective-permute-start | bytes 221192 | tf_op jit(solution)/shard_map/ppermute | solution.py:324
  38.0 0.0 collective-permute-start.5
  38.0 0.6 collective-permute-start.4
  38.7 2.5 %collective-permute-done.6 = f32[144,128]{1,0:T(8,128)S(1)} collective-permute-done((f32[144,128]{1,0:T(8,128)S(1)}, f32[144,128]{1,0:T(8,128)S(1)}, u32[]{:S(2)}, u32[]{:S(2)}) %collective-permute-start.6) | collective-permute-done | bytes 73760 | tf_op jit(solution)/shard_map/ppermute | solution.py:324
  41.2 2.7 %collective-permute-done.5 = f32[144,128]{1,0:T(8,128)S(1)} collective-permute-done((f32[144,128]{1,0:T(8,128)S(1)}, f32[144,128]{1,0:T(8,128)S(1)}, u32[]{:S(2)}, u32[]{:S(2)}) %collective-permute-start.5) | collective-permute-done | bytes 73760 | tf_op jit(solution)/shard_map/ppermute | solution.py:324
  43.8 0.1 collective-permute-done.4
  44.0 1.6 %collective-permute-start.7 = (f32[144,128]{1,0:T(8,128)S(1)}, f32[144,128]{1,0:T(8,128)S(1)}, u32[]{:S(2)}, u32[]{:S(2)}) collective-permute-start(f32[144,128]{1,0:T(8,128)S(1)} %get-tuple-element.11), channel_id=1, source_target_pairs={{0,8},{8,0},{16,24},{24,16},{1,9},{9,1},{17,25},{25,17},{2,10},{10... | collective-permute-start | bytes 221192 | tf_op jit(solution)/shard_map/ppermute | solution.py:324
  45.5 1.5 %collective-permute-start.8 = (f32[144,128]{1,0:T(8,128)S(1)}, f32[144,128]{1,0:T(8,128)S(1)}, u32[]{:S(2)}, u32[]{:S(2)}) collective-permute-start(f32[144,128]{1,0:T(8,128)S(1)} %get-tuple-element.11), channel_id=1, source_target_pairs={{0,16},{8,24},{16,0},{24,8},{1,17},{9,25},{17,1},{25,9},{2,18},{10... | collective-permute-start | bytes 221192 | tf_op jit(solution)/shard_map/ppermute | solution.py:324
  47.1 1.4 %collective-permute-start.9 = (f32[144,128]{1,0:T(8,128)S(1)}, f32[144,128]{1,0:T(8,128)S(1)}, u32[]{:S(2)}, u32[]{:S(2)}) collective-permute-start(f32[144,128]{1,0:T(8,128)S(1)} %get-tuple-element.11), channel_id=1, source_target_pairs={{0,24},{8,16},{16,8},{24,0},{1,25},{9,17},{17,9},{25,1},{2,26},{10... | collective-permute-start | bytes 221192 | tf_op jit(solution)/shard_map/ppermute | solution.py:324
  48.4 0.8 collective-permute-done.7
  49.2 3.2 %collective-permute-done.8 = f32[144,128]{1,0:T(8,128)S(1)} collective-permute-done((f32[144,128]{1,0:T(8,128)S(1)}, f32[144,128]{1,0:T(8,128)S(1)}, u32[]{:S(2)}, u32[]{:S(2)}) %collective-permute-start.8) | collective-permute-done | bytes 73760 | tf_op jit(solution)/shard_map/ppermute | solution.py:324
  52.4 0.9 collective-permute-done.9
  53.4 0.4 collective-permute-start.10
  53.7 1.3 %collective-permute-start.11 = (f32[576,128]{1,0:T(8,128)S(1)}, f32[576,128]{1,0:T(8,128)S(1)}, u32[]{:S(2)}, u32[]{:S(2)}) collective-permute-start(f32[576,128]{1,0:T(8,128)S(1)} %pad_maximum_fusion), channel_id=1, source_target_pairs={{0,4},{1,5},{2,6},{3,7},{4,0},{5,1},{6,2},{7,3},{8,12},{9,13},{10,... | collective-permute-start | bytes 884744 | tf_op jit(solution)/shard_map/ppermute | solution.py:324
  55.1 1.8 %collective-permute-start.12 = (f32[576,128]{1,0:T(8,128)S(1)}, f32[576,128]{1,0:T(8,128)S(1)}, u32[]{:S(2)}, u32[]{:S(2)}) collective-permute-start(f32[576,128]{1,0:T(8,128)S(1)} %pad_maximum_fusion), channel_id=1, source_target_pairs={{0,6},{1,7},{2,4},{3,5},{4,2},{5,3},{6,0},{7,1},{8,14},{9,15},{10,... | collective-permute-start | bytes 884744 | tf_op jit(solution)/shard_map/ppermute | solution.py:324
  56.9 6.4 %collective-permute-done.10 = f32[576,128]{1,0:T(8,128)S(1)} collective-permute-done((f32[576,128]{1,0:T(8,128)S(1)}, f32[576,128]{1,0:T(8,128)S(1)}, u32[]{:S(2)}, u32[]{:S(2)}) %collective-permute-start.10) | collective-permute-done | bytes 294944 | tf_op jit(solution)/shard_map/ppermute | solution.py:324
  63.4 0.0 collective-permute-done.11
  63.4 3.8 %collective-permute-done.12 = f32[576,128]{1,0:T(8,128)S(1)} collective-permute-done((f32[576,128]{1,0:T(8,128)S(1)}, f32[576,128]{1,0:T(8,128)S(1)}, u32[]{:S(2)}, u32[]{:S(2)}) %collective-permute-start.12) | collective-permute-done | bytes 294944 | tf_op jit(solution)/shard_map/ppermute | solution.py:324
  67.3 0.0 copy-start
  67.3 0.1 collective-permute-start.13
  67.3 2.8 %collective-permute-done.13.far_ref = f32[2304,128]{1,0:T(8,128)S(1)} collective-permute-done((f32[2304,128]{1,0:T(8,128)S(1)}, f32[2304,128]{1,0:T(8,128)S(1)}, u32[]{:S(2)}, u32[]{:S(2)}) %collective-permute-start.13) | collective-permute-done | bytes 1179680 | tf_op jit(solution)/shard_map/ppermute | solution.py:324
  70.2 0.0 copy-done
  70.2 0.0 copy-start.1
  70.2 1.0 %copy-done.1 = f32[2304,128]{1,0:T(8,128)} copy-done((f32[2304,128]{1,0:T(8,128)}, f32[2304,128]{1,0:T(8,128)S(1)}, u32[]{:S(2)}) %copy-start.1) | copy-done | bytes 1179672
  71.2 27.9 %factor.1 = (f32[128,1024]{1,0:T(8,128)}, f32[8,128]{1,0:T(8,128)}) custom-call(f32[2304,128]{1,0:T(8,128)} %copy-done, f32[2304,128]{1,0:T(8,128)} %copy-done.1), custom_call_target="tpu_custom_call" | custom-call | tf_op jit(solution)/shard_map/factor/pallas_call | solution.py:304
  (8 shorter events, 0.1 us)
Async XLA Ops:
  9.1 4.3 %collective-permute-start = (f32[2304,128]{1,0:T(8,128)}, f32[2304,128]{1,0:T(8,128)S(1)}, u32[]{:S(2)}, u32[]{:S(2)}) collective-permute-start(f32[2304,128]{1,0:T(8,128)} %get-tuple-element.7), channel_id=1, source_target_pairs={{0,1},{1,0},{2,3},{3,2},{4,5},{5,4},{6,7},{7,6},{8,9},{9,8},{10,11... | collective-permute-start | bytes 3538952 | tf_op jit(solution)/shard_map/ppermute | solution.py:324
  14.8 11.7 %collective-permute-start.3 = (f32[576,128]{1,0:T(8,128)S(1)}, f32[576,128]{1,0:T(8,128)S(1)}, u32[]{:S(2)}, u32[]{:S(2)}) collective-permute-start(f32[576,128]{1,0:T(8,128)S(1)} %get-tuple-element.13), channel_id=1, source_target_pairs={{0,6},{1,7},{2,4},{3,5},{4,2},{5,3},{6,0},{7,1},{8,14},{9,15},{10,... | collective-permute-start | bytes 884744 | tf_op jit(solution)/shard_map/ppermute | solution.py:324
  18.7 13.7 %collective-permute-start.2 = (f32[576,128]{1,0:T(8,128)S(1)}, f32[576,128]{1,0:T(8,128)S(1)}, u32[]{:S(2)}, u32[]{:S(2)}) collective-permute-start(f32[576,128]{1,0:T(8,128)S(1)} %get-tuple-element.14), channel_id=1, source_target_pairs={{0,4},{1,5},{2,6},{3,7},{4,0},{5,1},{6,2},{7,3},{8,12},{9,13},{10,... | collective-permute-start | bytes 884744 | tf_op jit(solution)/shard_map/ppermute | solution.py:324
  21.3 12.2 %collective-permute-start.1 = (f32[576,128]{1,0:T(8,128)S(1)}, f32[576,128]{1,0:T(8,128)S(1)}, u32[]{:S(2)}, u32[]{:S(2)}) collective-permute-start(f32[576,128]{1,0:T(8,128)S(1)} %get-tuple-element.15), channel_id=1, source_target_pairs={{0,2},{1,3},{2,0},{3,1},{4,6},{5,7},{6,4},{7,5},{8,10},{9,11},{10,... | collective-permute-start | bytes 884744 | tf_op jit(solution)/shard_map/ppermute | solution.py:324
  33.5 7.6 %collective-permute-start.6 = (f32[144,128]{1,0:T(8,128)S(1)}, f32[144,128]{1,0:T(8,128)S(1)}, u32[]{:S(2)}, u32[]{:S(2)}) collective-permute-start(f32[144,128]{1,0:T(8,128)S(1)} %get-tuple-element.17), channel_id=1, source_target_pairs={{0,24},{8,16},{16,8},{24,0},{1,25},{9,17},{17,9},{25,1},{2,26},{10... | collective-permute-start | bytes 221192 | tf_op jit(solution)/shard_map/ppermute | solution.py:324
  38.0 5.8 %collective-permute-start.5 = (f32[144,128]{1,0:T(8,128)S(1)}, f32[144,128]{1,0:T(8,128)S(1)}, u32[]{:S(2)}, u32[]{:S(2)}) collective-permute-start(f32[144,128]{1,0:T(8,128)S(1)} %get-tuple-element.18), channel_id=1, source_target_pairs={{0,16},{8,24},{16,0},{24,8},{1,17},{9,25},{17,1},{25,9},{2,18},{10... | collective-permute-start | bytes 221192 | tf_op jit(solution)/shard_map/ppermute | solution.py:324
  38.0 5.9 %collective-permute-start.4 = (f32[144,128]{1,0:T(8,128)S(1)}, f32[144,128]{1,0:T(8,128)S(1)}, u32[]{:S(2)}, u32[]{:S(2)}) collective-permute-start(f32[144,128]{1,0:T(8,128)S(1)} %get-tuple-element.16), channel_id=1, source_target_pairs={{0,8},{8,0},{16,24},{24,16},{1,9},{9,1},{17,25},{25,17},{2,10},{10... | collective-permute-start | bytes 221192 | tf_op jit(solution)/shard_map/ppermute | solution.py:324
  44.0 5.2 %collective-permute-start.7 = (f32[144,128]{1,0:T(8,128)S(1)}, f32[144,128]{1,0:T(8,128)S(1)}, u32[]{:S(2)}, u32[]{:S(2)}) collective-permute-start(f32[144,128]{1,0:T(8,128)S(1)} %get-tuple-element.11), channel_id=1, source_target_pairs={{0,8},{8,0},{16,24},{24,16},{1,9},{9,1},{17,25},{25,17},{2,10},{10... | collective-permute-start | bytes 221192 | tf_op jit(solution)/shard_map/ppermute | solution.py:324
  45.5 6.8 %collective-permute-start.8 = (f32[144,128]{1,0:T(8,128)S(1)}, f32[144,128]{1,0:T(8,128)S(1)}, u32[]{:S(2)}, u32[]{:S(2)}) collective-permute-start(f32[144,128]{1,0:T(8,128)S(1)} %get-tuple-element.11), channel_id=1, source_target_pairs={{0,16},{8,24},{16,0},{24,8},{1,17},{9,25},{17,1},{25,9},{2,18},{10... | collective-permute-start | bytes 221192 | tf_op jit(solution)/shard_map/ppermute | solution.py:324
  47.1 6.3 %collective-permute-start.9 = (f32[144,128]{1,0:T(8,128)S(1)}, f32[144,128]{1,0:T(8,128)S(1)}, u32[]{:S(2)}, u32[]{:S(2)}) collective-permute-start(f32[144,128]{1,0:T(8,128)S(1)} %get-tuple-element.11), channel_id=1, source_target_pairs={{0,24},{8,16},{16,8},{24,0},{1,25},{9,17},{17,9},{25,1},{2,26},{10... | collective-permute-start | bytes 221192 | tf_op jit(solution)/shard_map/ppermute | solution.py:324
  53.4 10.0 %collective-permute-start.10 = (f32[576,128]{1,0:T(8,128)S(1)}, f32[576,128]{1,0:T(8,128)S(1)}, u32[]{:S(2)}, u32[]{:S(2)}) collective-permute-start(f32[576,128]{1,0:T(8,128)S(1)} %pad_maximum_fusion), channel_id=1, source_target_pairs={{0,2},{1,3},{2,0},{3,1},{4,6},{5,7},{6,4},{7,5},{8,10},{9,11},{10,... | collective-permute-start | bytes 884744 | tf_op jit(solution)/shard_map/ppermute | solution.py:324
  53.7 9.6 %collective-permute-start.11 = (f32[576,128]{1,0:T(8,128)S(1)}, f32[576,128]{1,0:T(8,128)S(1)}, u32[]{:S(2)}, u32[]{:S(2)}) collective-permute-start(f32[576,128]{1,0:T(8,128)S(1)} %pad_maximum_fusion), channel_id=1, source_target_pairs={{0,4},{1,5},{2,6},{3,7},{4,0},{5,1},{6,2},{7,3},{8,12},{9,13},{10,... | collective-permute-start | bytes 884744 | tf_op jit(solution)/shard_map/ppermute | solution.py:324
  55.1 12.1 %collective-permute-start.12 = (f32[576,128]{1,0:T(8,128)S(1)}, f32[576,128]{1,0:T(8,128)S(1)}, u32[]{:S(2)}, u32[]{:S(2)}) collective-permute-start(f32[576,128]{1,0:T(8,128)S(1)} %pad_maximum_fusion), channel_id=1, source_target_pairs={{0,6},{1,7},{2,4},{3,5},{4,2},{5,3},{6,0},{7,1},{8,14},{9,15},{10,... | collective-permute-start | bytes 884744 | tf_op jit(solution)/shard_map/ppermute | solution.py:324
  67.3 2.9 %copy-start = (f32[2304,128]{1,0:T(8,128)}, f32[2304,128]{1,0:T(8,128)S(1)}, u32[]{:S(2)}) copy-start(f32[2304,128]{1,0:T(8,128)S(1)} %constant_dynamic-update-slice_fusion.own_ref) | copy-start | bytes 3538948
  67.3 2.9 %collective-permute-start.13 = (f32[2304,128]{1,0:T(8,128)S(1)}, f32[2304,128]{1,0:T(8,128)S(1)}, u32[]{:S(2)}, u32[]{:S(2)}) collective-permute-start(f32[2304,128]{1,0:T(8,128)S(1)} %constant_dynamic-update-slice_fusion.own_ref), channel_id=1, source_target_pairs={{0,1},{1,0},{2,3},{3,2},{4,5},{5,4},{6,7},{7,6},{8,9},{9,8},{10,11... | collective-permute-start | bytes 3538952 | tf_op jit(solution)/shard_map/ppermute | solution.py:324
  70.2 1.0 %copy-start.1 = (f32[2304,128]{1,0:T(8,128)}, f32[2304,128]{1,0:T(8,128)S(1)}, u32[]{:S(2)}) copy-start(f32[2304,128]{1,0:T(8,128)S(1)} %collective-permute-done.13.far_ref) | copy-start | bytes 3538948

commit v5 on v4

--- a/solution.py
+++ b/solution.py
@@ -10,7 +10,10 @@
 F32 = jnp.float32
 BF16 = jnp.bfloat16
 NB = 128
-VMEM = pltpu.CompilerParams(vmem_limit_bytes=56 * 2**20)
+
+
+def vmem(mib):
+    return pltpu.CompilerParams(vmem_limit_bytes=mib * 2**20)
 
 
 def split(x):
@@ -32,82 +35,115 @@
     return lax.dot_general(a, b, (((0,), (0,)), ((), ())), preferred_element_type=F32)
 
 
-def gram_kernel(step_rows, sent, count_ref, rows_ref, vals_ref, prior_ref, pinfo_ref, keep_ref, send_ref, acc, info):
-    t = pl.program_id(0)
-    width = rows_ref.shape[1]
+def row_cuts(cap):
+    cuts = [0, cap // 8, 3 * cap // 8, 5 * cap // 8, cap]
+    return list(zip(cuts[:-1], cuts[1:])) if cap % 128 == 0 else [(0, cap)]
+
+
+def gram_kernel(sent, count_ref, rows_ref, vals_ref, prior_ref, pinfo_ref, keep_ref, send_ref, x, stage, acc, info, sem, out_sem):
+    cap, width = rows_ref.shape
     nb = width // NB
-    live = count_ref[0] - t * step_rows
+    half = sent // 2
+    total = nb * (nb + 1) // 2 * NB
     tile = min(2 * NB, width)
-    tiles = [(i, i + tile, i, width) for i in range(0, width, tile)]
-
-    @pl.when(t == 0)
-    def _():
-        p = prior_ref[...]
-        hi = p.astype(BF16)
-        rest = p - hi.astype(F32)
-        mid = rest.astype(BF16)
-        lo = (rest - mid.astype(F32)).astype(BF16)
-        left = jnp.concatenate([hi, hi, mid, mid, hi, lo], axis=0)
-        right = jnp.concatenate([hi, mid, hi, mid, lo, hi], axis=0)
-        for i0, i1, j0, j1 in tiles:
-            acc[i0:i1, j0:j1] = dot_t(left[:, i0:i1], right[:, j0:j1])
-        info[...] = jnp.broadcast_to(
-            jnp.dot(pinfo_ref[...], p, precision=lax.Precision.HIGHEST, preferred_element_type=F32), info.shape
+    tiles = [(i, i + tile) for i in range(0, width, tile)]
+    parts = row_cuts(cap)
+    copies = [
+        pltpu.make_async_copy(rows_ref.at[pl.ds(lo, hi - lo), :], x.at[pl.ds(lo, hi - lo), :], sem.at[n])
+        for n, (lo, hi) in enumerate(parts)
+    ]
+    for copy in copies:
+        copy.start()
+
+    p = prior_ref[...]
+    hi = p.astype(BF16)
+    rest = p - hi.astype(F32)
+    mid = rest.astype(BF16)
+    lo = (rest - mid.astype(F32)).astype(BF16)
+    left = jnp.concatenate([hi, hi, mid, mid, hi, lo], axis=0)
+    right = jnp.concatenate([hi, mid, hi, mid, lo, hi], axis=0)
+    for i, j in tiles:
+        acc[i:j, i:] = dot_t(left[:, i:j], right[:, i:])
+    info[...] = jnp.broadcast_to(
+        jnp.dot(pinfo_ref[...], p, precision=lax.Precision.HIGHEST, preferred_element_type=F32), info.shape
+    )
+    for row in range(total, sent, NB):
+        stage[row : row + NB, :] = jnp.zeros((NB, NB), F32)
+
+    place = block_at(width)
+    ends = [place[j // NB, j // NB] * NB if j < width else sent for _, j in tiles]
+    cuts = sorted({0, half, *ends})
+    pieces = list(zip(cuts[:-1], cuts[1:]))
+    side = lax.axis_index("blk") % 2
+
+    def out_copy(n, at_side):
+        lo, hi = pieces[n]
+        to = keep_ref if lo // half == at_side else send_ref
+        return pltpu.make_async_copy(
+            stage.at[pl.ds(lo, hi - lo), :], to.at[pl.ds(lo % half, hi - lo), :], out_sem.at[n]
         )
 
-    @pl.when(live > 0)
-    def _():
-        place = lax.broadcasted_iota(jnp.int32, (step_rows, 1), 0)
-        x = jnp.where(place < live, rows_ref[...], jnp.zeros((), BF16))
-        for i0, i1, j0, j1 in tiles:
-            acc[i0:i1, j0:j1] += dot_t(x[:, i0:i1], x[:, j0:j1])
-        v = vals_ref[pl.ds(pl.multiple_of(t * step_rows, step_rows), step_rows)].astype(F32).reshape(1, step_rows)
-        v = jnp.broadcast_to(v, (8, step_rows)).astype(BF16)
-        info[...] += jnp.dot(v, x, preferred_element_type=F32)
-
-    @pl.when(t == pl.num_programs(0) - 1)
-    def _():
-        half = sent // 2
-        side = lax.axis_index("blk") % 2
-
-        def pack(pair):
-            for (i, j), n in block_at(width).items():
-                out, off = pair[n * NB // half], n * NB % half
-                out[off : off + NB, :] = acc[i * NB : (i + 1) * NB, j * NB : (j + 1) * NB]
-            for row in range(nb * (nb + 1) // 2 * NB, sent, NB):
-                pair[row // half][row % half : row % half + NB, :] = jnp.zeros((NB, NB), F32)
-            hw = NB // 2
-            for b in range(2 * nb):
-                pair[0][hw + b : hw + b + 1, 0:hw] = info[0:1, b * hw : (b + 1) * hw]
-
-        @pl.when(side == 0)
+    def on_each_side(do):
+        for at_side in range(2):
+            pl.when(side == at_side)(functools.partial(do, at_side))
+
+    sent_out = 0
+    for n, (lo, hi) in enumerate(parts):
+        copies[n].wait()
+        live = count_ref[0] - lo
+
+        @pl.when(live < hi - lo)
         def _():
-            pack((keep_ref, send_ref))
-
-        @pl.when(side != 0)
-        def _():
-            pack((send_ref, keep_ref))
+            row = lax.broadcasted_iota(jnp.int32, (hi - lo, 1), 0)
+            x[lo:hi, :] = jnp.where(row < live, x[lo:hi, :], jnp.zeros((), BF16))
+
+        v = vals_ref[lo:hi].astype(F32).reshape(1, hi - lo)
+        v = jnp.broadcast_to(v, (16, hi - lo)).astype(BF16)
+        for (i, j), end in zip(tiles, ends):
+            if i == 0:
+                left = jnp.concatenate([x[lo:hi, i:j].T, v], axis=0)
+                both = jnp.dot(left, x[lo:hi, :], preferred_element_type=F32)
+                term = acc[i:j, i:] + both[0 : j - i, :]
+                info[...] += both[j - i : j - i + 8, :]
+            else:
+                term = acc[i:j, i:] + dot_t(x[lo:hi, i:j], x[lo:hi, i:])
+            if n + 1 < len(parts):
+                acc[i:j, i:] = term
+                continue
+            for bi in range(i // NB, j // NB):
+                for bj in range(bi, nb):
+                    at = place[bi, bj] * NB
+                    stage[at : at + NB, :] = term[bi * NB - i : bi * NB - i + NB, bj * NB - i : bj * NB - i + NB]
+            if i == 0:
+                hw = NB // 2
+                for b in range(2 * nb):
+                    stage[hw + b : hw + b + 1, 0:hw] = info[0:1, b * hw : (b + 1) * hw]
+            done = [m for m, (_, stop) in enumerate(pieces) if stop <= end and m >= sent_out]
+            on_each_side(lambda at_side, done=done: [out_copy(m, at_side).start() for m in done] and None)
+            sent_out += len(done)
+    on_each_side(lambda at_side: [out_copy(m, at_side).wait() for m in range(len(pieces))] and None)
 
 
 def gram(readings, values, counts, prior_root, prior_info, sent):
     cap, width = readings.shape
-    step_rows = min(1024, cap)
     whole = pl.BlockSpec(memory_space=pltpu.VMEM)
+    left_there = pl.BlockSpec(memory_space=pl.ANY)
+    in_hbm = pl.BlockSpec(memory_space=pltpu.HBM)
+    n_parts = len(row_cuts(cap))
     return pl.pallas_call(
-        functools.partial(gram_kernel, step_rows, sent),
-        grid=(cap // step_rows,),
-        in_specs=[
-            pl.BlockSpec(memory_space=pltpu.SMEM),
-            pl.BlockSpec((step_rows, width), lambda t: (t, 0)),
-            whole,
-            whole,
-            whole,
+        functools.partial(gram_kernel, sent),
+        in_specs=[pl.BlockSpec(memory_space=pltpu.SMEM), in_hbm, whole, whole, whole],
+        out_specs=[left_there] * 2,
+        out_shape=[jax.ShapeDtypeStruct((sent // 2, NB), F32)] * 2,
+        scratch_shapes=[
+            pltpu.VMEM((cap, width), BF16),
+            pltpu.VMEM((sent, NB), F32),
+            pltpu.VMEM((width, width), F32),
+            pltpu.VMEM((8, width), F32),
+            pltpu.SemaphoreType.DMA((n_parts,)),
+            pltpu.SemaphoreType.DMA((width // NB,)),
         ],
-        out_specs=[whole] * 2,
-        out_shape=[jax.ShapeDtypeStruct((sent // 2, NB), F32)] * 2,
-        scratch_shapes=[pltpu.VMEM((width, width), F32), pltpu.VMEM((8, width), F32)],
-        compiler_params=VMEM,
-        cost_estimate=pl.CostEstimate(flops=2 * cap * width * width, bytes_accessed=2 * cap * width, transcendentals=0),
+        compiler_params=vmem(60),
         name="gram",
     )(counts, readings, values, prior_root, prior_info.reshape(1, -1))
 
@@ -216,9 +252,6 @@
     lane = lax.broadcasted_iota(jnp.int32, (hw, NB), 1)
     s[0:hw, 0:NB] = corner[0:hw, :]
     s[hw:NB, 0:NB] = jnp.where(lane < hw, mirror[hw:, :], corner[hw:, :])
-    for b in range(1, nb):
-        s[0:NB, span(b)] = block(0, b)
-
     def inverse(i):
         return split(minv[span(i), :])
 
@@ -230,14 +263,15 @@
         uh, ul = split(u)
         uhi[span(i), c] = uh
         ulo[span(i), c] = ul
-        for b in range(c.start // NB, c.stop // NB):
-            t = u[:, b * NB - c.start : b * NB - c.start + NB].T
-            th, tl = split(t)
-            thi[span(b), span(i)] = th
-            tlo[span(b), span(i)] = tl
-
-    def reduce(i, c):
-        up = slice(0, i * NB)
+        return uh, ul
+
+    def turn(i, b):
+        th, tl = split(r[span(i), span(b)].T)
+        thi[span(b), span(i)] = th
+        tlo[span(b), span(i)] = tl
+
+    def reduce(i, c, rows):
+        up = slice(0, rows * NB)
         off = jnp.dot(
             three(thi[span(i), up], tlo[span(i), up], 1),
             three_other(uhi[up, c], ulo[up, c], 0),
@@ -251,9 +285,16 @@
         for c in cuts:
             solve(i, c)
             yield
+        if i + 2 < nb:
+            turn(i, i + 1)
+            turn(i, i + 2)
+            reduce(i + 2, span(i + 2), i + 1)
+            yield
         for c in cuts:
-            reduce(i + 1, c)
+            reduce(i + 1, c, i + 1)
             yield
+        for b in range(i + 3, nb):
+            turn(i, b)
         mh, ml = inverse(i)
         bh, bl = split(y[:, span(i)])
         yi = lax.dot_general(
@@ -286,9 +327,14 @@
         factor_block(read, write, other_work)
         for _ in other_work:
             pass
+        if i == 0:
+            for b in range(1, nb):
+                s[span(0), span(b)] = block(0, b)
         if i + 1 < nb:
-            solve(i, span(i + 1))
-            reduce(i + 1, span(i + 1))
+            uh, ul = solve(i, span(i + 1))
+            at = slice((i + 1) * NB, (i + 2) * NB)
+            have = s[at, at] if i else block(1, 1)
+            s[at, at] = have - dot_t(three(uh, ul, 0), three_other(uh, ul, 0))
         other_work = rest_of(i)
     for _ in other_work:
         pass
@@ -314,7 +360,7 @@
         ]
         + [pltpu.VMEM((width, width), BF16)] * 4
         + [pltpu.VMEM((8, width), F32)],
-        compiler_params=VMEM,
+        compiler_params=vmem(28),
         name="factor",
     )(own, far)
 

time: 99.6 us -> 97.1 us (0.975)
  starting transfers between devices: 21.3 us -> 18 us
  waiting for transfers between devices: 38.1 us -> 40.3 us
  local copies, waits for them, and re-layouts: 1.08 us -> 0.08 us
    ppermute x14, starting transfers between devices: 21.3 us -> 18 us  [swap(): return lax.ppermute(x, axis, [(d, d ^ mask) for d in range(n)])]
    ppermute x14, waiting for transfers between devices: 38.1 us -> 40.3 us  [swap(): return lax.ppermute(x, axis, [(d, d ^ mask) for d in range(n)])]
    pallas_call x1, Pallas kernels: 7.86 us -> 9.66 us  [gram(): pl.pallas_call(functools.partial(gram_kernel, sent), in_specs=[pl.BlockSp...]
    pallas_call x1, Pallas kernels: 27.9 us -> 26.1 us  [factor(): pl.pallas_call(functools.partial(factor_kernel, n_quarter, n_layer), in_s...]
    unnamed x9 -> x5, local copies, waits for them, and re-layouts: 1.06 us -> 0.06 us
  transfers between devices with their start and end apart: 14 -> 14, of which waited for: 13 -> 12; matrix products, arithmetic and copies ran while one was open for 0% -> 0% of each run, Pallas kernels for 0% -> 0%
where the time goes in v5:
time: 97.1 us; the launch traced here: 96.9 us
  waiting for transfers between devices  40.3 us (42%)
  Pallas kernels  35.7 us (37%)
  starting transfers between devices  18 us (19%)
  other arithmetic  1.47 us (2%)
  between operations  1.35 us (1%)
    ppermute x14, waiting for transfers between devices, swap(): return lax.ppermute(x, axis, [(d, d ^ mask) for d in range(n)])  40.3 us
    pallas_call x1, Pallas kernels, factor(): pl.pallas_call(functools.partial(factor_kernel, n_quarter, n_layer), in_s...  26.1 us
    ppermute x14, starting transfers between devices, swap(): return lax.ppermute(x, axis, [(d, d ^ mask) for d in range(n)])  18 us
    pallas_call x1, Pallas kernels, gram(): pl.pallas_call(functools.partial(gram_kernel, sent), in_specs=[pl.BlockSp...  9.66 us
  transfers between devices with their start and end apart: 14, of which 12 were waited for; matrix products, arithmetic and copies ran while one was open for 0% of the time, Pallas kernels for 0%

profile of v5, /device:TPU:0, one launch (start us, length us, event | category | flops | bytes accessed | tf_op | source)
XLA Modules:
  0.0 96.9 jit_solution(17446070522758000146)
XLA Ops:
  1.3 9.7 %gram.1 = (f32[2304,128]{1,0:T(8,128)}, f32[2304,128]{1,0:T(8,128)}) custom-call(s32[1]{0:T(128)S(6)} %copy.13.count_ref, bf16[4096,1024]{1,0:T(8,128)(2,1)} %rows_ref.1, bf16[4096]{0:T(1024)(128)(2,1)} %vals_ref.1, f32[32,1024]{1,0:T(8,128)} %prior_ref.1, f32[1,32]{1,0:T(1,128)} %bitcast.2), custom_call_target="tpu_custom_call" | custom-call | tf_op jit(solution)/shard_map/gram/pallas_call | solution.py:133
  10.9 0.8 collective-permute-start
  11.8 2.7 %collective-permute-done = f32[2304,128]{1,0:T(8,128)S(1)} collective-permute-done((f32[2304,128]{1,0:T(8,128)}, f32[2304,128]{1,0:T(8,128)S(1)}, u32[]{:S(2)}, u32[]{:S(2)}) %collective-permute-start) | collective-permute-done | bytes 1179680 | tf_op jit(solution)/shard_map/ppermute | solution.py:370
  14.4 1.3 %dynamic-slice_add_fusion.3 = (f32[576,128]{1,0:T(8,128)S(1)}, f32[576,128]{1,0:T(8,128)S(1)}, f32[576,128]{1,0:T(8,128)S(1)}, f32[576,128]{1,0:T(8,128)S(1)}) fusion(f32[2304,128]{1,0:T(8,128)S(1)} %collective-permute-done, s32[]{:T(128)S(6)} %select_n.22, f32[2304,128]{1,0:T(8,128)} %get-tuple-element.6, s32[]{:T(128)S(6)} %select_n.50, s32[]{:T(128)S(6)} %select_n.25, ...), kind=kLoop, calls=%fused_computation.4 | loop fusion | flops 294912 | bytes 3538960 | tf_op jit(solution)/shard_map/add | solution.py:376
  15.8 4.0 %collective-permute-start.3 = (f32[576,128]{1,0:T(8,128)S(1)}, f32[576,128]{1,0:T(8,128)S(1)}, u32[]{:S(2)}, u32[]{:S(2)}) collective-permute-start(f32[576,128]{1,0:T(8,128)S(1)} %get-tuple-element.13), channel_id=1, source_target_pairs={{0,6},{1,7},{2,4},{3,5},{4,2},{5,3},{6,0},{7,1},{8,14},{9,15},{10,... | collective-permute-start | bytes 884744 | tf_op jit(solution)/shard_map/ppermute | solution.py:370
  19.8 0.3 collective-permute-start.2
  20.1 0.3 collective-permute-start.1
  20.4 7.2 %collective-permute-done.3 = f32[576,128]{1,0:T(8,128)S(1)} collective-permute-done((f32[576,128]{1,0:T(8,128)S(1)}, f32[576,128]{1,0:T(8,128)S(1)}, u32[]{:S(2)}, u32[]{:S(2)}) %collective-permute-start.3) | collective-permute-done | bytes 294944 | tf_op jit(solution)/shard_map/ppermute | solution.py:370
  27.6 5.8 %collective-permute-done.2 = f32[576,128]{1,0:T(8,128)S(1)} collective-permute-done((f32[576,128]{1,0:T(8,128)S(1)}, f32[576,128]{1,0:T(8,128)S(1)}, u32[]{:S(2)}, u32[]{:S(2)}) %collective-permute-start.2) | collective-permute-done | bytes 294944 | tf_op jit(solution)/shard_map/ppermute | solution.py:370
  33.4 0.3 collective-permute-done.1
  33.7 0.1 dynamic-slice_add_fusion.6
  33.8 3.8 %collective-permute-start.6 = (f32[144,128]{1,0:T(8,128)S(1)}, f32[144,128]{1,0:T(8,128)S(1)}, u32[]{:S(2)}, u32[]{:S(2)}) collective-permute-start(f32[144,128]{1,0:T(8,128)S(1)} %get-tuple-element.17), channel_id=1, source_target_pairs={{0,24},{8,16},{16,8},{24,0},{1,25},{9,17},{17,9},{25,1},{2,26},{10... | collective-permute-start | bytes 221192 | tf_op jit(solution)/shard_map/ppermute | solution.py:370
  37.6 0.0 collective-permute-start.5
  37.6 0.6 collective-permute-start.4
  38.3 2.4 %collective-permute-done.6 = f32[144,128]{1,0:T(8,128)S(1)} collective-permute-done((f32[144,128]{1,0:T(8,128)S(1)}, f32[144,128]{1,0:T(8,128)S(1)}, u32[]{:S(2)}, u32[]{:S(2)}) %collective-permute-start.6) | collective-permute-done | bytes 73760 | tf_op jit(solution)/shard_map/ppermute | solution.py:370
  40.7 3.1 %collective-permute-done.5 = f32[144,128]{1,0:T(8,128)S(1)} collective-permute-done((f32[144,128]{1,0:T(8,128)S(1)}, f32[144,128]{1,0:T(8,128)S(1)}, u32[]{:S(2)}, u32[]{:S(2)}) %collective-permute-start.5) | collective-permute-done | bytes 73760 | tf_op jit(solution)/shard_map/ppermute | solution.py:370
  43.7 0.0 collective-permute-done.4
  43.8 1.1 %collective-permute-start.7 = (f32[144,128]{1,0:T(8,128)S(1)}, f32[144,128]{1,0:T(8,128)S(1)}, u32[]{:S(2)}, u32[]{:S(2)}) collective-permute-start(f32[144,128]{1,0:T(8,128)S(1)} %get-tuple-element.11), channel_id=1, source_target_pairs={{0,8},{8,0},{16,24},{24,16},{1,9},{9,1},{17,25},{25,17},{2,10},{10... | collective-permute-start | bytes 221192 | tf_op jit(solution)/shard_map/ppermute | solution.py:370
  44.8 2.2 %collective-permute-start.8 = (f32[144,128]{1,0:T(8,128)S(1)}, f32[144,128]{1,0:T(8,128)S(1)}, u32[]{:S(2)}, u32[]{:S(2)}) collective-permute-start(f32[144,128]{1,0:T(8,128)S(1)} %get-tuple-element.11), channel_id=1, source_target_pairs={{0,16},{8,24},{16,0},{24,8},{1,17},{9,25},{17,1},{25,9},{2,18},{10... | collective-permute-start | bytes 221192 | tf_op jit(solution)/shard_map/ppermute | solution.py:370
  47.0 1.2 %collective-permute-start.9 = (f32[144,128]{1,0:T(8,128)S(1)}, f32[144,128]{1,0:T(8,128)S(1)}, u32[]{:S(2)}, u32[]{:S(2)}) collective-permute-start(f32[144,128]{1,0:T(8,128)S(1)} %get-tuple-element.11), channel_id=1, source_target_pairs={{0,24},{8,16},{16,8},{24,0},{1,25},{9,17},{17,9},{25,1},{2,26},{10... | collective-permute-start | bytes 221192 | tf_op jit(solution)/shard_map/ppermute | solution.py:370
  48.2 0.4 collective-permute-done.7
  48.6 3.3 %collective-permute-done.8 = f32[144,128]{1,0:T(8,128)S(1)} collective-permute-done((f32[144,128]{1,0:T(8,128)S(1)}, f32[144,128]{1,0:T(8,128)S(1)}, u32[]{:S(2)}, u32[]{:S(2)}) %collective-permute-start.8) | collective-permute-done | bytes 73760 | tf_op jit(solution)/shard_map/ppermute | solution.py:370
  51.9 1.4 %collective-permute-done.9 = f32[144,128]{1,0:T(8,128)S(1)} collective-permute-done((f32[144,128]{1,0:T(8,128)S(1)}, f32[144,128]{1,0:T(8,128)S(1)}, u32[]{:S(2)}, u32[]{:S(2)}) %collective-permute-start.9) | collective-permute-done | bytes 73760 | tf_op jit(solution)/shard_map/ppermute | solution.py:370
  53.3 1.6 %collective-permute-start.10 = (f32[576,128]{1,0:T(8,128)S(1)}, f32[576,128]{1,0:T(8,128)S(1)}, u32[]{:S(2)}, u32[]{:S(2)}) collective-permute-start(f32[576,128]{1,0:T(8,128)S(1)} %pad_maximum_fusion), channel_id=1, source_target_pairs={{0,2},{1,3},{2,0},{3,1},{4,6},{5,7},{6,4},{7,5},{8,10},{9,11},{10,... | collective-permute-start | bytes 884744 | tf_op jit(solution)/shard_map/ppermute | solution.py:370
  54.9 0.1 collective-permute-start.11
  55.0 1.9 %collective-permute-start.12 = (f32[576,128]{1,0:T(8,128)S(1)}, f32[576,128]{1,0:T(8,128)S(1)}, u32[]{:S(2)}, u32[]{:S(2)}) collective-permute-start(f32[576,128]{1,0:T(8,128)S(1)} %pad_maximum_fusion), channel_id=1, source_target_pairs={{0,6},{1,7},{2,4},{3,5},{4,2},{5,3},{6,0},{7,1},{8,14},{9,15},{10,... | collective-permute-start | bytes 884744 | tf_op jit(solution)/shard_map/ppermute | solution.py:370
  56.9 6.4 %collective-permute-done.10 = f32[576,128]{1,0:T(8,128)S(1)} collective-permute-done((f32[576,128]{1,0:T(8,128)S(1)}, f32[576,128]{1,0:T(8,128)S(1)}, u32[]{:S(2)}, u32[]{:S(2)}) %collective-permute-start.10) | collective-permute-done | bytes 294944 | tf_op jit(solution)/shard_map/ppermute | solution.py:370
  63.3 4.6 %collective-permute-done.11 = f32[576,128]{1,0:T(8,128)S(1)} collective-permute-done((f32[576,128]{1,0:T(8,128)S(1)}, f32[576,128]{1,0:T(8,128)S(1)}, u32[]{:S(2)}, u32[]{:S(2)}) %collective-permute-start.11) | collective-permute-done | bytes 294944 | tf_op jit(solution)/shard_map/ppermute | solution.py:370
  67.9 0.0 collective-permute-done.12
  67.9 0.1 collective-permute-start.13
  68.0 2.8 %collective-permute-done.13.far_ref = f32[2304,128]{1,0:T(8,128)S(1)} collective-permute-done((f32[2304,128]{1,0:T(8,128)S(1)}, f32[2304,128]{1,0:T(8,128)S(1)}, u32[]{:S(2)}, u32[]{:S(2)}) %collective-permute-start.13) | collective-permute-done | bytes 1179680 | tf_op jit(solution)/shard_map/ppermute | solution.py:370
  70.9 26.1 %factor.1 = (f32[128,1024]{1,0:T(8,128)}, f32[8,128]{1,0:T(8,128)}) custom-call(f32[2304,128]{1,0:T(8,128)S(1)} %constant_dynamic-update-slice_fusion.own_ref, f32[2304,128]{1,0:T(8,128)S(1)} %collective-permute-done.13.far_ref), custom_call_target="tpu_custom_call" | custom-call | tf_op jit(solution)/shard_map/factor/pallas_call | solution.py:350
  (8 shorter events, 0.1 us)
Async XLA Ops:
  10.9 3.5 %collective-permute-start = (f32[2304,128]{1,0:T(8,128)}, f32[2304,128]{1,0:T(8,128)S(1)}, u32[]{:S(2)}, u32[]{:S(2)}) collective-permute-start(f32[2304,128]{1,0:T(8,128)} %get-tuple-element.7), channel_id=1, source_target_pairs={{0,1},{1,0},{2,3},{3,2},{4,5},{5,4},{6,7},{7,6},{8,9},{9,8},{10,11... | collective-permute-start | bytes 3538952 | tf_op jit(solution)/shard_map/ppermute | solution.py:370
  15.8 11.8 %collective-permute-start.3 = (f32[576,128]{1,0:T(8,128)S(1)}, f32[576,128]{1,0:T(8,128)S(1)}, u32[]{:S(2)}, u32[]{:S(2)}) collective-permute-start(f32[576,128]{1,0:T(8,128)S(1)} %get-tuple-element.13), channel_id=1, source_target_pairs={{0,6},{1,7},{2,4},{3,5},{4,2},{5,3},{6,0},{7,1},{8,14},{9,15},{10,... | collective-permute-start | bytes 884744 | tf_op jit(solution)/shard_map/ppermute | solution.py:370
  19.8 13.6 %collective-permute-start.2 = (f32[576,128]{1,0:T(8,128)S(1)}, f32[576,128]{1,0:T(8,128)S(1)}, u32[]{:S(2)}, u32[]{:S(2)}) collective-permute-start(f32[576,128]{1,0:T(8,128)S(1)} %get-tuple-element.14), channel_id=1, source_target_pairs={{0,4},{1,5},{2,6},{3,7},{4,0},{5,1},{6,2},{7,3},{8,12},{9,13},{10,... | collective-permute-start | bytes 884744 | tf_op jit(solution)/shard_map/ppermute | solution.py:370
  20.1 13.6 %collective-permute-start.1 = (f32[576,128]{1,0:T(8,128)S(1)}, f32[576,128]{1,0:T(8,128)S(1)}, u32[]{:S(2)}, u32[]{:S(2)}) collective-permute-start(f32[576,128]{1,0:T(8,128)S(1)} %get-tuple-element.15), channel_id=1, source_target_pairs={{0,2},{1,3},{2,0},{3,1},{4,6},{5,7},{6,4},{7,5},{8,10},{9,11},{10,... | collective-permute-start | bytes 884744 | tf_op jit(solution)/shard_map/ppermute | solution.py:370
  33.8 6.9 %collective-permute-start.6 = (f32[144,128]{1,0:T(8,128)S(1)}, f32[144,128]{1,0:T(8,128)S(1)}, u32[]{:S(2)}, u32[]{:S(2)}) collective-permute-start(f32[144,128]{1,0:T(8,128)S(1)} %get-tuple-element.17), channel_id=1, source_target_pairs={{0,24},{8,16},{16,8},{24,0},{1,25},{9,17},{17,9},{25,1},{2,26},{10... | collective-permute-start | bytes 221192 | tf_op jit(solution)/shard_map/ppermute | solution.py:370
  37.6 6.1 %collective-permute-start.5 = (f32[144,128]{1,0:T(8,128)S(1)}, f32[144,128]{1,0:T(8,128)S(1)}, u32[]{:S(2)}, u32[]{:S(2)}) collective-permute-start(f32[144,128]{1,0:T(8,128)S(1)} %get-tuple-element.18), channel_id=1, source_target_pairs={{0,16},{8,24},{16,0},{24,8},{1,17},{9,25},{17,1},{25,9},{2,18},{10... | collective-permute-start | bytes 221192 | tf_op jit(solution)/shard_map/ppermute | solution.py:370
  37.6 6.1 %collective-permute-start.4 = (f32[144,128]{1,0:T(8,128)S(1)}, f32[144,128]{1,0:T(8,128)S(1)}, u32[]{:S(2)}, u32[]{:S(2)}) collective-permute-start(f32[144,128]{1,0:T(8,128)S(1)} %get-tuple-element.16), channel_id=1, source_target_pairs={{0,8},{8,0},{16,24},{24,16},{1,9},{9,1},{17,25},{25,17},{2,10},{10... | collective-permute-start | bytes 221192 | tf_op jit(solution)/shard_map/ppermute | solution.py:370
  43.8 4.8 %collective-permute-start.7 = (f32[144,128]{1,0:T(8,128)S(1)}, f32[144,128]{1,0:T(8,128)S(1)}, u32[]{:S(2)}, u32[]{:S(2)}) collective-permute-start(f32[144,128]{1,0:T(8,128)S(1)} %get-tuple-element.11), channel_id=1, source_target_pairs={{0,8},{8,0},{16,24},{24,16},{1,9},{9,1},{17,25},{25,17},{2,10},{10... | collective-permute-start | bytes 221192 | tf_op jit(solution)/shard_map/ppermute | solution.py:370
  44.8 7.0 %collective-permute-start.8 = (f32[144,128]{1,0:T(8,128)S(1)}, f32[144,128]{1,0:T(8,128)S(1)}, u32[]{:S(2)}, u32[]{:S(2)}) collective-permute-start(f32[144,128]{1,0:T(8,128)S(1)} %get-tuple-element.11), channel_id=1, source_target_pairs={{0,16},{8,24},{16,0},{24,8},{1,17},{9,25},{17,1},{25,9},{2,18},{10... | collective-permute-start | bytes 221192 | tf_op jit(solution)/shard_map/ppermute | solution.py:370
  47.0 6.3 %collective-permute-start.9 = (f32[144,128]{1,0:T(8,128)S(1)}, f32[144,128]{1,0:T(8,128)S(1)}, u32[]{:S(2)}, u32[]{:S(2)}) collective-permute-start(f32[144,128]{1,0:T(8,128)S(1)} %get-tuple-element.11), channel_id=1, source_target_pairs={{0,24},{8,16},{16,8},{24,0},{1,25},{9,17},{17,9},{25,1},{2,26},{10... | collective-permute-start | bytes 221192 | tf_op jit(solution)/shard_map/ppermute | solution.py:370
  53.3 10.0 %collective-permute-start.10 = (f32[576,128]{1,0:T(8,128)S(1)}, f32[576,128]{1,0:T(8,128)S(1)}, u32[]{:S(2)}, u32[]{:S(2)}) collective-permute-start(f32[576,128]{1,0:T(8,128)S(1)} %pad_maximum_fusion), channel_id=1, source_target_pairs={{0,2},{1,3},{2,0},{3,1},{4,6},{5,7},{6,4},{7,5},{8,10},{9,11},{10,... | collective-permute-start | bytes 884744 | tf_op jit(solution)/shard_map/ppermute | solution.py:370
  54.9 13.0 %collective-permute-start.11 = (f32[576,128]{1,0:T(8,128)S(1)}, f32[576,128]{1,0:T(8,128)S(1)}, u32[]{:S(2)}, u32[]{:S(2)}) collective-permute-start(f32[576,128]{1,0:T(8,128)S(1)} %pad_maximum_fusion), channel_id=1, source_target_pairs={{0,4},{1,5},{2,6},{3,7},{4,0},{5,1},{6,2},{7,3},{8,12},{9,13},{10,... | collective-permute-start | bytes 884744 | tf_op jit(solution)/shard_map/ppermute | solution.py:370
  55.0 12.9 %collective-permute-start.12 = (f32[576,128]{1,0:T(8,128)S(1)}, f32[576,128]{1,0:T(8,128)S(1)}, u32[]{:S(2)}, u32[]{:S(2)}) collective-permute-start(f32[576,128]{1,0:T(8,128)S(1)} %pad_maximum_fusion), channel_id=1, source_target_pairs={{0,6},{1,7},{2,4},{3,5},{4,2},{5,3},{6,0},{7,1},{8,14},{9,15},{10,... | collective-permute-start | bytes 884744 | tf_op jit(solution)/shard_map/ppermute | solution.py:370
  67.9 2.9 %collective-permute-start.13 = (f32[2304,128]{1,0:T(8,128)S(1)}, f32[2304,128]{1,0:T(8,128)S(1)}, u32[]{:S(2)}, u32[]{:S(2)}) collective-permute-start(f32[2304,128]{1,0:T(8,128)S(1)} %constant_dynamic-update-slice_fusion.own_ref), channel_id=1, source_target_pairs={{0,1},{1,0},{2,3},{3,2},{4,5},{5,4},{6,7},{7,6},{8,9},{9,8},{10,11... | collective-permute-start | bytes 3538952 | tf_op jit(solution)/shard_map/ppermute | solution.py:370

commit v6 on v5

--- a/solution.py
+++ b/solution.py
@@ -40,7 +40,7 @@
     return list(zip(cuts[:-1], cuts[1:])) if cap % 128 == 0 else [(0, cap)]
 
 
-def gram_kernel(sent, count_ref, rows_ref, vals_ref, prior_ref, pinfo_ref, keep_ref, send_ref, x, stage, acc, info, sem, out_sem):
+def gram_kernel(sent, count_ref, rows_ref, vals_ref, prior_ref, pinfo_ref, keep_ref, send_ref, x, stage, acc, info, sem):
     cap, width = rows_ref.shape
     nb = width // NB
     half = sent // 2
@@ -71,23 +71,12 @@
         stage[row : row + NB, :] = jnp.zeros((NB, NB), F32)
 
     place = block_at(width)
-    ends = [place[j // NB, j // NB] * NB if j < width else sent for _, j in tiles]
-    cuts = sorted({0, half, *ends})
-    pieces = list(zip(cuts[:-1], cuts[1:]))
     side = lax.axis_index("blk") % 2
-
-    def out_copy(n, at_side):
-        lo, hi = pieces[n]
-        to = keep_ref if lo // half == at_side else send_ref
-        return pltpu.make_async_copy(
-            stage.at[pl.ds(lo, hi - lo), :], to.at[pl.ds(lo % half, hi - lo), :], out_sem.at[n]
-        )
 
     def on_each_side(do):
         for at_side in range(2):
             pl.when(side == at_side)(functools.partial(do, at_side))
 
-    sent_out = 0
     for n, (lo, hi) in enumerate(parts):
         copies[n].wait()
         live = count_ref[0] - lo
@@ -99,7 +88,7 @@
 
         v = vals_ref[lo:hi].astype(F32).reshape(1, hi - lo)
         v = jnp.broadcast_to(v, (16, hi - lo)).astype(BF16)
-        for (i, j), end in zip(tiles, ends):
+        for i, j in tiles:
             if i == 0:
                 left = jnp.concatenate([x[lo:hi, i:j].T, v], axis=0)
                 both = jnp.dot(left, x[lo:hi, :], preferred_element_type=F32)
@@ -118,10 +107,13 @@
                 hw = NB // 2
                 for b in range(2 * nb):
                     stage[hw + b : hw + b + 1, 0:hw] = info[0:1, b * hw : (b + 1) * hw]
-            done = [m for m, (_, stop) in enumerate(pieces) if stop <= end and m >= sent_out]
-            on_each_side(lambda at_side, done=done: [out_copy(m, at_side).start() for m in done] and None)
-            sent_out += len(done)
-    on_each_side(lambda at_side: [out_copy(m, at_side).wait() for m in range(len(pieces))] and None)
+
+    def give(at_side):
+        halves = (keep_ref, send_ref) if at_side == 0 else (send_ref, keep_ref)
+        for n, ref in enumerate(halves):
+            ref[...] = stage[n * half : (n + 1) * half, :]
+
+    on_each_side(give)
 
 
 def gram(readings, values, counts, prior_root, prior_info, sent):
@@ -133,7 +125,7 @@
     return pl.pallas_call(
         functools.partial(gram_kernel, sent),
         in_specs=[pl.BlockSpec(memory_space=pltpu.SMEM), in_hbm, whole, whole, whole],
-        out_specs=[left_there] * 2,
+        out_specs=[whole] * 2,
         out_shape=[jax.ShapeDtypeStruct((sent // 2, NB), F32)] * 2,
         scratch_shapes=[
             pltpu.VMEM((cap, width), BF16),
@@ -141,11 +133,10 @@
             pltpu.VMEM((width, width), F32),
             pltpu.VMEM((8, width), F32),
             pltpu.SemaphoreType.DMA((n_parts,)),
-            pltpu.SemaphoreType.DMA((width // NB,)),
         ],
-        compiler_params=vmem(60),
+        compiler_params=vmem(24),
         name="gram",
-    )(counts, readings, values, prior_root, prior_info.reshape(1, -1))
+    )(counts, *(pltpu.with_memory_space_constraint(x, pltpu.HBM) for x in (readings, values, prior_root, prior_info.reshape(1, -1))))
 
 
 def lane_of(v, at):

time: 97.1 us -> 94.8 us (0.976)
  other arithmetic: 1.47 us -> 0.24 us
    add x2, other arithmetic: 1.41 us -> 0.18 us  [shares(): a + b]
where the time goes in v6:
time: 94.8 us; the launch traced here: 94.7 us
  waiting for transfers between devices  40 us (42%)
  Pallas kernels  35.2 us (37%)
  starting transfers between devices  17.8 us (19%)
  between operations  1.35 us (1%)
    ppermute x14, waiting for transfers between devices, swap(): return lax.ppermute(x, axis, [(d, d ^ mask) for d in range(n)])  40 us
    pallas_call x1, Pallas kernels, factor(): pl.pallas_call(functools.partial(factor_kernel, n_quarter, n_layer), in_s...  26.1 us
    ppermute x14, starting transfers between devices, swap(): return lax.ppermute(x, axis, [(d, d ^ mask) for d in range(n)])  17.8 us
    pallas_call x1, Pallas kernels, gram(): pl.pallas_call(functools.partial(gram_kernel, sent), in_specs=[pl.BlockSp...  9.16 us
  transfers between devices with their start and end apart: 14, of which 12 were waited for; matrix products, arithmetic and copies ran while one was open for 0% of the time, Pallas kernels for 0%

profile of v6, /device:TPU:0, one launch (start us, length us, event | category | flops | bytes accessed | tf_op | source)
XLA Modules:
  0.0 94.7 jit_solution(11430925847696832399)
XLA Ops:
  1.3 9.2 %gram.1 = (f32[2304,128]{1,0:T(8,128)S(1)}, f32[2304,128]{1,0:T(8,128)S(1)}) custom-call(s32[1]{0:T(128)S(6)} %copy.13.count_ref, bf16[4096,1024]{1,0:T(8,128)(2,1)} %rows_ref.1, bf16[4096]{0:T(1024)(128)(2,1)} %vals_ref.1, f32[32,1024]{1,0:T(8,128)} %prior_ref.1, f32[1,32]{1,0:T(1,128)} %bitcast.2), custom_call_target="tpu_custom_call" | custom-call | tf_op jit(solution)/shard_map/gram/pallas_call | solution.py:125
  10.4 0.5 collective-permute-start
  11.0 2.5 %collective-permute-done = f32[2304,128]{1,0:T(8,128)S(1)} collective-permute-done((f32[2304,128]{1,0:T(8,128)S(1)}, f32[2304,128]{1,0:T(8,128)S(1)}, u32[]{:S(2)}, u32[]{:S(2)}) %collective-permute-start) | collective-permute-done | bytes 1179680 | tf_op jit(solution)/shard_map/ppermute | solution.py:361
  13.4 0.1 dynamic-slice_add_fusion.3
  13.6 3.9 %collective-permute-start.3 = (f32[576,128]{1,0:T(8,128)S(1)}, f32[576,128]{1,0:T(8,128)S(1)}, u32[]{:S(2)}, u32[]{:S(2)}) collective-permute-start(f32[576,128]{1,0:T(8,128)S(1)} %get-tuple-element.13), channel_id=1, source_target_pairs={{0,6},{1,7},{2,4},{3,5},{4,2},{5,3},{6,0},{7,1},{8,14},{9,15},{10,... | collective-permute-start | bytes 884744 | tf_op jit(solution)/shard_map/ppermute | solution.py:361
  17.4 0.8 collective-permute-start.2
  18.3 0.0 collective-permute-start.1
  18.3 7.0 %collective-permute-done.3 = f32[576,128]{1,0:T(8,128)S(1)} collective-permute-done((f32[576,128]{1,0:T(8,128)S(1)}, f32[576,128]{1,0:T(8,128)S(1)}, u32[]{:S(2)}, u32[]{:S(2)}) %collective-permute-start.3) | collective-permute-done | bytes 294944 | tf_op jit(solution)/shard_map/ppermute | solution.py:361
  25.3 5.8 %collective-permute-done.2 = f32[576,128]{1,0:T(8,128)S(1)} collective-permute-done((f32[576,128]{1,0:T(8,128)S(1)}, f32[576,128]{1,0:T(8,128)S(1)}, u32[]{:S(2)}, u32[]{:S(2)}) %collective-permute-start.2) | collective-permute-done | bytes 294944 | tf_op jit(solution)/shard_map/ppermute | solution.py:361
  31.1 0.3 collective-permute-done.1
  31.4 0.1 dynamic-slice_add_fusion.6
  31.4 3.7 %collective-permute-start.6 = (f32[144,128]{1,0:T(8,128)S(1)}, f32[144,128]{1,0:T(8,128)S(1)}, u32[]{:S(2)}, u32[]{:S(2)}) collective-permute-start(f32[144,128]{1,0:T(8,128)S(1)} %get-tuple-element.17), channel_id=1, source_target_pairs={{0,24},{8,16},{16,8},{24,0},{1,25},{9,17},{17,9},{25,1},{2,26},{10... | collective-permute-start | bytes 221192 | tf_op jit(solution)/shard_map/ppermute | solution.py:361
  35.2 0.0 collective-permute-start.5
  35.2 0.7 collective-permute-start.4
  35.9 2.0 %collective-permute-done.6 = f32[144,128]{1,0:T(8,128)S(1)} collective-permute-done((f32[144,128]{1,0:T(8,128)S(1)}, f32[144,128]{1,0:T(8,128)S(1)}, u32[]{:S(2)}, u32[]{:S(2)}) %collective-permute-start.6) | collective-permute-done | bytes 73760 | tf_op jit(solution)/shard_map/ppermute | solution.py:361
  37.9 3.7 %collective-permute-done.5 = f32[144,128]{1,0:T(8,128)S(1)} collective-permute-done((f32[144,128]{1,0:T(8,128)S(1)}, f32[144,128]{1,0:T(8,128)S(1)}, u32[]{:S(2)}, u32[]{:S(2)}) %collective-permute-start.5) | collective-permute-done | bytes 73760 | tf_op jit(solution)/shard_map/ppermute | solution.py:361
  41.6 0.0 collective-permute-done.4
  41.6 1.1 %collective-permute-start.7 = (f32[144,128]{1,0:T(8,128)S(1)}, f32[144,128]{1,0:T(8,128)S(1)}, u32[]{:S(2)}, u32[]{:S(2)}) collective-permute-start(f32[144,128]{1,0:T(8,128)S(1)} %get-tuple-element.11), channel_id=1, source_target_pairs={{0,8},{8,0},{16,24},{24,16},{1,9},{9,1},{17,25},{25,17},{2,10},{10... | collective-permute-start | bytes 221192 | tf_op jit(solution)/shard_map/ppermute | solution.py:361
  42.7 2.3 %collective-permute-start.8 = (f32[144,128]{1,0:T(8,128)S(1)}, f32[144,128]{1,0:T(8,128)S(1)}, u32[]{:S(2)}, u32[]{:S(2)}) collective-permute-start(f32[144,128]{1,0:T(8,128)S(1)} %get-tuple-element.11), channel_id=1, source_target_pairs={{0,16},{8,24},{16,0},{24,8},{1,17},{9,25},{17,1},{25,9},{2,18},{10... | collective-permute-start | bytes 221192 | tf_op jit(solution)/shard_map/ppermute | solution.py:361
  45.0 1.1 %collective-permute-start.9 = (f32[144,128]{1,0:T(8,128)S(1)}, f32[144,128]{1,0:T(8,128)S(1)}, u32[]{:S(2)}, u32[]{:S(2)}) collective-permute-start(f32[144,128]{1,0:T(8,128)S(1)} %get-tuple-element.11), channel_id=1, source_target_pairs={{0,24},{8,16},{16,8},{24,0},{1,25},{9,17},{17,9},{25,1},{2,26},{10... | collective-permute-start | bytes 221192 | tf_op jit(solution)/shard_map/ppermute | solution.py:361
  46.1 0.3 collective-permute-done.7
  46.3 3.2 %collective-permute-done.8 = f32[144,128]{1,0:T(8,128)S(1)} collective-permute-done((f32[144,128]{1,0:T(8,128)S(1)}, f32[144,128]{1,0:T(8,128)S(1)}, u32[]{:S(2)}, u32[]{:S(2)}) %collective-permute-start.8) | collective-permute-done | bytes 73760 | tf_op jit(solution)/shard_map/ppermute | solution.py:361
  49.5 1.6 %collective-permute-done.9 = f32[144,128]{1,0:T(8,128)S(1)} collective-permute-done((f32[144,128]{1,0:T(8,128)S(1)}, f32[144,128]{1,0:T(8,128)S(1)}, u32[]{:S(2)}, u32[]{:S(2)}) %collective-permute-start.9) | collective-permute-done | bytes 73760 | tf_op jit(solution)/shard_map/ppermute | solution.py:361
  51.1 1.4 %collective-permute-start.10 = (f32[576,128]{1,0:T(8,128)S(1)}, f32[576,128]{1,0:T(8,128)S(1)}, u32[]{:S(2)}, u32[]{:S(2)}) collective-permute-start(f32[576,128]{1,0:T(8,128)S(1)} %pad_maximum_fusion), channel_id=1, source_target_pairs={{0,2},{1,3},{2,0},{3,1},{4,6},{5,7},{6,4},{7,5},{8,10},{9,11},{10,... | collective-permute-start | bytes 884744 | tf_op jit(solution)/shard_map/ppermute | solution.py:361
  52.6 0.6 collective-permute-start.11
  53.1 1.6 %collective-permute-start.12 = (f32[576,128]{1,0:T(8,128)S(1)}, f32[576,128]{1,0:T(8,128)S(1)}, u32[]{:S(2)}, u32[]{:S(2)}) collective-permute-start(f32[576,128]{1,0:T(8,128)S(1)} %pad_maximum_fusion), channel_id=1, source_target_pairs={{0,6},{1,7},{2,4},{3,5},{4,2},{5,3},{6,0},{7,1},{8,14},{9,15},{10,... | collective-permute-start | bytes 884744 | tf_op jit(solution)/shard_map/ppermute | solution.py:361
  54.7 6.2 %collective-permute-done.10 = f32[576,128]{1,0:T(8,128)S(1)} collective-permute-done((f32[576,128]{1,0:T(8,128)S(1)}, f32[576,128]{1,0:T(8,128)S(1)}, u32[]{:S(2)}, u32[]{:S(2)}) %collective-permute-start.10) | collective-permute-done | bytes 294944 | tf_op jit(solution)/shard_map/ppermute | solution.py:361
  61.0 4.6 %collective-permute-done.11 = f32[576,128]{1,0:T(8,128)S(1)} collective-permute-done((f32[576,128]{1,0:T(8,128)S(1)}, f32[576,128]{1,0:T(8,128)S(1)}, u32[]{:S(2)}, u32[]{:S(2)}) %collective-permute-start.11) | collective-permute-done | bytes 294944 | tf_op jit(solution)/shard_map/ppermute | solution.py:361
  65.6 0.0 collective-permute-done.12
  65.7 0.1 collective-permute-start.13
  65.7 2.8 %collective-permute-done.13.far_ref = f32[2304,128]{1,0:T(8,128)S(1)} collective-permute-done((f32[2304,128]{1,0:T(8,128)S(1)}, f32[2304,128]{1,0:T(8,128)S(1)}, u32[]{:S(2)}, u32[]{:S(2)}) %collective-permute-start.13) | collective-permute-done | bytes 1179680 | tf_op jit(solution)/shard_map/ppermute | solution.py:361
  68.6 26.1 %factor.1 = (f32[128,1024]{1,0:T(8,128)}, f32[8,128]{1,0:T(8,128)}) custom-call(f32[2304,128]{1,0:T(8,128)S(1)} %constant_dynamic-update-slice_fusion.own_ref, f32[2304,128]{1,0:T(8,128)S(1)} %collective-permute-done.13.far_ref), custom_call_target="tpu_custom_call" | custom-call | tf_op jit(solution)/shard_map/factor/pallas_call | solution.py:341
  (8 shorter events, 0.1 us)
Async XLA Ops:
  10.4 3.0 %collective-permute-start = (f32[2304,128]{1,0:T(8,128)S(1)}, f32[2304,128]{1,0:T(8,128)S(1)}, u32[]{:S(2)}, u32[]{:S(2)}) collective-permute-start(f32[2304,128]{1,0:T(8,128)S(1)} %get-tuple-element.7), channel_id=1, source_target_pairs={{0,1},{1,0},{2,3},{3,2},{4,5},{5,4},{6,7},{7,6},{8,9},{9,8},{10,11... | collective-permute-start | bytes 3538952 | tf_op jit(solution)/shard_map/ppermute | solution.py:361
  13.6 11.7 %collective-permute-start.3 = (f32[576,128]{1,0:T(8,128)S(1)}, f32[576,128]{1,0:T(8,128)S(1)}, u32[]{:S(2)}, u32[]{:S(2)}) collective-permute-start(f32[576,128]{1,0:T(8,128)S(1)} %get-tuple-element.13), channel_id=1, source_target_pairs={{0,6},{1,7},{2,4},{3,5},{4,2},{5,3},{6,0},{7,1},{8,14},{9,15},{10,... | collective-permute-start | bytes 884744 | tf_op jit(solution)/shard_map/ppermute | solution.py:361
  17.4 13.7 %collective-permute-start.2 = (f32[576,128]{1,0:T(8,128)S(1)}, f32[576,128]{1,0:T(8,128)S(1)}, u32[]{:S(2)}, u32[]{:S(2)}) collective-permute-start(f32[576,128]{1,0:T(8,128)S(1)} %get-tuple-element.14), channel_id=1, source_target_pairs={{0,4},{1,5},{2,6},{3,7},{4,0},{5,1},{6,2},{7,3},{8,12},{9,13},{10,... | collective-permute-start | bytes 884744 | tf_op jit(solution)/shard_map/ppermute | solution.py:361
  18.3 13.1 %collective-permute-start.1 = (f32[576,128]{1,0:T(8,128)S(1)}, f32[576,128]{1,0:T(8,128)S(1)}, u32[]{:S(2)}, u32[]{:S(2)}) collective-permute-start(f32[576,128]{1,0:T(8,128)S(1)} %get-tuple-element.15), channel_id=1, source_target_pairs={{0,2},{1,3},{2,0},{3,1},{4,6},{5,7},{6,4},{7,5},{8,10},{9,11},{10,... | collective-permute-start | bytes 884744 | tf_op jit(solution)/shard_map/ppermute | solution.py:361
  31.4 6.4 %collective-permute-start.6 = (f32[144,128]{1,0:T(8,128)S(1)}, f32[144,128]{1,0:T(8,128)S(1)}, u32[]{:S(2)}, u32[]{:S(2)}) collective-permute-start(f32[144,128]{1,0:T(8,128)S(1)} %get-tuple-element.17), channel_id=1, source_target_pairs={{0,24},{8,16},{16,8},{24,0},{1,25},{9,17},{17,9},{25,1},{2,26},{10... | collective-permute-start | bytes 221192 | tf_op jit(solution)/shard_map/ppermute | solution.py:361
  35.2 6.4 %collective-permute-start.5 = (f32[144,128]{1,0:T(8,128)S(1)}, f32[144,128]{1,0:T(8,128)S(1)}, u32[]{:S(2)}, u32[]{:S(2)}) collective-permute-start(f32[144,128]{1,0:T(8,128)S(1)} %get-tuple-element.18), channel_id=1, source_target_pairs={{0,16},{8,24},{16,0},{24,8},{1,17},{9,25},{17,1},{25,9},{2,18},{10... | collective-permute-start | bytes 221192 | tf_op jit(solution)/shard_map/ppermute | solution.py:361
  35.2 6.4 %collective-permute-start.4 = (f32[144,128]{1,0:T(8,128)S(1)}, f32[144,128]{1,0:T(8,128)S(1)}, u32[]{:S(2)}, u32[]{:S(2)}) collective-permute-start(f32[144,128]{1,0:T(8,128)S(1)} %get-tuple-element.16), channel_id=1, source_target_pairs={{0,8},{8,0},{16,24},{24,16},{1,9},{9,1},{17,25},{25,17},{2,10},{10... | collective-permute-start | bytes 221192 | tf_op jit(solution)/shard_map/ppermute | solution.py:361
  41.6 4.7 %collective-permute-start.7 = (f32[144,128]{1,0:T(8,128)S(1)}, f32[144,128]{1,0:T(8,128)S(1)}, u32[]{:S(2)}, u32[]{:S(2)}) collective-permute-start(f32[144,128]{1,0:T(8,128)S(1)} %get-tuple-element.11), channel_id=1, source_target_pairs={{0,8},{8,0},{16,24},{24,16},{1,9},{9,1},{17,25},{25,17},{2,10},{10... | collective-permute-start | bytes 221192 | tf_op jit(solution)/shard_map/ppermute | solution.py:361
  42.7 6.9 %collective-permute-start.8 = (f32[144,128]{1,0:T(8,128)S(1)}, f32[144,128]{1,0:T(8,128)S(1)}, u32[]{:S(2)}, u32[]{:S(2)}) collective-permute-start(f32[144,128]{1,0:T(8,128)S(1)} %get-tuple-element.11), channel_id=1, source_target_pairs={{0,16},{8,24},{16,0},{24,8},{1,17},{9,25},{17,1},{25,9},{2,18},{10... | collective-permute-start | bytes 221192 | tf_op jit(solution)/shard_map/ppermute | solution.py:361
  45.0 6.2 %collective-permute-start.9 = (f32[144,128]{1,0:T(8,128)S(1)}, f32[144,128]{1,0:T(8,128)S(1)}, u32[]{:S(2)}, u32[]{:S(2)}) collective-permute-start(f32[144,128]{1,0:T(8,128)S(1)} %get-tuple-element.11), channel_id=1, source_target_pairs={{0,24},{8,16},{16,8},{24,0},{1,25},{9,17},{17,9},{25,1},{2,26},{10... | collective-permute-start | bytes 221192 | tf_op jit(solution)/shard_map/ppermute | solution.py:361
  51.1 9.8 %collective-permute-start.10 = (f32[576,128]{1,0:T(8,128)S(1)}, f32[576,128]{1,0:T(8,128)S(1)}, u32[]{:S(2)}, u32[]{:S(2)}) collective-permute-start(f32[576,128]{1,0:T(8,128)S(1)} %pad_maximum_fusion), channel_id=1, source_target_pairs={{0,2},{1,3},{2,0},{3,1},{4,6},{5,7},{6,4},{7,5},{8,10},{9,11},{10,... | collective-permute-start | bytes 884744 | tf_op jit(solution)/shard_map/ppermute | solution.py:361
  52.6 13.0 %collective-permute-start.11 = (f32[576,128]{1,0:T(8,128)S(1)}, f32[576,128]{1,0:T(8,128)S(1)}, u32[]{:S(2)}, u32[]{:S(2)}) collective-permute-start(f32[576,128]{1,0:T(8,128)S(1)} %pad_maximum_fusion), channel_id=1, source_target_pairs={{0,4},{1,5},{2,6},{3,7},{4,0},{5,1},{6,2},{7,3},{8,12},{9,13},{10,... | collective-permute-start | bytes 884744 | tf_op jit(solution)/shard_map/ppermute | solution.py:361
  53.1 12.5 %collective-permute-start.12 = (f32[576,128]{1,0:T(8,128)S(1)}, f32[576,128]{1,0:T(8,128)S(1)}, u32[]{:S(2)}, u32[]{:S(2)}) collective-permute-start(f32[576,128]{1,0:T(8,128)S(1)} %pad_maximum_fusion), channel_id=1, source_target_pairs={{0,6},{1,7},{2,4},{3,5},{4,2},{5,3},{6,0},{7,1},{8,14},{9,15},{10,... | collective-permute-start | bytes 884744 | tf_op jit(solution)/shard_map/ppermute | solution.py:361
  65.7 2.9 %collective-permute-start.13 = (f32[2304,128]{1,0:T(8,128)S(1)}, f32[2304,128]{1,0:T(8,128)S(1)}, u32[]{:S(2)}, u32[]{:S(2)}) collective-permute-start(f32[2304,128]{1,0:T(8,128)S(1)} %constant_dynamic-update-slice_fusion.own_ref), channel_id=1, source_target_pairs={{0,1},{1,0},{2,3},{3,2},{4,5},{5,4},{6,7},{7,6},{8,9},{9,8},{10,11... | collective-permute-start | bytes 3538952 | tf_op jit(solution)/shard_map/ppermute | solution.py:361

commit v7 on v6

--- a/solution.py
+++ b/solution.py
@@ -21,14 +21,18 @@
     return hi, (x - hi.astype(F32)).astype(BF16)
 
 
-def block_at(width):
+def packed_rows(width):
     nb = width // NB
-    places, at = {}, 0
-    for i in range(nb):
-        for j in range(i, nb):
-            places[i, j] = at
-            at += 1
-    return places
+    rows, at = {}, 0
+    for t in range(0, nb, 2):
+        for i in (t, t + 1):
+            for j in range(i + 1, nb):
+                rows[i, j] = at
+                at += NB
+        for part in ((t, "top"), (t + 1, "top"), (t, "corner")):
+            rows[part] = at
+            at += NB // 2
+    return rows, at
 
 
 def dot_t(a, b):
@@ -44,8 +48,8 @@
     cap, width = rows_ref.shape
     nb = width // NB
     half = sent // 2
-    total = nb * (nb + 1) // 2 * NB
-    tile = min(2 * NB, width)
+    place, total = packed_rows(width)
+    tile = 2 * NB
     tiles = [(i, i + tile) for i in range(0, width, tile)]
     parts = row_cuts(cap)
     copies = [
@@ -67,10 +71,9 @@
     info[...] = jnp.broadcast_to(
         jnp.dot(pinfo_ref[...], p, precision=lax.Precision.HIGHEST, preferred_element_type=F32), info.shape
     )
-    for row in range(total, sent, NB):
-        stage[row : row + NB, :] = jnp.zeros((NB, NB), F32)
-
-    place = block_at(width)
+    if sent > total:
+        stage[total:sent, :] = jnp.zeros((sent - total, NB), F32)
+
     side = lax.axis_index("blk") % 2
 
     def on_each_side(do):
@@ -99,14 +102,24 @@
             if n + 1 < len(parts):
                 acc[i:j, i:] = term
                 continue
-            for bi in range(i // NB, j // NB):
-                for bj in range(bi, nb):
-                    at = place[bi, bj] * NB
-                    stage[at : at + NB, :] = term[bi * NB - i : bi * NB - i + NB, bj * NB - i : bj * NB - i + NB]
+            hw = NB // 2
+            first = i // NB
+            for bi in (first, first + 1):
+                up = bi * NB - i
+                for bj in range(bi + 1, nb):
+                    at = place[bi, bj]
+                    stage[at : at + NB, :] = term[up : up + NB, bj * NB - i : bj * NB - i + NB]
+                at = place[bi, "top"]
+                stage[at : at + hw, :] = term[up : up + hw, up : up + NB]
+            at = place[first, "corner"]
+            stage[at : at + hw, :] = jnp.concatenate(
+                [term[hw:NB, hw:NB], term[NB + hw : 2 * NB, NB + hw : 2 * NB]], axis=1
+            )
             if i == 0:
-                hw = NB // 2
-                for b in range(2 * nb):
-                    stage[hw + b : hw + b + 1, 0:hw] = info[0:1, b * hw : (b + 1) * hw]
+                q = NB // 4
+                at = place[0, "top"] + q
+                for b in range(width // q):
+                    stage[at + b : at + b + 1, 0:q] = info[0:1, b * q : (b + 1) * q]
 
     def give(at_side):
         halves = (keep_ref, send_ref) if at_side == 0 else (send_ref, keep_ref)
@@ -218,7 +231,7 @@
 def factor_kernel(n_quarter, n_layer, own_ref, far_ref, root_ref, info_ref, g, s, minv, r, uhi, ulo, thi, tlo, y):
     width = r.shape[1]
     nb = width // NB
-    place = block_at(width)
+    place, _ = packed_rows(width)
     blk, layer = lax.axis_index("blk"), lax.axis_index("fibre")
     side, quarter = blk % 2, blk // 2
     piece = own_ref.shape[0] // (n_quarter * n_layer)
@@ -229,20 +242,32 @@
                 at = (ms * n_layer + mz) * piece
                 g[pl.ds(pl.multiple_of(to, 8), piece), :] = ref[at : at + piece, :]
 
+    hw, q = NB // 2, NB // 4
+
     def block(i, j):
-        return g[place[i, j] * NB : place[i, j] * NB + NB, :]
+        if i != j:
+            return g[place[i, j] : place[i, j] + NB, :]
+        at = place[i, "top"]
+        top = g[at : at + hw, :]
+        at = place[i - i % 2, "corner"]
+        corner = g[at : at + hw, :]
+        mirror = jnp.concatenate([top, top], axis=0).T
+        lane = lax.broadcasted_iota(jnp.int32, (hw, NB), 1)
+        if i % 2 == 0:
+            corner = jnp.concatenate([corner[:, hw:], corner[:, :hw]], axis=1)
+        if i == 0:
+            row = lax.broadcasted_iota(jnp.int32, (hw, NB), 0)
+            top = jnp.where((lane < q) & (row >= q), mirror[:hw, :], top)
+        return jnp.concatenate([top, jnp.where(lane < hw, mirror[hw:, :], corner)], axis=0)
 
     def span(i):
         return slice(i * NB, i * NB + NB)
 
-    hw = NB // 2
-    corner = g[0:NB, :]
-    mirror = corner.T
-    for b in range(2 * nb):
-        y[:, b * hw : (b + 1) * hw] = jnp.broadcast_to(corner[hw + b : hw + b + 1, 0:hw], (8, hw))
-    lane = lax.broadcasted_iota(jnp.int32, (hw, NB), 1)
-    s[0:hw, 0:NB] = corner[0:hw, :]
-    s[hw:NB, 0:NB] = jnp.where(lane < hw, mirror[hw:, :], corner[hw:, :])
+    for b in range(width // q):
+        at = place[0, "top"] + q + b
+        y[:, b * q : (b + 1) * q] = jnp.broadcast_to(g[at : at + 1, 0:q], (8, q))
+    s[span(0), span(0)] = block(0, 0)
+
     def inverse(i):
         return split(minv[span(i), :])
 
@@ -304,7 +329,14 @@
             r[span(i), 0 : i * NB] = jnp.zeros((NB, i * NB), F32)
             yield
 
-    other_work = iter(())
+    def begin():
+        s[span(1), span(1)] = block(1, 1)
+        yield
+        for b in range(1, nb):
+            s[span(0), span(b)] = block(0, b)
+        yield
+
+    other_work = begin()
     for i in range(nb):
 
         def read(u):
@@ -318,14 +350,10 @@
         factor_block(read, write, other_work)
         for _ in other_work:
             pass
-        if i == 0:
-            for b in range(1, nb):
-                s[span(0), span(b)] = block(0, b)
         if i + 1 < nb:
             uh, ul = solve(i, span(i + 1))
             at = slice((i + 1) * NB, (i + 2) * NB)
-            have = s[at, at] if i else block(1, 1)
-            s[at, at] = have - dot_t(three(uh, ul, 0), three_other(uh, ul, 0))
+            s[at, at] -= dot_t(three(uh, ul, 0), three_other(uh, ul, 0))
         other_work = rest_of(i)
     for _ in other_work:
         pass
@@ -385,8 +413,7 @@
     quarters = [2 * m for m in range(1, n_quarter)]
     layers = list(range(1, n_fibre))
     unit = 8 * n_blk * n_fibre
-    nb = width // NB
-    sent = -(-(nb * (nb + 1) // 2 * NB) // unit) * unit
+    sent = -(-packed_rows(width)[1] // unit) * unit
 
     keep, send = gram(readings, values, counts, prior_root, prior_info, sent)
     parts = [keep, swap(send, "blk", 1)]

time: 94.8 us -> 93 us (0.981)
  waiting for transfers between devices: 40 us -> 38.1 us
    ppermute x14, waiting for transfers between devices: 40 us -> 38.1 us  [swap(): return lax.ppermute(x, axis, [(d, d ^ mask) for d in range(n)])]
where the time goes in v7:
time: 93 us
  waiting for transfers between devices  38.1 us (41%)
  Pallas kernels  35.5 us (38%)
  starting transfers between devices  17.7 us (19%)
  between operations  1.35 us (1%)
    ppermute x14, waiting for transfers between devices, swap(): return lax.ppermute(x, axis, [(d, d ^ mask) for d in range(n)])  38.1 us
    pallas_call x1, Pallas kernels, factor(): pl.pallas_call(functools.partial(factor_kernel, n_quarter, n_layer), in_s...  26.2 us
    ppermute x14, starting transfers between devices, swap(): return lax.ppermute(x, axis, [(d, d ^ mask) for d in range(n)])  17.7 us
    pallas_call x1, Pallas kernels, gram(): pl.pallas_call(functools.partial(gram_kernel, sent), in_specs=[pl.BlockSp...  9.36 us
  transfers between devices with their start and end apart: 14, of which 12 were waited for; matrix products, arithmetic and copies ran while one was open for 0% of the time, Pallas kernels for 0%

profile of v7, /device:TPU:0, one launch (start us, length us, event | category | flops | bytes accessed | tf_op | source)
XLA Modules:
  0.0 93.0 jit_solution(2148603648700931128)
XLA Ops:
  1.3 9.4 %gram.1 = (f32[2176,128]{1,0:T(8,128)S(1)}, f32[2176,128]{1,0:T(8,128)S(1)}) custom-call(s32[1]{0:T(128)S(6)} %copy.13.count_ref, bf16[4096,1024]{1,0:T(8,128)(2,1)} %rows_ref.1, bf16[4096]{0:T(1024)(128)(2,1)} %vals_ref.1, f32[32,1024]{1,0:T(8,128)} %prior_ref.1, f32[1,32]{1,0:T(1,128)} %bitcast.2), custom_call_target="tpu_custom_call" | custom-call | tf_op jit(solution)/shard_map/gram/pallas_call | solution.py:138
  10.6 0.4 collective-permute-start
  11.0 2.4 %collective-permute-done = f32[2176,128]{1,0:T(8,128)S(1)} collective-permute-done((f32[2176,128]{1,0:T(8,128)S(1)}, f32[2176,128]{1,0:T(8,128)S(1)}, u32[]{:S(2)}, u32[]{:S(2)}) %collective-permute-start) | collective-permute-done | bytes 1114144 | tf_op jit(solution)/shard_map/ppermute | solution.py:389
  13.5 0.1 dynamic-slice_add_fusion.3
  13.6 4.1 %collective-permute-start.3 = (f32[544,128]{1,0:T(8,128)S(1)}, f32[544,128]{1,0:T(8,128)S(1)}, u32[]{:S(2)}, u32[]{:S(2)}) collective-permute-start(f32[544,128]{1,0:T(8,128)S(1)} %get-tuple-element.13), channel_id=1, source_target_pairs={{0,6},{1,7},{2,4},{3,5},{4,2},{5,3},{6,0},{7,1},{8,14},{9,15},{10,... | collective-permute-start | bytes 835592 | tf_op jit(solution)/shard_map/ppermute | solution.py:389
  17.7 0.5 collective-permute-start.2
  18.2 0.1 collective-permute-start.1
  18.3 6.8 %collective-permute-done.3 = f32[544,128]{1,0:T(8,128)S(1)} collective-permute-done((f32[544,128]{1,0:T(8,128)S(1)}, f32[544,128]{1,0:T(8,128)S(1)}, u32[]{:S(2)}, u32[]{:S(2)}) %collective-permute-start.3) | collective-permute-done | bytes 278560 | tf_op jit(solution)/shard_map/ppermute | solution.py:389
  25.2 5.4 %collective-permute-done.2 = f32[544,128]{1,0:T(8,128)S(1)} collective-permute-done((f32[544,128]{1,0:T(8,128)S(1)}, f32[544,128]{1,0:T(8,128)S(1)}, u32[]{:S(2)}, u32[]{:S(2)}) %collective-permute-start.2) | collective-permute-done | bytes 278560 | tf_op jit(solution)/shard_map/ppermute | solution.py:389
  30.6 0.3 collective-permute-done.1
  30.9 0.1 dynamic-slice_add_fusion.6
  31.0 3.3 %collective-permute-start.6 = (f32[136,128]{1,0:T(8,128)S(1)}, f32[136,128]{1,0:T(8,128)S(1)}, u32[]{:S(2)}, u32[]{:S(2)}) collective-permute-start(f32[136,128]{1,0:T(8,128)S(1)} %get-tuple-element.17), channel_id=1, source_target_pairs={{0,24},{8,16},{16,8},{24,0},{1,25},{9,17},{17,9},{25,1},{2,26},{10... | collective-permute-start | bytes 208904 | tf_op jit(solution)/shard_map/ppermute | solution.py:389
  34.3 0.0 collective-permute-start.5
  34.3 1.1 %collective-permute-start.4 = (f32[136,128]{1,0:T(8,128)S(1)}, f32[136,128]{1,0:T(8,128)S(1)}, u32[]{:S(2)}, u32[]{:S(2)}) collective-permute-start(f32[136,128]{1,0:T(8,128)S(1)} %get-tuple-element.16), channel_id=1, source_target_pairs={{0,8},{8,0},{16,24},{24,16},{1,9},{9,1},{17,25},{25,17},{2,10},{10... | collective-permute-start | bytes 208904 | tf_op jit(solution)/shard_map/ppermute | solution.py:389
  35.4 2.3 %collective-permute-done.6 = f32[136,128]{1,0:T(8,128)S(1)} collective-permute-done((f32[136,128]{1,0:T(8,128)S(1)}, f32[136,128]{1,0:T(8,128)S(1)}, u32[]{:S(2)}, u32[]{:S(2)}) %collective-permute-start.6) | collective-permute-done | bytes 69664 | tf_op jit(solution)/shard_map/ppermute | solution.py:389
  37.7 2.8 %collective-permute-done.5 = f32[136,128]{1,0:T(8,128)S(1)} collective-permute-done((f32[136,128]{1,0:T(8,128)S(1)}, f32[136,128]{1,0:T(8,128)S(1)}, u32[]{:S(2)}, u32[]{:S(2)}) %collective-permute-start.5) | collective-permute-done | bytes 69664 | tf_op jit(solution)/shard_map/ppermute | solution.py:389
  40.5 0.0 collective-permute-done.4
  40.6 0.9 collective-permute-start.7
  41.4 2.3 %collective-permute-start.8 = (f32[136,128]{1,0:T(8,128)S(1)}, f32[136,128]{1,0:T(8,128)S(1)}, u32[]{:S(2)}, u32[]{:S(2)}) collective-permute-start(f32[136,128]{1,0:T(8,128)S(1)} %get-tuple-element.11), channel_id=1, source_target_pairs={{0,16},{8,24},{16,0},{24,8},{1,17},{9,25},{17,1},{25,9},{2,18},{10... | collective-permute-start | bytes 208904 | tf_op jit(solution)/shard_map/ppermute | solution.py:389
  43.7 1.3 %collective-permute-start.9 = (f32[136,128]{1,0:T(8,128)S(1)}, f32[136,128]{1,0:T(8,128)S(1)}, u32[]{:S(2)}, u32[]{:S(2)}) collective-permute-start(f32[136,128]{1,0:T(8,128)S(1)} %get-tuple-element.11), channel_id=1, source_target_pairs={{0,24},{8,16},{16,8},{24,0},{1,25},{9,17},{17,9},{25,1},{2,26},{10... | collective-permute-start | bytes 208904 | tf_op jit(solution)/shard_map/ppermute | solution.py:389
  45.0 0.5 collective-permute-done.7
  45.5 3.0 %collective-permute-done.8 = f32[136,128]{1,0:T(8,128)S(1)} collective-permute-done((f32[136,128]{1,0:T(8,128)S(1)}, f32[136,128]{1,0:T(8,128)S(1)}, u32[]{:S(2)}, u32[]{:S(2)}) %collective-permute-start.8) | collective-permute-done | bytes 69664 | tf_op jit(solution)/shard_map/ppermute | solution.py:389
  48.5 1.4 %collective-permute-done.9 = f32[136,128]{1,0:T(8,128)S(1)} collective-permute-done((f32[136,128]{1,0:T(8,128)S(1)}, f32[136,128]{1,0:T(8,128)S(1)}, u32[]{:S(2)}, u32[]{:S(2)}) %collective-permute-start.9) | collective-permute-done | bytes 69664 | tf_op jit(solution)/shard_map/ppermute | solution.py:389
  49.9 1.8 %collective-permute-start.10 = (f32[544,128]{1,0:T(8,128)S(1)}, f32[544,128]{1,0:T(8,128)S(1)}, u32[]{:S(2)}, u32[]{:S(2)}) collective-permute-start(f32[544,128]{1,0:T(8,128)S(1)} %pad_maximum_fusion), channel_id=1, source_target_pairs={{0,2},{1,3},{2,0},{3,1},{4,6},{5,7},{6,4},{7,5},{8,10},{9,11},{10,... | collective-permute-start | bytes 835592 | tf_op jit(solution)/shard_map/ppermute | solution.py:389
  51.7 0.0 collective-permute-start.11
  51.7 1.8 %collective-permute-start.12 = (f32[544,128]{1,0:T(8,128)S(1)}, f32[544,128]{1,0:T(8,128)S(1)}, u32[]{:S(2)}, u32[]{:S(2)}) collective-permute-start(f32[544,128]{1,0:T(8,128)S(1)} %pad_maximum_fusion), channel_id=1, source_target_pairs={{0,6},{1,7},{2,4},{3,5},{4,2},{5,3},{6,0},{7,1},{8,14},{9,15},{10,... | collective-permute-start | bytes 835592 | tf_op jit(solution)/shard_map/ppermute | solution.py:389
  53.5 5.6 %collective-permute-done.10 = f32[544,128]{1,0:T(8,128)S(1)} collective-permute-done((f32[544,128]{1,0:T(8,128)S(1)}, f32[544,128]{1,0:T(8,128)S(1)}, u32[]{:S(2)}, u32[]{:S(2)}) %collective-permute-start.10) | collective-permute-done | bytes 278560 | tf_op jit(solution)/shard_map/ppermute | solution.py:389
  59.2 4.7 %collective-permute-done.11 = f32[544,128]{1,0:T(8,128)S(1)} collective-permute-done((f32[544,128]{1,0:T(8,128)S(1)}, f32[544,128]{1,0:T(8,128)S(1)}, u32[]{:S(2)}, u32[]{:S(2)}) %collective-permute-start.11) | collective-permute-done | bytes 278560 | tf_op jit(solution)/shard_map/ppermute | solution.py:389
  63.9 0.0 collective-permute-done.12
  64.0 0.1 collective-permute-start.13
  64.0 2.7 %collective-permute-done.13.far_ref = f32[2176,128]{1,0:T(8,128)S(1)} collective-permute-done((f32[2176,128]{1,0:T(8,128)S(1)}, f32[2176,128]{1,0:T(8,128)S(1)}, u32[]{:S(2)}, u32[]{:S(2)}) %collective-permute-start.13) | collective-permute-done | bytes 1114144 | tf_op jit(solution)/shard_map/ppermute | solution.py:389
  66.8 26.2 %factor.1 = (f32[128,1024]{1,0:T(8,128)}, f32[8,128]{1,0:T(8,128)}) custom-call(f32[2176,128]{1,0:T(8,128)S(1)} %constant_dynamic-update-slice_fusion.own_ref, f32[2176,128]{1,0:T(8,128)S(1)} %collective-permute-done.13.far_ref), custom_call_target="tpu_custom_call" | custom-call | tf_op jit(solution)/shard_map/factor/pallas_call | solution.py:369
  (8 shorter events, 0.1 us)
Async XLA Ops:
  10.6 2.8 %collective-permute-start = (f32[2176,128]{1,0:T(8,128)S(1)}, f32[2176,128]{1,0:T(8,128)S(1)}, u32[]{:S(2)}, u32[]{:S(2)}) collective-permute-start(f32[2176,128]{1,0:T(8,128)S(1)} %get-tuple-element.7), channel_id=1, source_target_pairs={{0,1},{1,0},{2,3},{3,2},{4,5},{5,4},{6,7},{7,6},{8,9},{9,8},{10,11... | collective-permute-start | bytes 3342344 | tf_op jit(solution)/shard_map/ppermute | solution.py:389
  13.6 11.6 %collective-permute-start.3 = (f32[544,128]{1,0:T(8,128)S(1)}, f32[544,128]{1,0:T(8,128)S(1)}, u32[]{:S(2)}, u32[]{:S(2)}) collective-permute-start(f32[544,128]{1,0:T(8,128)S(1)} %get-tuple-element.13), channel_id=1, source_target_pairs={{0,6},{1,7},{2,4},{3,5},{4,2},{5,3},{6,0},{7,1},{8,14},{9,15},{10,... | collective-permute-start | bytes 835592 | tf_op jit(solution)/shard_map/ppermute | solution.py:389
  17.7 12.9 %collective-permute-start.2 = (f32[544,128]{1,0:T(8,128)S(1)}, f32[544,128]{1,0:T(8,128)S(1)}, u32[]{:S(2)}, u32[]{:S(2)}) collective-permute-start(f32[544,128]{1,0:T(8,128)S(1)} %get-tuple-element.14), channel_id=1, source_target_pairs={{0,4},{1,5},{2,6},{3,7},{4,0},{5,1},{6,2},{7,3},{8,12},{9,13},{10,... | collective-permute-start | bytes 835592 | tf_op jit(solution)/shard_map/ppermute | solution.py:389
  18.2 12.7 %collective-permute-start.1 = (f32[544,128]{1,0:T(8,128)S(1)}, f32[544,128]{1,0:T(8,128)S(1)}, u32[]{:S(2)}, u32[]{:S(2)}) collective-permute-start(f32[544,128]{1,0:T(8,128)S(1)} %get-tuple-element.15), channel_id=1, source_target_pairs={{0,2},{1,3},{2,0},{3,1},{4,6},{5,7},{6,4},{7,5},{8,10},{9,11},{10,... | collective-permute-start | bytes 835592 | tf_op jit(solution)/shard_map/ppermute | solution.py:389
  31.0 6.8 %collective-permute-start.6 = (f32[136,128]{1,0:T(8,128)S(1)}, f32[136,128]{1,0:T(8,128)S(1)}, u32[]{:S(2)}, u32[]{:S(2)}) collective-permute-start(f32[136,128]{1,0:T(8,128)S(1)} %get-tuple-element.17), channel_id=1, source_target_pairs={{0,24},{8,16},{16,8},{24,0},{1,25},{9,17},{17,9},{25,1},{2,26},{10... | collective-permute-start | bytes 208904 | tf_op jit(solution)/shard_map/ppermute | solution.py:389
  34.3 6.2 %collective-permute-start.5 = (f32[136,128]{1,0:T(8,128)S(1)}, f32[136,128]{1,0:T(8,128)S(1)}, u32[]{:S(2)}, u32[]{:S(2)}) collective-permute-start(f32[136,128]{1,0:T(8,128)S(1)} %get-tuple-element.18), channel_id=1, source_target_pairs={{0,16},{8,24},{16,0},{24,8},{1,17},{9,25},{17,1},{25,9},{2,18},{10... | collective-permute-start | bytes 208904 | tf_op jit(solution)/shard_map/ppermute | solution.py:389
  34.3 6.2 %collective-permute-start.4 = (f32[136,128]{1,0:T(8,128)S(1)}, f32[136,128]{1,0:T(8,128)S(1)}, u32[]{:S(2)}, u32[]{:S(2)}) collective-permute-start(f32[136,128]{1,0:T(8,128)S(1)} %get-tuple-element.16), channel_id=1, source_target_pairs={{0,8},{8,0},{16,24},{24,16},{1,9},{9,1},{17,25},{25,17},{2,10},{10... | collective-permute-start | bytes 208904 | tf_op jit(solution)/shard_map/ppermute | solution.py:389
  40.6 4.9 %collective-permute-start.7 = (f32[136,128]{1,0:T(8,128)S(1)}, f32[136,128]{1,0:T(8,128)S(1)}, u32[]{:S(2)}, u32[]{:S(2)}) collective-permute-start(f32[136,128]{1,0:T(8,128)S(1)} %get-tuple-element.11), channel_id=1, source_target_pairs={{0,8},{8,0},{16,24},{24,16},{1,9},{9,1},{17,25},{25,17},{2,10},{10... | collective-permute-start | bytes 208904 | tf_op jit(solution)/shard_map/ppermute | solution.py:389
  41.4 7.1 %collective-permute-start.8 = (f32[136,128]{1,0:T(8,128)S(1)}, f32[136,128]{1,0:T(8,128)S(1)}, u32[]{:S(2)}, u32[]{:S(2)}) collective-permute-start(f32[136,128]{1,0:T(8,128)S(1)} %get-tuple-element.11), channel_id=1, source_target_pairs={{0,16},{8,24},{16,0},{24,8},{1,17},{9,25},{17,1},{25,9},{2,18},{10... | collective-permute-start | bytes 208904 | tf_op jit(solution)/shard_map/ppermute | solution.py:389
  43.7 6.2 %collective-permute-start.9 = (f32[136,128]{1,0:T(8,128)S(1)}, f32[136,128]{1,0:T(8,128)S(1)}, u32[]{:S(2)}, u32[]{:S(2)}) collective-permute-start(f32[136,128]{1,0:T(8,128)S(1)} %get-tuple-element.11), channel_id=1, source_target_pairs={{0,24},{8,16},{16,8},{24,0},{1,25},{9,17},{17,9},{25,1},{2,26},{10... | collective-permute-start | bytes 208904 | tf_op jit(solution)/shard_map/ppermute | solution.py:389
  49.9 9.2 %collective-permute-start.10 = (f32[544,128]{1,0:T(8,128)S(1)}, f32[544,128]{1,0:T(8,128)S(1)}, u32[]{:S(2)}, u32[]{:S(2)}) collective-permute-start(f32[544,128]{1,0:T(8,128)S(1)} %pad_maximum_fusion), channel_id=1, source_target_pairs={{0,2},{1,3},{2,0},{3,1},{4,6},{5,7},{6,4},{7,5},{8,10},{9,11},{10,... | collective-permute-start | bytes 835592 | tf_op jit(solution)/shard_map/ppermute | solution.py:389
  51.7 12.2 %collective-permute-start.11 = (f32[544,128]{1,0:T(8,128)S(1)}, f32[544,128]{1,0:T(8,128)S(1)}, u32[]{:S(2)}, u32[]{:S(2)}) collective-permute-start(f32[544,128]{1,0:T(8,128)S(1)} %pad_maximum_fusion), channel_id=1, source_target_pairs={{0,4},{1,5},{2,6},{3,7},{4,0},{5,1},{6,2},{7,3},{8,12},{9,13},{10,... | collective-permute-start | bytes 835592 | tf_op jit(solution)/shard_map/ppermute | solution.py:389
  51.7 12.2 %collective-permute-start.12 = (f32[544,128]{1,0:T(8,128)S(1)}, f32[544,128]{1,0:T(8,128)S(1)}, u32[]{:S(2)}, u32[]{:S(2)}) collective-permute-start(f32[544,128]{1,0:T(8,128)S(1)} %pad_maximum_fusion), channel_id=1, source_target_pairs={{0,6},{1,7},{2,4},{3,5},{4,2},{5,3},{6,0},{7,1},{8,14},{9,15},{10,... | collective-permute-start | bytes 835592 | tf_op jit(solution)/shard_map/ppermute | solution.py:389
  64.0 2.8 %collective-permute-start.13 = (f32[2176,128]{1,0:T(8,128)S(1)}, f32[2176,128]{1,0:T(8,128)S(1)}, u32[]{:S(2)}, u32[]{:S(2)}) collective-permute-start(f32[2176,128]{1,0:T(8,128)S(1)} %constant_dynamic-update-slice_fusion.own_ref), channel_id=1, source_target_pairs={{0,1},{1,0},{2,3},{3,2},{4,5},{5,4},{6,7},{7,6},{8,9},{9,8},{10,11... | collective-permute-start | bytes 3342344 | tf_op jit(solution)/shard_map/ppermute | solution.py:389

commit v8 on v7

--- a/solution.py
+++ b/solution.py
@@ -235,11 +235,12 @@
     blk, layer = lax.axis_index("blk"), lax.axis_index("fibre")
     side, quarter = blk % 2, blk // 2
     piece = own_ref.shape[0] // (n_quarter * n_layer)
-    for ms in range(n_quarter):
-        for mz in range(n_layer):
-            for mc, ref in enumerate((own_ref, far_ref)):
-                to = (((side ^ mc) * n_quarter + (quarter ^ ms)) * n_layer + (layer ^ mz)) * piece
-                at = (ms * n_layer + mz) * piece
+    for mc, ref in enumerate((own_ref, far_ref)):
+        held = side ^ mc
+        for ns, ms in enumerate(distances(n_quarter, held != 0)):
+            for nz, mz in enumerate(distances(n_layer, False)):
+                to = ((held * n_quarter + (quarter ^ ms)) * n_layer + (layer ^ mz)) * piece
+                at = (ns * n_layer + nz) * piece
                 g[pl.ds(pl.multiple_of(to, 8), piece), :] = ref[at : at + piece, :]
 
     hw, q = NB // 2, NB // 4
@@ -384,25 +385,44 @@
     )(own, far)
 
 
-def swap(x, axis, mask):
-    n = lax.axis_size(axis)
-    return lax.ppermute(x, axis, [(d, d ^ mask) for d in range(n)])
-
-
-def shares(parts, count, me):
+def turns(n, odd):
+    first = list(range(1, n))
+    return first[::-1] if odd else first
+
+
+def swap(x, axis, step):
+    n_blk, n_fibre = lax.axis_size("blk"), lax.axis_size("fibre")
+    pairs = []
+    for f in range(n_fibre):
+        for d in range(n_blk):
+            if axis == "side":
+                to = f, d ^ 1
+            elif axis == "blk":
+                to = f, d ^ 2 * turns(n_blk // 2, d % 2)[step]
+            else:
+                to = f ^ turns(n_fibre, 0)[step], d
+            pairs.append((f * n_blk + d, to[0] * n_blk + to[1]))
+    return lax.ppermute(x, ("fibre", "blk"), pairs)
+
+
+def distances(n, odd):
+    return [0] + [jnp.where(odd, o, e) for e, o in zip(turns(n, 0), turns(n, 1))]
+
+
+def shares(parts, count, me, odd):
     rows = parts[0].shape[0] // count
     return [
         functools.reduce(lambda a, b: a + b, [lax.dynamic_slice_in_dim(x, (me ^ m) * rows, rows, 0) for x in parts])
-        for m in range(count)
+        for m in distances(count, odd)
     ]
 
 
-def trade(mine, axis, masks):
-    return [mine[0]] + [swap(x, axis, m) for x, m in zip(mine[1:], masks)]
-
-
-def gather(x, axis, masks):
-    return jnp.concatenate([x] + [swap(x, axis, m) for m in masks], axis=0)
+def trade(mine, axis):
+    return [mine[0]] + [swap(x, axis, n) for n, x in enumerate(mine[1:])]
+
+
+def gather(x, axis, count):
+    return jnp.concatenate([x] + [swap(x, axis, n) for n in range(count - 1)], axis=0)
 
 
 def local(readings, values, counts, prior_root, prior_info):
@@ -410,18 +430,17 @@
     n_blk, n_fibre = lax.axis_size("blk"), lax.axis_size("fibre")
     blk, fibre = lax.axis_index("blk"), lax.axis_index("fibre")
     n_quarter = n_blk // 2
-    quarters = [2 * m for m in range(1, n_quarter)]
-    layers = list(range(1, n_fibre))
+    odd = blk % 2 != 0
     unit = 8 * n_blk * n_fibre
     sent = -(-packed_rows(width)[1] // unit) * unit
 
     keep, send = gram(readings, values, counts, prior_root, prior_info, sent)
-    parts = [keep, swap(send, "blk", 1)]
-    parts = trade(shares(parts, n_quarter, blk // 2), "blk", quarters)
-    parts = trade(shares(parts, n_fibre, fibre), "fibre", layers)
+    parts = [keep, swap(send, "side", 0)]
+    parts = trade(shares(parts, n_quarter, blk // 2, odd), "blk")
+    parts = trade(shares(parts, n_fibre, fibre, False), "fibre")
     own = functools.reduce(lambda x, y: x + y, parts)
-    own = gather(gather(own, "fibre", layers), "blk", quarters)
-    far = swap(own, "blk", 1)
+    own = gather(gather(own, "fibre", n_fibre), "blk", n_quarter)
+    far = swap(own, "side", 0)
     root, info = factor(own, far, n_quarter, n_fibre, width, width // n_blk)
     return root, info.reshape(width)
 

time: 93 us -> 91.1 us (0.980)
  waiting for transfers between devices: 38.1 us -> 35.8 us
    ppermute x14, waiting for transfers between devices: 38.1 us -> 35.8 us  [swap(): return lax.ppermute(x, ('fibre', 'blk'), pairs)]
  transfers between devices with their start and end apart: 14 -> 14, of which waited for: 12 -> 11; matrix products, arithmetic and copies ran while one was open for 0% -> 0% of each run, Pallas kernels for 0% -> 0%
where the time goes in v8:
time: 91.1 us; the launch traced here: 90.6 us
  waiting for transfers between devices  35.8 us (39%)
  Pallas kernels  35.7 us (39%)
  starting transfers between devices  17.4 us (19%)
  between operations  1.35 us (1%)
    ppermute x14, waiting for transfers between devices, swap(): return lax.ppermute(x, ('fibre', 'blk'), pairs)  35.8 us
    pallas_call x1, Pallas kernels, factor(): pl.pallas_call(functools.partial(factor_kernel, n_quarter, n_layer), in_s...  26.2 us
    ppermute x14, starting transfers between devices, swap(): return lax.ppermute(x, ('fibre', 'blk'), pairs)  17.4 us
    pallas_call x1, Pallas kernels, gram(): pl.pallas_call(functools.partial(gram_kernel, sent), in_specs=[pl.BlockSp...  9.51 us
  transfers between devices with their start and end apart: 14, of which 11 were waited for; matrix products, arithmetic and copies ran while one was open for 0% of the time, Pallas kernels for 0%

profile of v8, /device:TPU:0, one launch (start us, length us, event | category | flops | bytes accessed | tf_op | source)
XLA Modules:
  0.0 90.6 jit_solution(2096784836869975686)
XLA Ops:
  1.3 9.5 %gram.1 = (f32[2176,128]{1,0:T(8,128)S(1)}, f32[2176,128]{1,0:T(8,128)S(1)}) custom-call(s32[1]{0:T(128)S(6)} %copy.13.count_ref, bf16[4096,1024]{1,0:T(8,128)(2,1)} %rows_ref.1, bf16[4096]{0:T(1024)(128)(2,1)} %vals_ref.1, f32[32,1024]{1,0:T(8,128)} %prior_ref.1, f32[1,32]{1,0:T(1,128)} %bitcast.2), custom_call_target="tpu_custom_call" | custom-call | tf_op jit(solution)/shard_map/gram/pallas_call | solution.py:138
  10.8 0.6 collective-permute-start
  11.4 2.4 %collective-permute-done = f32[2176,128]{1,0:T(8,128)S(1)} collective-permute-done((f32[2176,128]{1,0:T(8,128)S(1)}, f32[2176,128]{1,0:T(8,128)S(1)}, u32[]{:S(2)}, u32[]{:S(2)}) %collective-permute-start) | collective-permute-done | bytes 1114144 | tf_op jit(solution)/shard_map/ppermute | solution.py:405
  13.7 0.1 dynamic-slice_add_fusion.3
  13.9 3.5 %collective-permute-start.3 = (f32[544,128]{1,0:T(8,128)S(1)}, f32[544,128]{1,0:T(8,128)S(1)}, u32[]{:S(2)}, u32[]{:S(2)}) collective-permute-start(f32[544,128]{1,0:T(8,128)S(1)} %get-tuple-element.13), channel_id=1, source_target_pairs={{0,6},{1,3},{2,4},{3,1},{4,2},{5,7},{6,0},{7,5},{8,14},{9,11},{10,... | collective-permute-start | bytes 835592 | tf_op jit(solution)/shard_map/ppermute | solution.py:405
  17.4 0.5 collective-permute-start.2
  17.9 0.1 collective-permute-start.1
  18.0 6.8 %collective-permute-done.3 = f32[544,128]{1,0:T(8,128)S(1)} collective-permute-done((f32[544,128]{1,0:T(8,128)S(1)}, f32[544,128]{1,0:T(8,128)S(1)}, u32[]{:S(2)}, u32[]{:S(2)}) %collective-permute-start.3) | collective-permute-done | bytes 278560 | tf_op jit(solution)/shard_map/ppermute | solution.py:405
  24.8 6.0 %collective-permute-done.2 = f32[544,128]{1,0:T(8,128)S(1)} collective-permute-done((f32[544,128]{1,0:T(8,128)S(1)}, f32[544,128]{1,0:T(8,128)S(1)}, u32[]{:S(2)}, u32[]{:S(2)}) %collective-permute-start.2) | collective-permute-done | bytes 278560 | tf_op jit(solution)/shard_map/ppermute | solution.py:405
  30.8 0.0 collective-permute-done.1
  30.8 0.1 dynamic-slice_add_fusion.6
  30.9 4.0 %collective-permute-start.6 = (f32[136,128]{1,0:T(8,128)S(1)}, f32[136,128]{1,0:T(8,128)S(1)}, u32[]{:S(2)}, u32[]{:S(2)}) collective-permute-start(f32[136,128]{1,0:T(8,128)S(1)} %get-tuple-element.17), channel_id=1, source_target_pairs={{0,24},{1,25},{2,26},{3,27},{4,28},{5,29},{6,30},{7,31},{8,16},{9,... | collective-permute-start | bytes 208904 | tf_op jit(solution)/shard_map/ppermute | solution.py:405
  34.9 0.0 collective-permute-start.5
  34.9 0.6 collective-permute-start.4
  35.5 2.1 %collective-permute-done.6 = f32[136,128]{1,0:T(8,128)S(1)} collective-permute-done((f32[136,128]{1,0:T(8,128)S(1)}, f32[136,128]{1,0:T(8,128)S(1)}, u32[]{:S(2)}, u32[]{:S(2)}) %collective-permute-start.6) | collective-permute-done | bytes 69664 | tf_op jit(solution)/shard_map/ppermute | solution.py:405
  37.6 2.6 %collective-permute-done.5 = f32[136,128]{1,0:T(8,128)S(1)} collective-permute-done((f32[136,128]{1,0:T(8,128)S(1)}, f32[136,128]{1,0:T(8,128)S(1)}, u32[]{:S(2)}, u32[]{:S(2)}) %collective-permute-start.5) | collective-permute-done | bytes 69664 | tf_op jit(solution)/shard_map/ppermute | solution.py:405
  40.2 0.1 collective-permute-done.4
  40.3 0.8 collective-permute-start.7
  41.1 2.3 %collective-permute-start.8 = (f32[136,128]{1,0:T(8,128)S(1)}, f32[136,128]{1,0:T(8,128)S(1)}, u32[]{:S(2)}, u32[]{:S(2)}) collective-permute-start(f32[136,128]{1,0:T(8,128)S(1)} %get-tuple-element.11), channel_id=1, source_target_pairs={{0,16},{1,17},{2,18},{3,19},{4,20},{5,21},{6,22},{7,23},{8,24},{9,... | collective-permute-start | bytes 208904 | tf_op jit(solution)/shard_map/ppermute | solution.py:405
  43.4 1.4 %collective-permute-start.9 = (f32[136,128]{1,0:T(8,128)S(1)}, f32[136,128]{1,0:T(8,128)S(1)}, u32[]{:S(2)}, u32[]{:S(2)}) collective-permute-start(f32[136,128]{1,0:T(8,128)S(1)} %get-tuple-element.11), channel_id=1, source_target_pairs={{0,24},{1,25},{2,26},{3,27},{4,28},{5,29},{6,30},{7,31},{8,16},{9,... | collective-permute-start | bytes 208904 | tf_op jit(solution)/shard_map/ppermute | solution.py:405
  44.8 0.0 collective-permute-done.7
  44.8 2.5 %collective-permute-done.8 = f32[136,128]{1,0:T(8,128)S(1)} collective-permute-done((f32[136,128]{1,0:T(8,128)S(1)}, f32[136,128]{1,0:T(8,128)S(1)}, u32[]{:S(2)}, u32[]{:S(2)}) %collective-permute-start.8) | collective-permute-done | bytes 69664 | tf_op jit(solution)/shard_map/ppermute | solution.py:405
  47.3 2.2 %collective-permute-done.9 = f32[136,128]{1,0:T(8,128)S(1)} collective-permute-done((f32[136,128]{1,0:T(8,128)S(1)}, f32[136,128]{1,0:T(8,128)S(1)}, u32[]{:S(2)}, u32[]{:S(2)}) %collective-permute-start.9) | collective-permute-done | bytes 69664 | tf_op jit(solution)/shard_map/ppermute | solution.py:405
  49.5 1.4 %collective-permute-start.10 = (f32[544,128]{1,0:T(8,128)S(1)}, f32[544,128]{1,0:T(8,128)S(1)}, u32[]{:S(2)}, u32[]{:S(2)}) collective-permute-start(f32[544,128]{1,0:T(8,128)S(1)} %pad_maximum_fusion), channel_id=1, source_target_pairs={{0,2},{1,7},{2,0},{3,5},{4,6},{5,3},{6,4},{7,1},{8,10},{9,15},{10,... | collective-permute-start | bytes 835592 | tf_op jit(solution)/shard_map/ppermute | solution.py:405
  50.9 0.6 collective-permute-start.11
  51.5 1.5 %collective-permute-start.12 = (f32[544,128]{1,0:T(8,128)S(1)}, f32[544,128]{1,0:T(8,128)S(1)}, u32[]{:S(2)}, u32[]{:S(2)}) collective-permute-start(f32[544,128]{1,0:T(8,128)S(1)} %pad_maximum_fusion), channel_id=1, source_target_pairs={{0,6},{1,3},{2,4},{3,1},{4,2},{5,7},{6,0},{7,5},{8,14},{9,11},{10,... | collective-permute-start | bytes 835592 | tf_op jit(solution)/shard_map/ppermute | solution.py:405
  53.1 5.7 %collective-permute-done.10 = f32[544,128]{1,0:T(8,128)S(1)} collective-permute-done((f32[544,128]{1,0:T(8,128)S(1)}, f32[544,128]{1,0:T(8,128)S(1)}, u32[]{:S(2)}, u32[]{:S(2)}) %collective-permute-start.10) | collective-permute-done | bytes 278560 | tf_op jit(solution)/shard_map/ppermute | solution.py:405
  58.8 0.0 collective-permute-done.11
  58.8 2.8 %collective-permute-done.12 = f32[544,128]{1,0:T(8,128)S(1)} collective-permute-done((f32[544,128]{1,0:T(8,128)S(1)}, f32[544,128]{1,0:T(8,128)S(1)}, u32[]{:S(2)}, u32[]{:S(2)}) %collective-permute-start.12) | collective-permute-done | bytes 278560 | tf_op jit(solution)/shard_map/ppermute | solution.py:405
  61.6 0.1 collective-permute-start.13
  61.7 2.7 %collective-permute-done.13.far_ref = f32[2176,128]{1,0:T(8,128)S(1)} collective-permute-done((f32[2176,128]{1,0:T(8,128)S(1)}, f32[2176,128]{1,0:T(8,128)S(1)}, u32[]{:S(2)}, u32[]{:S(2)}) %collective-permute-start.13) | collective-permute-done | bytes 1114144 | tf_op jit(solution)/shard_map/ppermute | solution.py:405
  64.4 26.2 %factor.1 = (f32[128,1024]{1,0:T(8,128)}, f32[8,128]{1,0:T(8,128)}) custom-call(f32[2176,128]{1,0:T(8,128)S(1)} %constant_dynamic-update-slice_fusion.own_ref, f32[2176,128]{1,0:T(8,128)S(1)} %collective-permute-done.13.far_ref), custom_call_target="tpu_custom_call" | custom-call | tf_op jit(solution)/shard_map/factor/pallas_call | solution.py:370
  (8 shorter events, 0.1 us)
Async XLA Ops:
  10.8 2.9 %collective-permute-start = (f32[2176,128]{1,0:T(8,128)S(1)}, f32[2176,128]{1,0:T(8,128)S(1)}, u32[]{:S(2)}, u32[]{:S(2)}) collective-permute-start(f32[2176,128]{1,0:T(8,128)S(1)} %get-tuple-element.7), channel_id=1, source_target_pairs={{0,1},{1,0},{2,3},{3,2},{4,5},{5,4},{6,7},{7,6},{8,9},{9,8},{10,11... | collective-permute-start | bytes 3342344 | tf_op jit(solution)/shard_map/ppermute | solution.py:405
  13.9 11.0 %collective-permute-start.3 = (f32[544,128]{1,0:T(8,128)S(1)}, f32[544,128]{1,0:T(8,128)S(1)}, u32[]{:S(2)}, u32[]{:S(2)}) collective-permute-start(f32[544,128]{1,0:T(8,128)S(1)} %get-tuple-element.13), channel_id=1, source_target_pairs={{0,6},{1,3},{2,4},{3,1},{4,2},{5,7},{6,0},{7,5},{8,14},{9,11},{10,... | collective-permute-start | bytes 835592 | tf_op jit(solution)/shard_map/ppermute | solution.py:405
  17.4 13.4 %collective-permute-start.2 = (f32[544,128]{1,0:T(8,128)S(1)}, f32[544,128]{1,0:T(8,128)S(1)}, u32[]{:S(2)}, u32[]{:S(2)}) collective-permute-start(f32[544,128]{1,0:T(8,128)S(1)} %get-tuple-element.14), channel_id=1, source_target_pairs={{0,4},{1,5},{2,6},{3,7},{4,0},{5,1},{6,2},{7,3},{8,12},{9,13},{10,... | collective-permute-start | bytes 835592 | tf_op jit(solution)/shard_map/ppermute | solution.py:405
  17.9 12.9 %collective-permute-start.1 = (f32[544,128]{1,0:T(8,128)S(1)}, f32[544,128]{1,0:T(8,128)S(1)}, u32[]{:S(2)}, u32[]{:S(2)}) collective-permute-start(f32[544,128]{1,0:T(8,128)S(1)} %get-tuple-element.15), channel_id=1, source_target_pairs={{0,2},{1,7},{2,0},{3,5},{4,6},{5,3},{6,4},{7,1},{8,10},{9,15},{10,... | collective-permute-start | bytes 835592 | tf_op jit(solution)/shard_map/ppermute | solution.py:405
  30.9 6.7 %collective-permute-start.6 = (f32[136,128]{1,0:T(8,128)S(1)}, f32[136,128]{1,0:T(8,128)S(1)}, u32[]{:S(2)}, u32[]{:S(2)}) collective-permute-start(f32[136,128]{1,0:T(8,128)S(1)} %get-tuple-element.17), channel_id=1, source_target_pairs={{0,24},{1,25},{2,26},{3,27},{4,28},{5,29},{6,30},{7,31},{8,16},{9,... | collective-permute-start | bytes 208904 | tf_op jit(solution)/shard_map/ppermute | solution.py:405
  34.9 5.3 %collective-permute-start.5 = (f32[136,128]{1,0:T(8,128)S(1)}, f32[136,128]{1,0:T(8,128)S(1)}, u32[]{:S(2)}, u32[]{:S(2)}) collective-permute-start(f32[136,128]{1,0:T(8,128)S(1)} %get-tuple-element.18), channel_id=1, source_target_pairs={{0,16},{1,17},{2,18},{3,19},{4,20},{5,21},{6,22},{7,23},{8,24},{9,... | collective-permute-start | bytes 208904 | tf_op jit(solution)/shard_map/ppermute | solution.py:405
  34.9 5.4 %collective-permute-start.4 = (f32[136,128]{1,0:T(8,128)S(1)}, f32[136,128]{1,0:T(8,128)S(1)}, u32[]{:S(2)}, u32[]{:S(2)}) collective-permute-start(f32[136,128]{1,0:T(8,128)S(1)} %get-tuple-element.16), channel_id=1, source_target_pairs={{0,8},{1,9},{2,10},{3,11},{4,12},{5,13},{6,14},{7,15},{8,0},{9,1},... | collective-permute-start | bytes 208904 | tf_op jit(solution)/shard_map/ppermute | solution.py:405
  40.3 4.5 %collective-permute-start.7 = (f32[136,128]{1,0:T(8,128)S(1)}, f32[136,128]{1,0:T(8,128)S(1)}, u32[]{:S(2)}, u32[]{:S(2)}) collective-permute-start(f32[136,128]{1,0:T(8,128)S(1)} %get-tuple-element.11), channel_id=1, source_target_pairs={{0,8},{1,9},{2,10},{3,11},{4,12},{5,13},{6,14},{7,15},{8,0},{9,1},... | collective-permute-start | bytes 208904 | tf_op jit(solution)/shard_map/ppermute | solution.py:405
  41.1 6.2 %collective-permute-start.8 = (f32[136,128]{1,0:T(8,128)S(1)}, f32[136,128]{1,0:T(8,128)S(1)}, u32[]{:S(2)}, u32[]{:S(2)}) collective-permute-start(f32[136,128]{1,0:T(8,128)S(1)} %get-tuple-element.11), channel_id=1, source_target_pairs={{0,16},{1,17},{2,18},{3,19},{4,20},{5,21},{6,22},{7,23},{8,24},{9,... | collective-permute-start | bytes 208904 | tf_op jit(solution)/shard_map/ppermute | solution.py:405
  43.4 6.1 %collective-permute-start.9 = (f32[136,128]{1,0:T(8,128)S(1)}, f32[136,128]{1,0:T(8,128)S(1)}, u32[]{:S(2)}, u32[]{:S(2)}) collective-permute-start(f32[136,128]{1,0:T(8,128)S(1)} %get-tuple-element.11), channel_id=1, source_target_pairs={{0,24},{1,25},{2,26},{3,27},{4,28},{5,29},{6,30},{7,31},{8,16},{9,... | collective-permute-start | bytes 208904 | tf_op jit(solution)/shard_map/ppermute | solution.py:405
  49.5 9.2 %collective-permute-start.10 = (f32[544,128]{1,0:T(8,128)S(1)}, f32[544,128]{1,0:T(8,128)S(1)}, u32[]{:S(2)}, u32[]{:S(2)}) collective-permute-start(f32[544,128]{1,0:T(8,128)S(1)} %pad_maximum_fusion), channel_id=1, source_target_pairs={{0,2},{1,7},{2,0},{3,5},{4,6},{5,3},{6,4},{7,1},{8,10},{9,15},{10,... | collective-permute-start | bytes 835592 | tf_op jit(solution)/shard_map/ppermute | solution.py:405
  50.9 7.8 %collective-permute-start.11 = (f32[544,128]{1,0:T(8,128)S(1)}, f32[544,128]{1,0:T(8,128)S(1)}, u32[]{:S(2)}, u32[]{:S(2)}) collective-permute-start(f32[544,128]{1,0:T(8,128)S(1)} %pad_maximum_fusion), channel_id=1, source_target_pairs={{0,4},{1,5},{2,6},{3,7},{4,0},{5,1},{6,2},{7,3},{8,12},{9,13},{10,... | collective-permute-start | bytes 835592 | tf_op jit(solution)/shard_map/ppermute | solution.py:405
  51.5 10.0 %collective-permute-start.12 = (f32[544,128]{1,0:T(8,128)S(1)}, f32[544,128]{1,0:T(8,128)S(1)}, u32[]{:S(2)}, u32[]{:S(2)}) collective-permute-start(f32[544,128]{1,0:T(8,128)S(1)} %pad_maximum_fusion), channel_id=1, source_target_pairs={{0,6},{1,3},{2,4},{3,1},{4,2},{5,7},{6,0},{7,5},{8,14},{9,11},{10,... | collective-permute-start | bytes 835592 | tf_op jit(solution)/shard_map/ppermute | solution.py:405
  61.6 2.8 %collective-permute-start.13 = (f32[2176,128]{1,0:T(8,128)S(1)}, f32[2176,128]{1,0:T(8,128)S(1)}, u32[]{:S(2)}, u32[]{:S(2)}) collective-permute-start(f32[2176,128]{1,0:T(8,128)S(1)} %constant_dynamic-update-slice_fusion.own_ref), channel_id=1, source_target_pairs={{0,1},{1,0},{2,3},{3,2},{4,5},{5,4},{6,7},{7,6},{8,9},{9,8},{10,11... | collective-permute-start | bytes 3342344 | tf_op jit(solution)/shard_map/ppermute | solution.py:405
